TPU v7x, 256 devices: a whole 4x4x8 slice. The times are simulated.
256 devices in a mesh: feat: 16 (over y, x), rep: 16 (over z, core).
Axes of the slice: x: 4, y: 4, z: 8, core: 2. Of those that a mesh axis runs over, the one named last changes fastest.
Arguments:
- feature_table: bfloat16 [768, 32768], P('feat'), may hold values from -6 to 6
- node_ids: int32 [16, 8192], P('rep'), may hold values from 0 to 32767
- neigh_one: int32 [16, 15, 2048], P('rep'), may hold values from 0 to 511
- count_one: int32 [16, 2048], P('rep'), may hold values from 1 to 15
- neigh_two: int32 [16, 25, 1024], P('rep', None, 'feat'), may hold values from 0 to 127
- count_two: int32 [16, 1024], P('rep', 'feat'), may hold values from 1 to 25
- w_one_self: bfloat16 [768, 1024], P('feat'), may hold values from -0.21875 to 0.21875
- w_one_neigh: bfloat16 [768, 1024], P('feat'), may hold values from -0.21875 to 0.21875
- w_two_self: bfloat16 [1024, 153], replicated, may hold values from -0.1875 to 0.1875
- w_two_neigh: bfloat16 [1024, 153], replicated, may hold values from -0.1875 to 0.1875
- logit_grad: bfloat16 [16, 1024, 153], P('rep', 'feat'), may hold values from -0.046875 to 0.046875
Outputs:
- logits: bfloat16 [16, 1024, 153], P('rep', 'feat')
- grad_w1_self: float32 [768, 1024], P('feat')
- grad_w1_neigh: float32 [768, 1024], P('feat')
- grad_w2_self: float32 [1024, 153], replicated
- grad_w2_neigh: float32 [1024, 153], replicated
Inputs may be any that keep to these rules, and one draw needn't show every extreme that they name: `count_one`: slots at or beyond a node's count are padding and ignored; a count reaches its fanout on some rows.
All inputs are finite; a program needn't handle non-finite values.
Results may differ from a plain program's by a relative error of at most 0.0051.
Values may be sent and summed in bfloat16 or wider, within the bound.
No kernel may reach another device: no remote copies, remote signals or barrier semaphores. Data moves between devices by JAX's collectives and lax.ppermute only.
A program may use at most 64 MiB of HBM per device.

v0:
```python
import jax
import jax.numpy as jnp
from jax import lax
from jax.sharding import PartitionSpec as P


def gelu_tanh(values):
    return jax.nn.gelu(values, approximate=True)


def mean_rows(source, lookup, counts):
    picked = jnp.take(source, lookup, axis=0).astype(jnp.float32)
    slot_ids = lax.broadcasted_iota(jnp.int32, lookup.shape, 1)
    live_slots = (slot_ids < counts[:, None])[:, :, None]
    summed = jnp.sum(jnp.where(live_slots, picked, 0.0), axis=1)
    return summed / counts.astype(jnp.float32)[:, None]


def mean_columns(source, lookup, counts):
    picked = jnp.take(source, lookup, axis=1).astype(jnp.float32)
    slot_ids = lax.broadcasted_iota(jnp.int32, lookup.shape, 0)
    live_slots = (slot_ids < counts[None, :])[None, :, :]
    summed = jnp.sum(jnp.where(live_slots, picked, 0.0), axis=1)
    return summed / counts.astype(jnp.float32)[None, :]


def contract_rows(first_op, second_op):
    return lax.dot_general(
        first_op, second_op, (((0,), (0,)), ((), ())), preferred_element_type=jnp.float32
    )


def contract_cols(first_op, second_op):
    return lax.dot_general(
        first_op, second_op, (((1,), (1,)), ((), ())), preferred_element_type=jnp.float32
    )


def on_device(
    feature_table,
    node_ids,
    neigh_one,
    count_one,
    neigh_two,
    count_two,
    w_one_self,
    w_one_neigh,
    w_two_self,
    w_two_neigh,
    logit_grad,
):
    groups = lax.axis_size("feat")
    part_cols = feature_table.shape[0]
    hidden_width = w_one_self.shape[1]
    rows_all = neigh_one.shape[2]
    own_rows = rows_all // groups
    input_rows = node_ids.shape[1] // groups
    inputs_cols = jnp.take(feature_table, node_ids[0], axis=1)
    self_cols = inputs_cols.reshape(part_cols, groups, input_rows)[:, :, :own_rows].reshape(
        part_cols, rows_all
    )
    offsets = lax.broadcasted_iota(jnp.int32, (1, rows_all), 1) // own_rows * input_rows
    agg_cols = mean_columns(inputs_cols, neigh_one[0] + offsets, count_one[0]).astype(jnp.bfloat16)
    part_self = self_cols
    part_agg = agg_cols
    pre_one = lax.psum_scatter(
        contract_rows(part_self, w_one_self) + contract_rows(part_agg, w_one_neigh),
        "feat",
        scatter_dimension=0,
        tiled=True,
    )
    hidden_one = gelu_tanh(pre_one).astype(jnp.bfloat16)
    neigh_rows = neigh_two[0].T
    targets = neigh_rows.shape[0]
    self_two = hidden_one[:targets]
    agg_two = mean_rows(hidden_one, neigh_rows, count_two[0]).astype(jnp.bfloat16)
    scores = jnp.dot(self_two, w_two_self, preferred_element_type=jnp.float32) + jnp.dot(
        agg_two, w_two_neigh, preferred_element_type=jnp.float32
    )
    logits = scores.astype(jnp.bfloat16)[None]
    upstream = logit_grad[0]
    grad_two_self = contract_rows(self_two, upstream)
    grad_two_neigh = contract_rows(agg_two, upstream)
    grad_self_rows = contract_cols(upstream, w_two_self)
    grad_agg_rows = contract_cols(upstream, w_two_neigh) / count_two[0].astype(jnp.float32)[:, None]
    slot_ids = lax.broadcasted_iota(jnp.int32, neigh_rows.shape, 1)
    live_slots = slot_ids < count_two[0][:, None]
    node_row = lax.broadcasted_iota(jnp.int32, (1, 1, own_rows), 2)
    spread = jnp.sum(
        ((neigh_rows[:, :, None] == node_row) & live_slots[:, :, None]).astype(jnp.float32), axis=1
    )
    grad_hidden = lax.dot_general(
        spread,
        grad_agg_rows,
        (((0,), (0,)), ((), ())),
        precision=lax.Precision.HIGHEST,
        preferred_element_type=jnp.float32,
    )
    grad_hidden = grad_hidden.at[:targets].add(grad_self_rows)
    pullback = jax.vjp(gelu_tanh, pre_one)[1]
    grad_pre = pullback(grad_hidden)[0].astype(jnp.bfloat16)
    shard_piece = lax.all_gather(grad_pre, "feat", axis=0, tiled=True)
    part_self = self_cols
    part_agg = agg_cols
    grad_first = jnp.concatenate(
        [
            jnp.dot(part_self, shard_piece, preferred_element_type=jnp.float32),
            jnp.dot(part_agg, shard_piece, preferred_element_type=jnp.float32),
        ],
        axis=1,
    )
    grad_first = lax.psum(grad_first, "rep")
    grad_head_self, grad_head_neigh = lax.psum((grad_two_self, grad_two_neigh), ("feat", "rep"))
    return (
        logits,
        grad_first[:, :hidden_width],
        grad_first[:, hidden_width:],
        grad_head_self,
        grad_head_neigh,
    )


def solution(mesh):
    return jax.shard_map(
        on_device,
        mesh=mesh,
        in_specs=(
            P("feat", None),
            P("rep", None),
            P("rep", None, None),
            P("rep", None),
            P("rep", None, "feat"),
            P("rep", "feat"),
            P("feat", None),
            P("feat", None),
            P(),
            P(),
            P("rep", "feat", None),
        ),
        out_specs=(P("rep", "feat", None), P("feat", None), P("feat", None), P(), P()),
        check_vma=False,
    )
```

profile of v0, /device:TPU:1, one launch (start us, length us, event | category | flops | bytes accessed | tf_op | source)
XLA Modules:
  0.0 730.7 jit_solution(8356214233402359195)
XLA Ops:
  7.2 0.8 compare_select_fusion.2
  8.1 0.8 compare_and_fusion.1
  8.8 0.7 convert_element_type.37
  10.1 1.5 reduce.7
  11.6 1.0 compare_select_fusion
  12.7 1.0 iota_compare_fusion.1
  13.7 8.2 %copy.23 = bf16[48,32768]{0,1:T(8,128)(2,1)} copy(bf16[48,32768]{1,0:T(8,128)(2,1)} %param.13) | data formatting | bytes 6291456 | tf_op args[0]
  21.9 32.6 %gather_fusion = bf16[8192,48]{1,0:T(8,128)(2,1)} fusion(bf16[48,32768]{0,1:T(8,128)(2,1)} %copy.23, s32[8192]{0:T(1024)S(1)} %broadcast_clamp_fusion.1), kind=kCustom, calls=%fused_computation | custom fusion | bytes 1605632 | tf_op jit(solution)/shard_map/jit(_take)/gather | solution.py:58
  54.5 5.8 bitcast_select_fusion
  60.4 1.4 slice_select_fusion
  61.8 107.8 %gather_fusion.1 = bf16[30720,48]{1,0:T(8,128)(2,1)} fusion(bf16[48,8192]{0,1:T(8,128)(2,1)S(1)} %bitcast_select_fusion, s32[30720]{0:T(1024)S(1)} %broadcast_clamp_fusion), kind=kCustom, calls=%fused_computation.1 | custom fusion | bytes 6021120 | tf_op jit(solution)/shard_map/jit(_take)/gather | solution.py:20
  169.5 1.2 fusion.26
  170.8 2.0 copy-done.1
  172.8 10.4 %select_reduce_fusion = f32[2048,48]{1,0:T(8,128)S(1)} fusion(bf16[15,2048,48]{2,1,0:T(8,128)(2,1)S(1)} %bitcast.57, pred[15,2048]{1,0:T(8,128)(4,1)S(1)} %get-tuple-element.23, pred[15,2048]{1,0:T(8,128)(4,1)S(1)} %get-tuple-element.24), kind=kLoop, calls=%fused_computation.3 | loop fusion | flops 5799936 | bytes 3403776 | tf_op jit(solution)/shard_map/reduce_sum | solution.py:23
  183.2 4.6 convolution_add_fusion
  190.3 90.5 %reduce-scatter.2.cloned.1.call-done = f32[128,1024]{1,0:T(8,128)} async-done(((f32[2048,1024]{1,0:T(8,128)}), f32[128,1024]{1,0:T(8,128)}) %reduce-scatter.2.cloned.1.call-update) | async-done | bytes 524304 | tf_op jit(solution)/shard_map/reduce_scatter | solution.py:66
  280.8 2.1 fusion.10
  283.4 6.5 gather_fusion.2
  289.8 4.9 reshape.240
  294.8 3.4 select_reduce_fusion.1
  298.2 1.1 fusion.15
  299.3 41.6 %all-gather.2.cloned.1.call-done = bf16[2048,1024]{1,0:T(8,128)(2,1)} async-done(((bf16[128,1024]{1,0:T(8,128)(2,1)}), bf16[2048,1024]{1,0:T(8,128)(2,1)}) %all-gather.2.cloned.1.call-update) | async-done | bytes 4194320 | tf_op jit(solution)/shard_map/all_gather | solution.py:102
  341.0 3.6 fusion.24
  344.5 0.9 fusion.28
  345.4 0.8 pad_maximum_fusion
  346.3 1.1 fusion.11
  347.7 0.9 fusion.2
  348.5 107.0 %all-reduce.4.cloned.1.call-done = f32[48,2048]{1,0:T(8,128)} async-done(((f32[48,2048]{1,0:T(8,128)}), f32[48,2048]{1,0:T(8,128)}) %all-reduce.4.cloned.1.call-update) | async-done | bytes 393232 | tf_op jit(solution)/shard_map/psum | solution.py:112
  455.5 1.8 fusion.25
  457.3 262.9 %all-reduce.6.cloned.1.call-done = (f32[1024,153]{0,1:T(8,128)}, f32[1024,153]{0,1:T(8,128)}) async-done(((f32[1024,153]{0,1:T(8,128)}, f32[1024,153]{0,1:T(8,128)}), (f32[1024,153]{0,1:T(8,128)}, f32[1024,153]{0,1:T(8,128)})) %all-reduce.6.cloned.1.call-update) | async-done | bytes 1253392 | tf_op jit(solution)/shard_map/psum | solution.py:113
  720.2 2.0 copy.42
  722.2 2.0 copy.43
  (50 shorter events, 3.8 us)
Async XLA Ops:
  7.2 182.9 %copy-start = (bf16[1024,153]{0,1:T(8,128)(2,1)S(1)}, bf16[1024,153]{0,1:T(8,128)(2,1)}, u32[]{:S(2)}) copy-start(bf16[1024,153]{0,1:T(8,128)(2,1)} %param.21) | copy-start | bytes 940036
  7.2 273.6 %reduce-scatter.2.cloned.1.call-start = ((), (), s32[]{:S(2)}) async-start(), calls=%async_computation.1 | async-start | bytes 8912896 | tf_op jit(solution)/shard_map/reduce_scatter | solution.py:66
  11.6 10.3 %copy-start.7 = (pred[16,512]{1,0:T(8,128)(4,1)}, pred[16,512]{1,0:T(8,128)(4,1)S(1)}, u32[]{:S(2)}) copy-start(pred[16,512]{1,0:T(8,128)(4,1)S(1)} %compare_and_fusion.2) | copy-start | bytes 24580
  54.5 5.8 slice-start
  61.8 107.8 %copy-start.5 = (bf16[48,1024]{1,0:T(8,128)(2,1)S(1)}, bf16[48,1024]{1,0:T(8,128)(2,1)}, u32[]{:S(2)}) copy-start(bf16[48,1024]{1,0:T(8,128)(2,1)} %param.19) | copy-start | bytes 294916
  169.5 3.2 copy-start.1
  172.8 10.4 %copy-start.6 = (bf16[48,1024]{1,0:T(8,128)(2,1)S(1)}, bf16[48,1024]{1,0:T(8,128)(2,1)}, u32[]{:S(2)}) copy-start(bf16[48,1024]{1,0:T(8,128)(2,1)} %param.20) | copy-start | bytes 294916
  187.8 0.7 copy-start.8
  187.8 0.8 copy-start.4
  187.8 1.5 copy-start.3
  187.8 1.5 copy-start.9
  187.8 153.2 %all-gather.2.cloned.1.call-start = ((), (), s32[]{:S(2)}) async-start(), calls=%async_computation.2 | async-start | bytes 4456448 | tf_op jit(solution)/shard_map/all_gather | solution.py:102
  282.9 172.6 %all-reduce.4.cloned.1.call-start = ((), (), s32[]{:S(2)}) async-start(), calls=%async_computation.3 | async-start | bytes 786432 | tf_op jit(solution)/shard_map/psum | solution.py:112
  341.0 3.6 copy-start.2
  346.2 374.0 %all-reduce.6.cloned.1.call-start = ((), (), s32[]{:S(2)}) async-start(), calls=%async_computation.4 | async-start | bytes 2621440 | tf_op jit(solution)/shard_map/psum | solution.py:113
Sparse Core Ops, SparseCore 0:
  187.9 92.8 reduce-scatter.1
  283.8 57.1 all-gather.1
  346.3 109.1 all-reduce.3
  462.4 257.7 all-reduce.5
where the time goes:
time: 732 us; the launch traced here: 731 us
  waiting for transfers between devices  502 us (69%)
  local copies, waits for them, and re-layouts  169 us (23%)
  other arithmetic  30.5 us (4%)
  matrix products  14.6 us (2%)
  between operations  14 us (2%)
    psum x1, waiting for transfers between devices, on_device(): lax.psum((grad_two_self, grad_two_neigh), ('feat', 'rep'))  263 us
    gather x1, local copies, waits for them, and re-layouts, mean_columns(): picked = jnp.take(source, lookup, axis=1).astype(jnp.float32)  108 us
    psum x1, waiting for transfers between devices, on_device(): grad_first = lax.psum(grad_first, 'rep')  107 us
    reduce_scatter x1, waiting for transfers between devices, on_device(): lax.psum_scatter(contract_rows(part_self, w_one_self) + contract_rows(par...  90.5 us
    all_gather x1, waiting for transfers between devices, on_device(): shard_piece = lax.all_gather(grad_pre, 'feat', axis=0, tiled=True)  41.6 us
    gather x1, local copies, waits for them, and re-layouts, on_device(): inputs_cols = jnp.take(feature_table, node_ids[0], axis=1)  32.6 us
    unnamed x25, local copies, waits for them, and re-layouts  15.3 us
  transfers between devices with their start and end apart: 4, of which 4 were waited for; matrix products, arithmetic and copies ran while one was open for 3% of the time, Pallas kernels for 0%

commit v1 on v0

v1 whole, which is shorter than its diff:
```python
import functools

import jax
import jax.numpy as jnp
import numpy as np
from jax import lax
from jax.experimental import pallas as pl
from jax.experimental.pallas import tpu as pltpu
from jax.sharding import Mesh, PartitionSpec as P

BF = jnp.bfloat16
F32 = jnp.float32
GELU_C = 0.7978845608028654
FEAT = ("y", "x")
REP = ("z", "c")
SUB = 128
INP = 512
TGT = 64
CHUNK = 512
CLS_ROWS = 10


def mm(first, second):
    return jnp.dot(first, second, preferred_element_type=F32)


def mm_nt(first, second):
    return lax.dot_general(first, second, (((1,), (1,)), ((), ())), preferred_element_type=F32)


def vmem(count):
    return [pl.BlockSpec(memory_space=pltpu.VMEM)] * count


def gather_kernel(ids_ref, neigh_ref, count_ref, table_ref, out_ref, turned, rows):
    cols, papers = table_ref.shape

    def turn(step, carry):
        start = pl.multiple_of(step * CHUNK, CHUNK)
        block = table_ref[:, pl.ds(start, CHUNK)].astype(F32)
        turned[pl.ds(start, CHUNK), :cols] = block.T
        return carry

    lax.fori_loop(0, papers // CHUNK, turn, 0, unroll=2)

    position = lax.broadcasted_iota(jnp.int32, (INP // 2, SUB), 0).astype(F32).astype(BF)
    one = jnp.ones((INP // 2, SUB), BF)
    zero = jnp.zeros((INP // 2, SUB), BF)

    def sub_batch(g, carry):
        base = g * INP
        for j in range(INP):
            rows[pl.ds(j, 1), :] = turned[pl.ds(ids_ref[0, base + j], 1), :]
        nodes = pl.ds(pl.multiple_of(g * SUB, SUB), SUB)
        count = count_ref[:, nodes]
        halves = [zero, zero]
        for k in range(neigh_ref.shape[1]):
            near = jnp.where(k < count, neigh_ref[0, pl.ds(k, 1), nodes], -1)
            for h in range(2):
                here = (near - h * (INP // 2)).astype(F32).astype(BF)
                halves[h] = halves[h] + jnp.where(position == here, one, zero)
        picked = rows[...].T[:cols].astype(BF)
        summed = mm(picked[:, : INP // 2], halves[0]) + mm(picked[:, INP // 2 :], halves[1])
        agg = (summed / count.astype(F32)).astype(BF)
        own = picked[:, :SUB]
        lanes = pl.ds(pl.multiple_of((g % 4) * SUB, SUB), SUB)
        for x in range(4):
            out_ref[(g // 4) * 4 + x, :cols, lanes] = own
            out_ref[(g // 4) * 4 + x, cols:, lanes] = agg
        return carry

    lax.fori_loop(0, 16, sub_batch, 0)


def gather(node_ids, neigh_one, count_one, feature_table):
    cols, papers = feature_table.shape
    return pl.pallas_call(
        gather_kernel,
        out_shape=jax.ShapeDtypeStruct((16, 2 * cols, 4 * SUB), BF),
        in_specs=[pl.BlockSpec(memory_space=pltpu.SMEM)] + vmem(3),
        out_specs=pl.BlockSpec(memory_space=pltpu.VMEM),
        scratch_shapes=[pltpu.VMEM((papers, 128), F32), pltpu.VMEM((INP, 128), F32)],
        compiler_params=pltpu.CompilerParams(vmem_limit_bytes=48 * 2**20),
        cost_estimate=pl.CostEstimate(flops=30_000_000_000, bytes_accessed=5_000_000, transcendentals=0),
        name="gather",
    )(node_ids, neigh_one, count_one, feature_table)


def prepare_kernel(w_ref, up_ref, neigh_ref, count_ref, w2s_ref, w2n_ref, wt_ref, gh_ref, spread_ref, upt_ref):
    wt_ref[...] = w_ref[...].T
    position = lax.broadcasted_iota(jnp.int32, (SUB, TGT), 0)
    for g in range(4):
        count = count_ref[pl.ds(g, 1), :]
        spread = jnp.zeros((SUB, TGT), F32)
        for k in range(25):
            near = jnp.where(k < count, neigh_ref[g, pl.ds(k, 1), :], -1)
            spread = spread + jnp.where(position == near, 1.0, 0.0)
        spread = spread.astype(BF)
        spread_ref[g] = spread
        upstream = up_ref[g]
        own = mm(upstream, w2s_ref[...])
        near_grad = mm(upstream, w2n_ref[...]).T / count.astype(F32)
        high = near_grad.astype(BF)
        low = (near_grad - high.astype(F32)).astype(BF)
        grad = mm_nt(high, spread) + mm_nt(low, spread)
        gh_ref[:, g * SUB : (g + 1) * SUB] = grad + jnp.concatenate([own.T, jnp.zeros(own.T.shape, F32)], axis=1)
        upt_ref[:153, g * TGT : (g + 1) * TGT] = upstream.astype(F32).T.astype(BF)
    upt_ref[153:] = jnp.zeros((7, 4 * TGT), BF)


def prepare(w_x, up_y, neigh_y, count_y, w2s_x, w2n_x):
    return pl.pallas_call(
        prepare_kernel,
        out_shape=(
            jax.ShapeDtypeStruct((256, 1536), BF),
            jax.ShapeDtypeStruct((256, 4 * SUB), F32),
            jax.ShapeDtypeStruct((4, SUB, TGT), BF),
            jax.ShapeDtypeStruct((160, 4 * TGT), BF),
        ),
        in_specs=vmem(6),
        out_specs=tuple(vmem(4)),
        cost_estimate=pl.CostEstimate(flops=6_000_000_000, bytes_accessed=2_000_000, transcendentals=0),
        name="prepare",
    )(w_x, up_y, neigh_y, count_y, w2s_x, w2n_x)


def layers_kernel(st_ref, wt_ref, gh_ref, spread_ref, count_ref, upt_ref, w2_ref, grads_ref, scores_ref):
    pre = mm(wt_ref[...], st_ref[...])
    square = pre * pre
    bend = jnp.tanh(GELU_C * pre * (1.0 + 0.044715 * square))
    half = 0.5 * (1.0 + bend)
    hidden = (pre * half).astype(BF)
    slope = half + 0.5 * pre * (1.0 - bend * bend) * (GELU_C * (1.0 + 3.0 * 0.044715 * square))
    grad_pre = (gh_ref[...] * slope).astype(BF)
    grad = mm_nt(st_ref[...], grad_pre).astype(BF)
    rows = grad.shape[0] // 16
    for f in range(16):
        grads_ref[f, :rows] = grad[f * rows : (f + 1) * rows]
    own, near = [], []
    for g in range(4):
        nodes = hidden[:, g * SUB : (g + 1) * SUB]
        own.append(nodes[:, :TGT])
        near.append((mm(nodes, spread_ref[g]) / count_ref[pl.ds(g, 1), :].astype(F32)).astype(BF))
    both = jnp.concatenate([jnp.concatenate(own, axis=1), jnp.concatenate(near, axis=1)], axis=0)
    scores_ref[...] = mm(w2_ref[...], both).T
    head = mm_nt(upt_ref[...], both)
    for f in range(16):
        part = head[f * CLS_ROWS : (f + 1) * CLS_ROWS].astype(BF)
        grads_ref[f, 96 : 96 + CLS_ROWS] = part[:, :256]
        grads_ref[f, 112 : 112 + CLS_ROWS] = part[:, 256:]
        grads_ref[f, 96 + CLS_ROWS : 112] = jnp.zeros((16 - CLS_ROWS, 256), BF)
        grads_ref[f, 112 + CLS_ROWS :] = jnp.zeros((16 - CLS_ROWS, 256), BF)


def layers(st, wt, gh, spread, count_y, upt, w2_x):
    return pl.pallas_call(
        layers_kernel,
        out_shape=(
            jax.ShapeDtypeStruct((16, 128, 256), BF),
            jax.ShapeDtypeStruct((4 * TGT, 153), F32),
        ),
        in_specs=vmem(7),
        out_specs=tuple(vmem(2)),
        cost_estimate=pl.CostEstimate(flops=6_000_000_000, bytes_accessed=4_000_000, transcendentals=200_000),
        name="layers",
    )(st, wt, gh, spread, count_y, upt, w2_x)


def sum_feat_kernel(in_ref, out_ref):
    for x in range(4):
        total = sum(in_ref[4 * y + x].astype(F32) for y in range(4))
        for h in range(2):
            half = total[:, h * 128 : (h + 1) * 128]
            z = 2 * x + h
            out_ref[2 * z, :48] = half[:48]
            out_ref[2 * z + 1, :48] = half[48:96]
            out_ref[z, 48:] = half[96:112]
            out_ref[8 + z, 48:] = half[112:]


def sum_feat(parts):
    return pl.pallas_call(
        sum_feat_kernel,
        out_shape=jax.ShapeDtypeStruct((16, 64, 128), F32),
        in_specs=vmem(1),
        out_specs=vmem(1)[0],
        cost_estimate=pl.CostEstimate(flops=10_000_000, bytes_accessed=1_500_000, transcendentals=0),
        name="sum_feat",
    )(parts)


def place_kernel(in_ref, self_ref, neigh_ref, head_self_ref, head_neigh_ref):
    for z in range(8):
        lanes = slice(z * 128, (z + 1) * 128)
        self_ref[:, lanes] = in_ref[2 * z, :48].astype(F32)
        neigh_ref[:, lanes] = in_ref[2 * z + 1, :48].astype(F32)
        head_self_ref[:, lanes] = in_ref[z, 48:].astype(F32)[:153]
        head_neigh_ref[:, lanes] = in_ref[8 + z, 48:].astype(F32)[:153]


def place(parts):
    first = jax.ShapeDtypeStruct((48, 1024), F32)
    head = jax.ShapeDtypeStruct((153, 1024), F32)
    return pl.pallas_call(
        place_kernel,
        out_shape=(first, first, head, head),
        in_specs=vmem(1),
        out_specs=tuple(vmem(4)),
        cost_estimate=pl.CostEstimate(flops=1_000_000, bytes_accessed=2_500_000, transcendentals=0),
        name="place",
    )(parts)


def on_device(
    feature_table,
    node_ids,
    neigh_one,
    count_one,
    neigh_two,
    count_two,
    w_one_self,
    w_one_neigh,
    w_two_self,
    w_two_neigh,
    logit_grad,
):
    column = lax.axis_index("x") * 256
    w_local = jnp.concatenate([w_one_self, w_one_neigh], axis=0)
    w_send = w_local.reshape(96, 4, 256).transpose(1, 0, 2)
    w_send = jnp.broadcast_to(w_send[None], (4, 4, 96, 256)).reshape(16, 96, 256)
    w_x = lax.all_to_all(w_send, FEAT, 0, 0, tiled=True).reshape(1536, 256)
    up_y = lax.all_gather(logit_grad[0], "x", axis=0)
    neigh_y = lax.all_gather(neigh_two[0], "x", axis=0)
    count_y = lax.all_gather(count_two[0], "x", axis=0)

    st = lax.all_to_all(gather(node_ids, neigh_one, count_one, feature_table), FEAT, 0, 0, tiled=True)

    w2s_x = lax.dynamic_slice_in_dim(w_two_self.T, column, 256, 1)
    w2n_x = lax.dynamic_slice_in_dim(w_two_neigh.T, column, 256, 1)
    wt, gh, spread, upt = prepare(w_x, up_y, neigh_y, count_y, w2s_x, w2n_x)
    grads, scores = layers(
        st.reshape(1536, 4 * SUB), wt, gh, spread, count_y, upt, jnp.concatenate([w2s_x, w2n_x], axis=1)
    )
    summed = sum_feat(lax.all_to_all(grads, FEAT, 0, 0, tiled=True))
    scores = lax.all_to_all(scores.reshape(4, TGT, 153), "x", 0, 0, tiled=True)
    logits = jnp.sum(scores, axis=0).astype(BF)[None]

    total = jnp.sum(lax.all_to_all(summed, REP, 0, 0, tiled=True), axis=0)
    head = jnp.broadcast_to(total[48:][None], (16, 16, 128))
    head = lax.all_to_all(head, FEAT, 0, 0, tiled=True)[:, :CLS_ROWS].reshape(160, 128)
    final = jnp.concatenate([total[:48], head], axis=0).astype(BF)
    final = lax.all_gather(final, REP, axis=0)
    grad_self, grad_neigh, head_self, head_neigh = place(final)
    return logits, grad_self, grad_neigh, head_self.T, head_neigh.T


def solution(mesh):
    fine = Mesh(np.asarray(mesh.devices).reshape(4, 4, 8, 2), ("y", "x", "z", "c"))
    return jax.shard_map(
        on_device,
        mesh=fine,
        in_specs=(
            P(FEAT, None),
            P(REP, None),
            P(REP, None, None),
            P(REP, None),
            P(REP, None, FEAT),
            P(REP, FEAT),
            P(FEAT, None),
            P(FEAT, None),
            P(),
            P(),
            P(REP, FEAT, None),
        ),
        out_specs=(P(REP, FEAT, None), P(FEAT, None), P(FEAT, None), P(), P()),
        check_vma=False,
    )
```

time: 732 us -> 186 us (0.25)
  waiting for transfers between devices: 502 us -> 26.5 us
  local copies, waits for them, and re-layouts: 169 us -> 3.98 us
  blocking collectives: 0 us -> 78.6 us
  starting transfers between devices: 0.16 us -> 40.1 us
  Pallas kernels: 0 us -> 32.9 us
  other arithmetic: 30.5 us -> 2.33 us
  matrix products: 14.6 us -> 0 us
  between operations: 14 us -> 0.84 us
    psum x2 -> x0, waiting for transfers between devices: 370 us -> none  [the longest x1 263 us: on_device(): lax.psum((grad_two_self, grad_two_neigh), ('feat', 'rep'))]
    gather x4 -> x0, local copies, waits for them, and re-layouts: 152 us -> none  [the longest x1 108 us: mean_columns(): picked = jnp.take(source, lookup, axis=1).astype(jnp.float32)]
    reduce_scatter x1 -> x0, waiting for transfers between devices: 90.5 us -> none  [on_device(): lax.psum_scatter(contract_rows(part_self, w_one_self) + contract_rows(par...]
    all_gather x0 -> x4, blocking collectives: none -> 59.7 us  [the longest x1 20.4 us: on_device(): count_y = lax.all_gather(count_two[0], 'x', axis=0)]
    all_gather x1 -> x0, waiting for transfers between devices: 41.6 us -> none  [on_device(): shard_piece = lax.all_gather(grad_pre, 'feat', axis=0, tiled=True)]
    all_to_all x0 -> x5, starting transfers between devices: none -> 40.1 us  [the longest x1 18.7 us: on_device(): total = jnp.sum(lax.all_to_all(summed, REP, 0, 0, tiled=True), axis=0)]
    pallas_call x0 -> x5, Pallas kernels: none -> 32.9 us  [the longest x1 20.3 us: gather(): pl.pallas_call(gather_kernel, out_shape=jax.ShapeDtypeStruct((16, 2 * col...]
    all_to_all x0 -> x5, waiting for transfers between devices: none -> 26.5 us  [the longest x1 16.7 us: on_device(): total = jnp.sum(lax.all_to_all(summed, REP, 0, 0, tiled=True), axis=0)]
  transfers between devices with their start and end apart: 4 -> 5, of which waited for: 4 -> 3; matrix products, arithmetic and copies ran while one was open for 3% -> 1% of each run, Pallas kernels for 0% -> 14%
where the time goes in v1:
time: 186 us; the launch traced here: 185 us
  blocking collectives  78.6 us (42%)
  starting transfers between devices  40.1 us (22%)
  Pallas kernels  32.9 us (18%)
  waiting for transfers between devices  26.5 us (14%)
  local copies, waits for them, and re-layouts  3.98 us (2%)
  other arithmetic  2.33 us (1%)
    all_gather x1, blocking collectives, on_device(): count_y = lax.all_gather(count_two[0], 'x', axis=0)  20.4 us
    pallas_call x1, Pallas kernels, gather(): pl.pallas_call(gather_kernel, out_shape=jax.ShapeDtypeStruct((16, 2 * col...  20.3 us
    all_to_all x1, blocking collectives, on_device(): summed = sum_feat(lax.all_to_all(grads, FEAT, 0, 0, tiled=True))  18.9 us
    all_to_all x1, starting transfers between devices, on_device(): total = jnp.sum(lax.all_to_all(summed, REP, 0, 0, tiled=True), axis=0)  18.7 us
    all_gather x1, blocking collectives, on_device(): final = lax.all_gather(final, REP, axis=0)  18.4 us
    all_to_all x1, waiting for transfers between devices, on_device(): total = jnp.sum(lax.all_to_all(summed, REP, 0, 0, tiled=True), axis=0)  16.7 us
    all_gather x1, blocking collectives, on_device(): neigh_y = lax.all_gather(neigh_two[0], 'x', axis=0)  11.1 us
    all_gather x1, blocking collectives, on_device(): up_y = lax.all_gather(logit_grad[0], 'x', axis=0)  9.83 us
  transfers between devices with their start and end apart: 5, of which 3 were waited for; matrix products, arithmetic and copies ran while one was open for 1% of the time, Pallas kernels for 14%

profile of v1, /device:TPU:1, one launch (start us, length us, event | category | flops | bytes accessed | tf_op | source)
XLA Modules:
  0.0 185.3 jit_solution(1670181005726992359)
XLA Ops:
  0.6 1.0 pad_maximum_fusion
  1.6 0.0 copy-start.6
  1.6 0.1 reshape.69
  1.7 0.0 copy-start
  1.7 0.0 copy-start.1
  1.8 0.0 copy-start.2
  1.8 1.0 broadcast_in_dim.4
  2.8 7.8 %all-to-all-start.1 = ((bf16[16,96,256]{2,1,0:T(8,128)(2,1)}), bf16[16,96,256]{2,1,0:T(8,128)(2,1)}, u32[]{:S(2)}, u32[]{:S(2)}) async-start(bf16[16,96,256]{2,1,0:T(8,128)(2,1)} %bitcast.19), calls=%async_computation.1 | async-start | bytes 1572864 | tf_op jit(solution)/shard_map/all_to_all | solution.py:231
  10.6 20.3 %gather.1 = bf16[16,96,512]{2,1,0:T(8,128)(2,1)} custom-call(s32[1,8192]{1,0:T(1,128)S(1)} %copy-done.1, s32[1,15,2048]{2,1,0:T(8,128)S(1)} %copy.24.neigh_ref, s32[1,2048]{1,0:T(1,128)S(1)} %copy-done.2, bf16[48,32768]{1,0:T(8,128)(2,1)S(1)} %copy-done), custom_call_target="tpu_custom_call" | custom-call | flops 30000001024 | bytes 5000000 | tf_op jit(solution)/shard_map/gather/pallas_call | solution.py:77
  30.9 0.0 all-to-all-done.1
  30.9 6.8 %all-to-all-start = ((bf16[16,96,512]{2,1,0:T(8,128)(2,1)}), bf16[16,96,512]{2,1,0:T(8,128)(2,1)S(1)}, u32[]{:S(2)}, u32[]{:S(2)}) async-start(bf16[16,96,512]{2,1,0:T(8,128)(2,1)} %gather.1), calls=%async_computation | async-start | bytes 3145728 | tf_op jit(solution)/shard_map/all_to_all | solution.py:236
  37.7 20.4 %all-gather = s32[4,1,64]{2,1,0:T(1,128)} all-gather(s32[1,1,64]{2,1,0:T(1,128)S(1)} %bitcast.26), channel_id=1, replica_groups=mesh['y'=4,'x'=4,'z'=8,'c'=2] {'x'}, dimensions={0}, use_global_device_ids=true | all-gather | bytes 1280 | tf_op jit(solution)/shard_map/all_gather | solution.py:234
  58.1 11.1 %all_gather.14.neigh_ref = s32[4,25,64]{2,1,0:T(8,128)} all-gather(s32[1,25,64]{2,1,0:T(8,128)S(1)} %copy.26), channel_id=1, replica_groups=mesh['y'=4,'x'=4,'z'=8,'c'=2] {'x'}, dimensions={0}, use_global_device_ids=true | all-gather | bytes 32000 | tf_op jit(solution)/shard_map/all_gather | solution.py:233
  69.2 9.8 %all_gather.13.up_ref = bf16[4,64,153]{2,1,0:T(8,128)(2,1)} all-gather(bf16[1,64,153]{2,1,0:T(8,128)(2,1)S(1)} %copy-done.7), channel_id=1, replica_groups=mesh['y'=4,'x'=4,'z'=8,'c'=2] {'x'}, dimensions={0}, use_global_device_ids=true | all-gather | bytes 97920 | tf_op jit(solution)/shard_map/all_gather | solution.py:232
  79.0 0.9 dynamic-slice_bitcast_fusion
  80.0 0.0 copy-start.5
  80.0 0.7 pad_maximum_fusion.1.w2_ref
  80.7 3.4 %prepare.1 = (bf16[256,1536]{1,0:T(8,128)(2,1)}, f32[256,512]{1,0:T(8,128)}, bf16[4,128,64]{2,1,0:T(8,128)(2,1)}, bf16[160,256]{1,0:T(8,128)(2,1)}) custom-call(bf16[1536,256]{1,0:T(8,128)(2,1)} %bitcast.3.w_ref, bf16[4,64,153]{2,1,0:T(8,128)(2,1)} %all_gather.13.up_ref, s32[4,25,64]{2,1,0:T(8,128)} %all_gather.14.neigh_ref, s32[4,64]{1,0:T(4,128)} %bitcast.24, ...), custom_call_target="tpu_custom_call" | custom-call | flops 6000000000 | bytes 2000000 | tf_op jit(solution)/shard_map/prepare/pallas_call | solution.py:112
  84.1 1.2 copy-done.3
  85.3 4.6 %layers.1 = (bf16[16,128,256]{2,1,0:T(8,128)(2,1)}, f32[256,153]{1,0:T(8,128)}) custom-call(bf16[1536,512]{1,0:T(8,128)(2,1)} %bitcast.20, bf16[256,1536]{1,0:T(8,128)(2,1)} %get-tuple-element.15.wt_ref, f32[256,512]{1,0:T(8,128)} %get-tuple-element.16.gh_ref, bf16[4,128,64]{2,1,0:T(8,128)(2,1)} %get-tuple-element.17.spread_ref, s32[4,64]{1,0:T(4,128)} %bitcast.25, ...), custom_call_target="tpu_custom_call" | custom-call | flops 6000000000 | bytes 4000000 | tf_op jit(solution)/shard_map/layers/pallas_call | solution.py:156
  89.8 18.9 %all_to_all.30.in_ref = bf16[16,128,256]{2,1,0:T(8,128)(2,1)} all-to-all(bf16[16,128,256]{2,1,0:T(8,128)(2,1)} %get-tuple-element.20), channel_id=1, replica_groups=mesh['y'=4,'x'=4,'z'=8,'c'=2] {'y','x'}, dimensions={0} | all-to-all | bytes 2097152 | tf_op jit(solution)/shard_map/all_to_all | solution.py:244
  108.8 3.4 %all-to-all-start.2 = ((f32[4,64,153]{2,1,0:T(8,128)}), f32[4,64,153]{2,1,0:T(8,128)S(1)}, u32[]{:S(2)}, u32[]{:S(2)}) async-start(f32[4,64,153]{2,1,0:T(8,128)} %bitcast.8), calls=%async_computation.2 | async-start | bytes 524288 | tf_op jit(solution)/shard_map/all_to_all | solution.py:245
  112.2 2.1 %sum_feat.1 = f32[16,64,128]{2,1,0:T(8,128)} custom-call(bf16[16,128,256]{2,1,0:T(8,128)(2,1)} %all_to_all.30.in_ref), custom_call_target="tpu_custom_call" | custom-call | flops 10000000 | bytes 1500000 | tf_op jit(solution)/shard_map/sum_feat/pallas_call | solution.py:182
  114.3 3.4 %all-to-all-done.2 = f32[4,64,153]{2,1,0:T(8,128)S(1)} async-done(((f32[4,64,153]{2,1,0:T(8,128)}), f32[4,64,153]{2,1,0:T(8,128)S(1)}, u32[]{:S(2)}, u32[]{:S(2)}) %all-to-all-start.2) | async-done | bytes 156704 | tf_op jit(solution)/shard_map/all_to_all | solution.py:245
  117.7 18.7 %all-to-all-start.4 = ((f32[16,64,128]{2,1,0:T(8,128)}), f32[16,64,128]{2,1,0:T(8,128)S(1)}, u32[]{:S(2)}, u32[]{:S(2)}) async-start(f32[16,64,128]{2,1,0:T(8,128)} %sum_feat.1), calls=%async_computation.4 | async-start | bytes 1048576 | tf_op jit(solution)/shard_map/all_to_all | solution.py:248
  136.4 0.6 reduce_sum.18
  137.0 16.7 %all-to-all-done.4 = f32[16,64,128]{2,1,0:T(8,128)S(1)} async-done(((f32[16,64,128]{2,1,0:T(8,128)}), f32[16,64,128]{2,1,0:T(8,128)S(1)}, u32[]{:S(2)}, u32[]{:S(2)}) %all-to-all-start.4) | async-done | bytes 524320 | tf_op jit(solution)/shard_map/all_to_all | solution.py:248
  153.8 0.6 broadcast_in_dim.5
  154.4 3.5 %all-to-all-start.5 = ((bf16[16,16,128]{2,1,0:T(8,128)(2,1)}), bf16[16,16,128]{2,1,0:T(8,128)(2,1)S(1)}, u32[]{:S(2)}, u32[]{:S(2)}) async-start(bf16[16,16,128]{2,1,0:T(8,128)(2,1)} %broadcast_in_dim.5), calls=%async_computation.5 | async-start | bytes 131072 | tf_op jit(solution)/shard_map/all_to_all | solution.py:250
  157.9 6.4 %all-to-all-done.5 = bf16[16,16,128]{2,1,0:T(8,128)(2,1)S(1)} async-done(((bf16[16,16,128]{2,1,0:T(8,128)(2,1)}), bf16[16,16,128]{2,1,0:T(8,128)(2,1)S(1)}, u32[]{:S(2)}, u32[]{:S(2)}) %all-to-all-start.5) | async-done | bytes 65568 | tf_op jit(solution)/shard_map/all_to_all | solution.py:250
  164.4 18.4 %all_gather.16.in_ref = bf16[16,208,128]{2,1,0:T(8,128)(2,1)} all-gather(bf16[1,208,128]{2,1,0:T(8,128)(2,1)S(1)} %pad_maximum_fusion.2), channel_id=1, replica_groups=mesh['y'=4,'x'=4,'z'=8,'c'=2] {'z','c'}, dimensions={0}, use_global_device_ids=true | all-gather | bytes 905216 | tf_op jit(solution)/shard_map/all_gather | solution.py:252
  182.8 2.5 %place.1 = (f32[48,1024]{1,0:T(8,128)}, f32[48,1024]{1,0:T(8,128)}, f32[153,1024]{1,0:T(8,128)}, f32[153,1024]{1,0:T(8,128)}) custom-call(bf16[16,208,128]{2,1,0:T(8,128)(2,1)} %all_gather.16.in_ref), custom_call_target="tpu_custom_call" | custom-call | flops 1000000 | bytes 2500000 | tf_op jit(solution)/shard_map/place/pallas_call | solution.py:204
  (23 shorter events, 0.2 us)
Async XLA Ops:
  1.6 8.9 %copy-start.6 = (s32[1,15,2048]{2,0,1:T(1,128)S(1)}, s32[1,15,2048]{2,0,1:T(1,128)}, u32[]{:S(2)}) copy-start(s32[1,15,2048]{2,0,1:T(1,128)} %param.13) | copy-start | bytes 368644
  1.7 8.9 %copy-start = (bf16[48,32768]{1,0:T(8,128)(2,1)S(1)}, bf16[48,32768]{1,0:T(8,128)(2,1)}, u32[]{:S(2)}) copy-start(bf16[48,32768]{1,0:T(8,128)(2,1)} %table_ref.1) | copy-start | bytes 9437188
  1.7 8.9 %copy-start.1 = (s32[1,8192]{1,0:T(1,128)S(1)}, s32[1,8192]{1,0:T(1,128)}, u32[]{:S(2)}) copy-start(s32[1,8192]{1,0:T(1,128)} %ids_ref.1) | copy-start | bytes 98308
  1.8 8.9 %copy-start.2 = (s32[1,2048]{1,0:T(1,128)S(1)}, s32[1,2048]{1,0:T(1,128)}, u32[]{:S(2)}) copy-start(s32[1,2048]{1,0:T(1,128)} %count_ref.1) | copy-start | bytes 24580
  2.8 28.2 %all-to-all-start.1 = ((bf16[16,96,256]{2,1,0:T(8,128)(2,1)}), bf16[16,96,256]{2,1,0:T(8,128)(2,1)}, u32[]{:S(2)}, u32[]{:S(2)}) async-start(bf16[16,96,256]{2,1,0:T(8,128)(2,1)} %bitcast.19), calls=%async_computation.1 | async-start | bytes 1572864 | tf_op jit(solution)/shard_map/all_to_all | solution.py:231
  30.9 6.8 %copy-start.8 = (s32[1,25,64]{2,0,1:T(1,128)S(1)}, s32[1,25,64]{2,0,1:T(1,128)}, u32[]{:S(2)}) copy-start(s32[1,25,64]{2,0,1:T(1,128)} %param.15) | copy-start | bytes 19204
  30.9 6.8 %copy-start.9 = (s32[1,64]{1,0:T(1,128)S(1)}, s32[1,64]{1,0:T(1,128)}, u32[]{:S(2)}) copy-start(s32[1,64]{1,0:T(1,128)} %param.16) | copy-start | bytes 772
  30.9 38.3 %copy-start.7 = (bf16[1,64,153]{2,1,0:T(8,128)(2,1)S(1)}, bf16[1,64,153]{2,1,0:T(8,128)(2,1)}, u32[]{:S(2)}) copy-start(bf16[1,64,153]{2,1,0:T(8,128)(2,1)} %param.21) | copy-start | bytes 58756
  30.9 53.2 %all-to-all-start = ((bf16[16,96,512]{2,1,0:T(8,128)(2,1)}), bf16[16,96,512]{2,1,0:T(8,128)(2,1)S(1)}, u32[]{:S(2)}, u32[]{:S(2)}) async-start(bf16[16,96,512]{2,1,0:T(8,128)(2,1)} %gather.1), calls=%async_computation | async-start | bytes 3145728 | tf_op jit(solution)/shard_map/all_to_all | solution.py:236
  80.0 0.7 copy-start.4
  80.0 0.7 copy-start.5
  84.1 1.2 copy-start.3
  108.8 8.9 %all-to-all-start.2 = ((f32[4,64,153]{2,1,0:T(8,128)}), f32[4,64,153]{2,1,0:T(8,128)S(1)}, u32[]{:S(2)}, u32[]{:S(2)}) async-start(f32[4,64,153]{2,1,0:T(8,128)} %bitcast.8), calls=%async_computation.2 | async-start | bytes 524288 | tf_op jit(solution)/shard_map/all_to_all | solution.py:245
  117.7 36.0 %all-to-all-start.4 = ((f32[16,64,128]{2,1,0:T(8,128)}), f32[16,64,128]{2,1,0:T(8,128)S(1)}, u32[]{:S(2)}, u32[]{:S(2)}) async-start(f32[16,64,128]{2,1,0:T(8,128)} %sum_feat.1), calls=%async_computation.4 | async-start | bytes 1048576 | tf_op jit(solution)/shard_map/all_to_all | solution.py:248
  154.4 10.0 %all-to-all-start.5 = ((bf16[16,16,128]{2,1,0:T(8,128)(2,1)}), bf16[16,16,128]{2,1,0:T(8,128)(2,1)S(1)}, u32[]{:S(2)}, u32[]{:S(2)}) async-start(bf16[16,16,128]{2,1,0:T(8,128)(2,1)} %broadcast_in_dim.5), calls=%async_computation.5 | async-start | bytes 131072 | tf_op jit(solution)/shard_map/all_to_all | solution.py:250

commit v2 on v1

--- a/solution.py
+++ b/solution.py
@@ -17,6 +17,7 @@
 INP = 512
 TGT = 64
 CHUNK = 512
+LISTS = 160
 CLS_ROWS = 10
 
 
@@ -86,29 +87,53 @@
     )(node_ids, neigh_one, count_one, feature_table)
 
 
-def prepare_kernel(w_ref, up_ref, neigh_ref, count_ref, w2s_ref, w2n_ref, wt_ref, gh_ref, spread_ref, upt_ref):
-    wt_ref[...] = w_ref[...].T
-    position = lax.broadcasted_iota(jnp.int32, (SUB, TGT), 0)
+def pack_kernel(w_self_ref, w_neigh_ref, up_ref, neigh_ref, count_ref, out_ref):
+    lists = jnp.concatenate([neigh_ref[...], count_ref[...]], axis=0).astype(F32).T.astype(BF)
+    for x in range(4):
+        lanes = slice(x * 256, (x + 1) * 256)
+        for y in range(4):
+            out_ref[4 * y + x, :48] = w_self_ref[:, lanes]
+            out_ref[4 * y + x, 48:96] = w_neigh_ref[:, lanes]
+            out_ref[4 * y + x, 96:, :153] = up_ref[...]
+            out_ref[4 * y + x, 96:, LISTS : LISTS + 26] = lists
+
+
+def pack(w_self, w_neigh, upstream, neigh, count):
+    return pl.pallas_call(
+        pack_kernel,
+        out_shape=jax.ShapeDtypeStruct((16, 96 + TGT, 256), BF),
+        in_specs=vmem(5),
+        out_specs=vmem(1)[0],
+        cost_estimate=pl.CostEstimate(flops=1_000_000, bytes_accessed=1_500_000, transcendentals=0),
+        name="pack",
+    )(w_self, w_neigh, upstream, neigh, count)
+
+
+def prepare_kernel(y_ref, in_ref, w2s_ref, w2n_ref, wt_ref, gh_ref, spread_ref, upt_ref, count_ref):
+    wt_ref[...] = jnp.concatenate([in_ref[f, :96] for f in range(16)], axis=0).T
+    position = lax.broadcasted_iota(jnp.int32, (SUB, TGT), 0).astype(F32)
     for g in range(4):
-        count = count_ref[pl.ds(g, 1), :]
+        upstream = in_ref[4 * y_ref[0] + g, 96:]
+        turned = upstream.astype(F32).T
+        count = turned[LISTS + 25 : LISTS + 26]
         spread = jnp.zeros((SUB, TGT), F32)
         for k in range(25):
-            near = jnp.where(k < count, neigh_ref[g, pl.ds(k, 1), :], -1)
+            near = jnp.where(k < count, turned[LISTS + k : LISTS + k + 1], -1.0)
             spread = spread + jnp.where(position == near, 1.0, 0.0)
         spread = spread.astype(BF)
         spread_ref[g] = spread
-        upstream = up_ref[g]
-        own = mm(upstream, w2s_ref[...])
-        near_grad = mm(upstream, w2n_ref[...]).T / count.astype(F32)
+        own = mm(upstream[:, :153], w2s_ref[...])
+        near_grad = mm(upstream[:, :153], w2n_ref[...]).T / count
         high = near_grad.astype(BF)
         low = (near_grad - high.astype(F32)).astype(BF)
         grad = mm_nt(high, spread) + mm_nt(low, spread)
         gh_ref[:, g * SUB : (g + 1) * SUB] = grad + jnp.concatenate([own.T, jnp.zeros(own.T.shape, F32)], axis=1)
-        upt_ref[:153, g * TGT : (g + 1) * TGT] = upstream.astype(F32).T.astype(BF)
+        upt_ref[:153, g * TGT : (g + 1) * TGT] = turned[:153].astype(BF)
+        count_ref[pl.ds(g, 1), :] = count
     upt_ref[153:] = jnp.zeros((7, 4 * TGT), BF)
 
 
-def prepare(w_x, up_y, neigh_y, count_y, w2s_x, w2n_x):
+def prepare(row, received, w2s_x, w2n_x):
     return pl.pallas_call(
         prepare_kernel,
         out_shape=(
@@ -116,15 +141,16 @@
             jax.ShapeDtypeStruct((256, 4 * SUB), F32),
             jax.ShapeDtypeStruct((4, SUB, TGT), BF),
             jax.ShapeDtypeStruct((160, 4 * TGT), BF),
+            jax.ShapeDtypeStruct((4, TGT), F32),
         ),
-        in_specs=vmem(6),
-        out_specs=tuple(vmem(4)),
+        in_specs=[pl.BlockSpec(memory_space=pltpu.SMEM)] + vmem(3),
+        out_specs=tuple(vmem(5)),
         cost_estimate=pl.CostEstimate(flops=6_000_000_000, bytes_accessed=2_000_000, transcendentals=0),
         name="prepare",
-    )(w_x, up_y, neigh_y, count_y, w2s_x, w2n_x)
-
-
-def layers_kernel(st_ref, wt_ref, gh_ref, spread_ref, count_ref, upt_ref, w2_ref, grads_ref, scores_ref):
+    )(row, received, w2s_x, w2n_x)
+
+
+def layers_kernel(x_ref, st_ref, wt_ref, gh_ref, spread_ref, count_ref, upt_ref, w2_ref, grads_ref, *scores_refs):
     pre = mm(wt_ref[...], st_ref[...])
     square = pre * pre
     bend = jnp.tanh(GELU_C * pre * (1.0 + 0.044715 * square))
@@ -140,9 +166,16 @@
     for g in range(4):
         nodes = hidden[:, g * SUB : (g + 1) * SUB]
         own.append(nodes[:, :TGT])
-        near.append((mm(nodes, spread_ref[g]) / count_ref[pl.ds(g, 1), :].astype(F32)).astype(BF))
+        near.append((mm(nodes, spread_ref[g]) / count_ref[pl.ds(g, 1), :]).astype(BF))
     both = jnp.concatenate([jnp.concatenate(own, axis=1), jnp.concatenate(near, axis=1)], axis=0)
-    scores_ref[...] = mm(w2_ref[...], both).T
+    scores = mm(w2_ref[...], both).T
+    for g in range(4):
+        for step, scores_ref in enumerate(scores_refs):
+
+            @pl.when(lax.rem(x_ref[0] + step, 4) == g)
+            def _():
+                scores_ref[...] = scores[g * TGT : (g + 1) * TGT]
+
     head = mm_nt(upt_ref[...], both)
     for f in range(16):
         part = head[f * CLS_ROWS : (f + 1) * CLS_ROWS].astype(BF)
@@ -152,18 +185,18 @@
         grads_ref[f, 112 + CLS_ROWS :] = jnp.zeros((16 - CLS_ROWS, 256), BF)
 
 
-def layers(st, wt, gh, spread, count_y, upt, w2_x):
+def layers(column, st, wt, gh, spread, count_y, upt, w2_x):
     return pl.pallas_call(
         layers_kernel,
         out_shape=(
             jax.ShapeDtypeStruct((16, 128, 256), BF),
-            jax.ShapeDtypeStruct((4 * TGT, 153), F32),
+            *[jax.ShapeDtypeStruct((TGT, 153), F32)] * 4,
         ),
-        in_specs=vmem(7),
-        out_specs=tuple(vmem(2)),
+        in_specs=[pl.BlockSpec(memory_space=pltpu.SMEM)] + vmem(7),
+        out_specs=tuple(vmem(5)),
         cost_estimate=pl.CostEstimate(flops=6_000_000_000, bytes_accessed=4_000_000, transcendentals=200_000),
         name="layers",
-    )(st, wt, gh, spread, count_y, upt, w2_x)
+    )(column, st, wt, gh, spread, count_y, upt, w2_x)
 
 
 def sum_feat_kernel(in_ref, out_ref):
@@ -189,7 +222,8 @@
     )(parts)
 
 
-def place_kernel(in_ref, self_ref, neigh_ref, head_self_ref, head_neigh_ref):
+def place_kernel(in_ref, score0, score1, score2, score3, logits_ref, self_ref, neigh_ref, head_self_ref, head_neigh_ref):
+    logits_ref[...] = (score0[...] + score1[...] + score2[...] + score3[...]).astype(BF)
     for z in range(8):
         lanes = slice(z * 128, (z + 1) * 128)
         self_ref[:, lanes] = in_ref[2 * z, :48].astype(F32)
@@ -198,17 +232,17 @@
         head_neigh_ref[:, lanes] = in_ref[8 + z, 48:].astype(F32)[:153]
 
 
-def place(parts):
+def place(parts, scores):
     first = jax.ShapeDtypeStruct((48, 1024), F32)
     head = jax.ShapeDtypeStruct((153, 1024), F32)
     return pl.pallas_call(
         place_kernel,
-        out_shape=(first, first, head, head),
-        in_specs=vmem(1),
-        out_specs=tuple(vmem(4)),
+        out_shape=(jax.ShapeDtypeStruct((TGT, 153), BF), first, first, head, head),
+        in_specs=vmem(5),
+        out_specs=tuple(vmem(5)),
         cost_estimate=pl.CostEstimate(flops=1_000_000, bytes_accessed=2_500_000, transcendentals=0),
         name="place",
-    )(parts)
+    )(parts, *scores)
 
 
 def on_device(
@@ -225,33 +259,29 @@
     logit_grad,
 ):
     column = lax.axis_index("x") * 256
-    w_local = jnp.concatenate([w_one_self, w_one_neigh], axis=0)
-    w_send = w_local.reshape(96, 4, 256).transpose(1, 0, 2)
-    w_send = jnp.broadcast_to(w_send[None], (4, 4, 96, 256)).reshape(16, 96, 256)
-    w_x = lax.all_to_all(w_send, FEAT, 0, 0, tiled=True).reshape(1536, 256)
-    up_y = lax.all_gather(logit_grad[0], "x", axis=0)
-    neigh_y = lax.all_gather(neigh_two[0], "x", axis=0)
-    count_y = lax.all_gather(count_two[0], "x", axis=0)
+    sent = pack(w_one_self, w_one_neigh, logit_grad[0], neigh_two[0], count_two)
+    received = lax.all_to_all(sent, FEAT, 0, 0, tiled=True)
 
     st = lax.all_to_all(gather(node_ids, neigh_one, count_one, feature_table), FEAT, 0, 0, tiled=True)
 
     w2s_x = lax.dynamic_slice_in_dim(w_two_self.T, column, 256, 1)
     w2n_x = lax.dynamic_slice_in_dim(w_two_neigh.T, column, 256, 1)
-    wt, gh, spread, upt = prepare(w_x, up_y, neigh_y, count_y, w2s_x, w2n_x)
-    grads, scores = layers(
-        st.reshape(1536, 4 * SUB), wt, gh, spread, count_y, upt, jnp.concatenate([w2s_x, w2n_x], axis=1)
+    row = lax.axis_index("y").reshape(1)
+    wt, gh, spread, upt, count_y = prepare(row, received, w2s_x, w2n_x)
+    grads, *scores = layers(
+        lax.axis_index("x").reshape(1), st.reshape(1536, 4 * SUB), wt, gh, spread, count_y, upt, jnp.concatenate([w2s_x, w2n_x], axis=1)
     )
     summed = sum_feat(lax.all_to_all(grads, FEAT, 0, 0, tiled=True))
-    scores = lax.all_to_all(scores.reshape(4, TGT, 153), "x", 0, 0, tiled=True)
-    logits = jnp.sum(scores, axis=0).astype(BF)[None]
+    for step in (1, 2, 3):
+        scores[step] = lax.ppermute(scores[step], "x", [(i, (i + step) % 4) for i in range(4)])
 
     total = jnp.sum(lax.all_to_all(summed, REP, 0, 0, tiled=True), axis=0)
     head = jnp.broadcast_to(total[48:][None], (16, 16, 128))
     head = lax.all_to_all(head, FEAT, 0, 0, tiled=True)[:, :CLS_ROWS].reshape(160, 128)
     final = jnp.concatenate([total[:48], head], axis=0).astype(BF)
     final = lax.all_gather(final, REP, axis=0)
-    grad_self, grad_neigh, head_self, head_neigh = place(final)
-    return logits, grad_self, grad_neigh, head_self.T, head_neigh.T
+    logits, grad_self, grad_neigh, head_self, head_neigh = place(final, scores)
+    return logits[None], grad_self, grad_neigh, head_self.T, head_neigh.T
 
 
 def solution(mesh):

time: 186 us -> 152 us (0.82)
  blocking collectives: 78.6 us -> 40.2 us
  waiting for transfers between devices: 26.5 us -> 36.8 us
  starting transfers between devices: 40.1 us -> 32 us
  Pallas kernels: 32.9 us -> 35.8 us
    all_gather x3 -> x0, blocking collectives: 41.3 us -> none  [the longest x1 20.4 us: on_device(): count_y = lax.all_gather(count_two[0], 'x', axis=0)]
    all_to_all x1, waiting for transfers between devices: 0.01 us -> 15.9 us  [on_device(): lax.all_to_all(gather(node_ids, neigh_one, count_one, feature_table), FEA...]
    all_to_all x1, starting transfers between devices: 18.7 us -> 11.2 us  [on_device(): total = jnp.sum(lax.all_to_all(summed, REP, 0, 0, tiled=True), axis=0)]
    all_to_all x2 -> x1, starting transfers between devices: 11.2 us -> 7.77 us  [on_device(): received = lax.all_to_all(sent, FEAT, 0, 0, tiled=True)]
    all_to_all x2 -> x1, waiting for transfers between devices: 3.36 us -> 0.01 us  [on_device(): received = lax.all_to_all(sent, FEAT, 0, 0, tiled=True)]
    all_to_all x1, blocking collectives: 18.9 us -> 21.8 us  [on_device(): summed = sum_feat(lax.all_to_all(grads, FEAT, 0, 0, tiled=True))]
    ppermute x0 -> x3, starting transfers between devices: none -> 2.86 us  [on_device(): lax.ppermute(scores[step], 'x', [(i, (i + step) % 4) for i in range(4)])]
    pallas_call x1 -> x2, Pallas kernels: 2.45 us -> 4.9 us  [the longest x1 2.52 us: place(): pl.pallas_call(place_kernel, out_shape=(jax.ShapeDtypeStruct((TGT, 153),...]
  transfers between devices with their start and end apart: 5 -> 7, of which waited for: 3 -> 3; matrix products, arithmetic and copies ran while one was open for 1% -> 2% of each run, Pallas kernels for 14% -> 16%
where the time goes in v2:
time: 152 us; the launch traced here: 151 us
  blocking collectives  40.2 us (26%)
  waiting for transfers between devices  36.8 us (24%)
  Pallas kernels  35.8 us (24%)
  starting transfers between devices  32 us (21%)
  local copies, waits for them, and re-layouts  4.83 us (3%)
    all_to_all x1, blocking collectives, on_device(): summed = sum_feat(lax.all_to_all(grads, FEAT, 0, 0, tiled=True))  21.8 us
    pallas_call x1, Pallas kernels, gather(): pl.pallas_call(gather_kernel, out_shape=jax.ShapeDtypeStruct((16, 2 * col...  20.3 us
    all_gather x1, blocking collectives, on_device(): final = lax.all_gather(final, REP, axis=0)  18.4 us
    all_to_all x1, waiting for transfers between devices, on_device(): lax.all_to_all(gather(node_ids, neigh_one, count_one, feature_table), FEA...  15.9 us
    all_to_all x1, waiting for transfers between devices, on_device(): total = jnp.sum(lax.all_to_all(summed, REP, 0, 0, tiled=True), axis=0)  14.4 us
    all_to_all x1, starting transfers between devices, on_device(): total = jnp.sum(lax.all_to_all(summed, REP, 0, 0, tiled=True), axis=0)  11.2 us
    all_to_all x1, starting transfers between devices, on_device(): received = lax.all_to_all(sent, FEAT, 0, 0, tiled=True)  7.77 us
    all_to_all x1, starting transfers between devices, on_device(): lax.all_to_all(gather(node_ids, neigh_one, count_one, feature_table), FEA...  6.61 us
  transfers between devices with their start and end apart: 7, of which 3 were waited for; matrix products, arithmetic and copies ran while one was open for 2% of the time, Pallas kernels for 16%

profile of v2, /device:TPU:1, one launch (start us, length us, event | category | flops | bytes accessed | tf_op | source)
XLA Modules:
  0.0 151.1 jit_solution(480034661594767940)
XLA Ops:
  0.6 1.3 copy.21
  1.9 2.4 %pack.1 = bf16[16,160,256]{2,1,0:T(8,128)(2,1)} custom-call(bf16[48,1024]{1,0:T(8,128)(2,1)} %w_self_ref.1, bf16[48,1024]{1,0:T(8,128)(2,1)} %w_neigh_ref.1, bf16[64,153]{1,0:T(8,128)(2,1)} %bitcast.20, s32[25,64]{1,0:T(8,128)} %bitcast.19, s32[1,64]{1,0:T(1,128)} %count_ref.3), custom_call_target="tpu_custom_call" | custom-call | flops 1000000 | bytes 1500000 | tf_op jit(solution)/shard_map/pack/pallas_call | solution.py:102
  4.3 7.8 %all-to-all-start.1 = ((bf16[16,160,256]{2,1,0:T(8,128)(2,1)}), bf16[16,160,256]{2,1,0:T(8,128)(2,1)}, u32[]{:S(2)}, u32[]{:S(2)}) async-start(bf16[16,160,256]{2,1,0:T(8,128)(2,1)} %pack.1), calls=%async_computation.1 | async-start | bytes 2621440 | tf_op jit(solution)/shard_map/all_to_all | solution.py:263
  12.2 20.3 %gather.1 = bf16[16,96,512]{2,1,0:T(8,128)(2,1)} custom-call(s32[1,8192]{1,0:T(1,128)S(1)} %copy-done.1, s32[1,15,2048]{2,1,0:T(8,128)S(1)} %copy.18.neigh_ref, s32[1,2048]{1,0:T(1,128)S(1)} %copy-done.2, bf16[48,32768]{1,0:T(8,128)(2,1)S(1)} %copy-done), custom_call_target="tpu_custom_call" | custom-call | flops 30000001024 | bytes 5000000 | tf_op jit(solution)/shard_map/gather/pallas_call | solution.py:78
  32.5 0.0 all-to-all-done.1.in_ref
  32.5 6.6 %all-to-all-start = ((bf16[16,96,512]{2,1,0:T(8,128)(2,1)}), bf16[16,96,512]{2,1,0:T(8,128)(2,1)S(1)}, u32[]{:S(2)}, u32[]{:S(2)}) async-start(bf16[16,96,512]{2,1,0:T(8,128)(2,1)} %gather.1), calls=%async_computation | async-start | bytes 3145728 | tf_op jit(solution)/shard_map/all_to_all | solution.py:265
  39.1 0.9 dynamic-slice_bitcast_fusion
  40.1 0.0 copy-start.5
  40.1 0.7 pad_maximum_fusion.w2_ref
  40.8 0.0 copy-done.4
  40.8 3.5 %prepare.1 = (bf16[256,1536]{1,0:T(8,128)(2,1)}, f32[256,512]{1,0:T(8,128)}, bf16[4,128,64]{2,1,0:T(8,128)(2,1)}, bf16[160,256]{1,0:T(8,128)(2,1)}, f32[4,64]{1,0:T(4,128)}) custom-call(s32[1]{0:T(128)} %bitcast.2.y_ref, bf16[16,160,256]{2,1,0:T(8,128)(2,1)} %all-to-all-done.1.in_ref, bf16[153,256]{1,0:T(8,128)(2,1)} %copy-done.5, bf16[153,256]{1,0:T(8,128)(2,1)} %copy-done.4), custom_call_target="tpu_custom_call" | custom-call | flops 6000000000 | bytes 2000000 | tf_op jit(solution)/shard_map/prepare/pallas_call | solution.py:137
  44.3 15.9 %all-to-all-done = bf16[16,96,512]{2,1,0:T(8,128)(2,1)S(1)} async-done(((bf16[16,96,512]{2,1,0:T(8,128)(2,1)}), bf16[16,96,512]{2,1,0:T(8,128)(2,1)S(1)}, u32[]{:S(2)}, u32[]{:S(2)}) %all-to-all-start) | async-done | bytes 1572896 | tf_op jit(solution)/shard_map/all_to_all | solution.py:265
  60.1 1.2 copy-done.3
  61.3 4.9 %layers.1 = (bf16[16,128,256]{2,1,0:T(8,128)(2,1)}, f32[64,153]{1,0:T(8,128)}, f32[64,153]{1,0:T(8,128)}, f32[64,153]{1,0:T(8,128)}, f32[64,153]{1,0:T(8,128)}) custom-call(s32[1]{0:T(128)} %bitcast.x_ref, bf16[1536,512]{1,0:T(8,128)(2,1)} %bitcast.17, bf16[256,1536]{1,0:T(8,128)(2,1)} %get-tuple-element.20.wt_ref, f32[256,512]{1,0:T(8,128)} %get-tuple-element.21.gh_ref, ...), custom_call_target="tpu_custom_call" | custom-call | flops 6000000000 | bytes 4000000 | tf_op jit(solution)/shard_map/layers/pallas_call | solution.py:189
  66.3 21.8 %all_to_all.25.in_ref = bf16[16,128,256]{2,1,0:T(8,128)(2,1)} all-to-all(bf16[16,128,256]{2,1,0:T(8,128)(2,1)} %get-tuple-element.25), channel_id=1, replica_groups=mesh['y'=4,'x'=4,'z'=8,'c'=2] {'y','x'}, dimensions={0} | all-to-all | bytes 2097152 | tf_op jit(solution)/shard_map/all_to_all | solution.py:274
  88.1 2.2 %sum_feat.1 = f32[16,64,128]{2,1,0:T(8,128)} custom-call(bf16[16,128,256]{2,1,0:T(8,128)(2,1)} %all_to_all.25.in_ref), custom_call_target="tpu_custom_call" | custom-call | flops 10000000 | bytes 1500000 | tf_op jit(solution)/shard_map/sum_feat/pallas_call | solution.py:215
  90.3 11.2 %all-to-all-start.3 = ((f32[16,64,128]{2,1,0:T(8,128)}), f32[16,64,128]{2,1,0:T(8,128)S(1)}, u32[]{:S(2)}, u32[]{:S(2)}) async-start(f32[16,64,128]{2,1,0:T(8,128)} %sum_feat.1), calls=%async_computation.3 | async-start | bytes 1048576 | tf_op jit(solution)/shard_map/all_to_all | solution.py:278
  101.5 0.4 collective-permute-start
  101.9 1.0 collective-permute-start.1
  102.9 1.4 collective-permute-start.2
  104.4 14.4 %all-to-all-done.3 = f32[16,64,128]{2,1,0:T(8,128)S(1)} async-done(((f32[16,64,128]{2,1,0:T(8,128)}), f32[16,64,128]{2,1,0:T(8,128)S(1)}, u32[]{:S(2)}, u32[]{:S(2)}) %all-to-all-start.3) | async-done | bytes 524320 | tf_op jit(solution)/shard_map/all_to_all | solution.py:278
  118.8 0.6 broadcast_in_dim.4
  119.5 3.5 %all-to-all-start.4 = ((bf16[16,16,128]{2,1,0:T(8,128)(2,1)}), bf16[16,16,128]{2,1,0:T(8,128)(2,1)S(1)}, u32[]{:S(2)}, u32[]{:S(2)}) async-start(bf16[16,16,128]{2,1,0:T(8,128)(2,1)} %broadcast_in_dim.4), calls=%async_computation.4 | async-start | bytes 131072 | tf_op jit(solution)/shard_map/all_to_all | solution.py:280
  123.0 6.4 %all-to-all-done.4 = bf16[16,16,128]{2,1,0:T(8,128)(2,1)S(1)} async-done(((bf16[16,16,128]{2,1,0:T(8,128)(2,1)}), bf16[16,16,128]{2,1,0:T(8,128)(2,1)S(1)}, u32[]{:S(2)}, u32[]{:S(2)}) %all-to-all-start.4) | async-done | bytes 65568 | tf_op jit(solution)/shard_map/all_to_all | solution.py:280
  129.5 18.4 %all_gather.4.in_ref = bf16[16,208,128]{2,1,0:T(8,128)(2,1)} all-gather(bf16[1,208,128]{2,1,0:T(8,128)(2,1)S(1)} %pad_maximum_fusion.1), channel_id=1, replica_groups=mesh['y'=4,'x'=4,'z'=8,'c'=2] {'z','c'}, dimensions={0}, use_global_device_ids=true | all-gather | bytes 905216 | tf_op jit(solution)/shard_map/all_gather | solution.py:282
  147.9 0.0 collective-permute-done.score1
  147.9 0.0 collective-permute-done.1.score2
  147.9 0.0 collective-permute-done.2.score3
  147.9 0.6 copy-done.7
  148.5 0.0 copy-done.8
  148.6 0.0 copy-done.9
  148.6 2.5 %place.1 = (bf16[64,153]{1,0:T(8,128)(2,1)}, f32[48,1024]{1,0:T(8,128)}, f32[48,1024]{1,0:T(8,128)}, f32[153,1024]{1,0:T(8,128)}, f32[153,1024]{1,0:T(8,128)}) custom-call(bf16[16,208,128]{2,1,0:T(8,128)(2,1)} %all_gather.4.in_ref, f32[64,153]{1,0:T(8,128)} %get-tuple-element.26.score0, f32[64,153]{1,0:T(8,128)} %copy-done.7, f32[64,153]{1,0:T(8,128)} %copy-done.8, ...), custom_call_target="tpu_custom_call" | custom-call | flops 1000000 | bytes 2500000 | tf_op jit(solution)/shard_map/place/pallas_call | solution.py:238
  (26 shorter events, 0.2 us)
Async XLA Ops:
  1.9 10.2 %copy-start = (bf16[48,32768]{1,0:T(8,128)(2,1)S(1)}, bf16[48,32768]{1,0:T(8,128)(2,1)}, u32[]{:S(2)}) copy-start(bf16[48,32768]{1,0:T(8,128)(2,1)} %table_ref.1) | copy-start | bytes 9437188
  4.3 7.8 %copy-start.6 = (s32[1,15,2048]{2,0,1:T(1,128)S(1)}, s32[1,15,2048]{2,0,1:T(1,128)}, u32[]{:S(2)}) copy-start(s32[1,15,2048]{2,0,1:T(1,128)} %param.13) | copy-start | bytes 368644
  4.3 7.9 %copy-start.1 = (s32[1,8192]{1,0:T(1,128)S(1)}, s32[1,8192]{1,0:T(1,128)}, u32[]{:S(2)}) copy-start(s32[1,8192]{1,0:T(1,128)} %ids_ref.1) | copy-start | bytes 98308
  4.3 7.9 %copy-start.2 = (s32[1,2048]{1,0:T(1,128)S(1)}, s32[1,2048]{1,0:T(1,128)}, u32[]{:S(2)}) copy-start(s32[1,2048]{1,0:T(1,128)} %count_ref.2) | copy-start | bytes 24580
  4.3 28.2 %all-to-all-start.1 = ((bf16[16,160,256]{2,1,0:T(8,128)(2,1)}), bf16[16,160,256]{2,1,0:T(8,128)(2,1)}, u32[]{:S(2)}, u32[]{:S(2)}) async-start(bf16[16,160,256]{2,1,0:T(8,128)(2,1)} %pack.1), calls=%async_computation.1 | async-start | bytes 2621440 | tf_op jit(solution)/shard_map/all_to_all | solution.py:263
  32.5 27.7 %all-to-all-start = ((bf16[16,96,512]{2,1,0:T(8,128)(2,1)}), bf16[16,96,512]{2,1,0:T(8,128)(2,1)S(1)}, u32[]{:S(2)}, u32[]{:S(2)}) async-start(bf16[16,96,512]{2,1,0:T(8,128)(2,1)} %gather.1), calls=%async_computation | async-start | bytes 3145728 | tf_op jit(solution)/shard_map/all_to_all | solution.py:265
  40.1 0.7 copy-start.4
  40.1 0.7 copy-start.5
  60.1 1.2 copy-start.3
  88.1 13.4 %copy-start.12 = (f32[64,153]{1,0:T(8,128)S(1)}, f32[64,153]{1,0:T(8,128)}, u32[]{:S(2)}) copy-start(f32[64,153]{1,0:T(8,128)} %get-tuple-element.27) | copy-start | bytes 117508
  88.1 13.8 %copy-start.11 = (f32[64,153]{1,0:T(8,128)S(1)}, f32[64,153]{1,0:T(8,128)}, u32[]{:S(2)}) copy-start(f32[64,153]{1,0:T(8,128)} %get-tuple-element.28) | copy-start | bytes 117508
  88.1 14.8 %copy-start.10 = (f32[64,153]{1,0:T(8,128)S(1)}, f32[64,153]{1,0:T(8,128)}, u32[]{:S(2)}) copy-start(f32[64,153]{1,0:T(8,128)} %get-tuple-element.29) | copy-start | bytes 117508
  90.3 28.5 %all-to-all-start.3 = ((f32[16,64,128]{2,1,0:T(8,128)}), f32[16,64,128]{2,1,0:T(8,128)S(1)}, u32[]{:S(2)}, u32[]{:S(2)}) async-start(f32[16,64,128]{2,1,0:T(8,128)} %sum_feat.1), calls=%async_computation.3 | async-start | bytes 1048576 | tf_op jit(solution)/shard_map/all_to_all | solution.py:278
  101.5 46.4 %collective-permute-start = (f32[64,153]{1,0:T(8,128)S(1)}, f32[64,153]{1,0:T(8,128)S(1)}, u32[]{:S(2)}, u32[]{:S(2)}) collective-permute-start(f32[64,153]{1,0:T(8,128)S(1)} %copy-done.12), channel_id=1, source_target_pairs={{0,16},{16,32},{32,48},{48,0},{1,17},{17,33},{33,49},{49,1},{2,18}... | collective-permute-start | bytes 117512 | tf_op jit(solution)/shard_map/ppermute | solution.py:276
  101.9 46.0 %collective-permute-start.1 = (f32[64,153]{1,0:T(8,128)S(1)}, f32[64,153]{1,0:T(8,128)S(1)}, u32[]{:S(2)}, u32[]{:S(2)}) collective-permute-start(f32[64,153]{1,0:T(8,128)S(1)} %copy-done.11), channel_id=1, source_target_pairs={{0,32},{16,48},{32,0},{48,16},{1,33},{17,49},{33,1},{49,17},{2,34}... | collective-permute-start | bytes 117512 | tf_op jit(solution)/shard_map/ppermute | solution.py:276
  102.9 45.0 %collective-permute-start.2 = (f32[64,153]{1,0:T(8,128)S(1)}, f32[64,153]{1,0:T(8,128)S(1)}, u32[]{:S(2)}, u32[]{:S(2)}) collective-permute-start(f32[64,153]{1,0:T(8,128)S(1)} %copy-done.10), channel_id=1, source_target_pairs={{0,48},{16,0},{32,16},{48,32},{1,49},{17,1},{33,17},{49,33},{2,50}... | collective-permute-start | bytes 117512 | tf_op jit(solution)/shard_map/ppermute | solution.py:276
  119.5 10.0 %all-to-all-start.4 = ((bf16[16,16,128]{2,1,0:T(8,128)(2,1)}), bf16[16,16,128]{2,1,0:T(8,128)(2,1)S(1)}, u32[]{:S(2)}, u32[]{:S(2)}) async-start(bf16[16,16,128]{2,1,0:T(8,128)(2,1)} %broadcast_in_dim.4), calls=%async_computation.4 | async-start | bytes 131072 | tf_op jit(solution)/shard_map/all_to_all | solution.py:280
  147.9 0.6 copy-start.7
  147.9 0.6 copy-start.8
  147.9 0.7 copy-start.9

commit v3 on v2

--- a/solution.py
+++ b/solution.py
@@ -18,7 +18,9 @@
 TGT = 64
 CHUNK = 512
 LISTS = 160
-CLS_ROWS = 10
+CLS_ROWS = 20
+CLS_PAD = 24
+PIECE = 128
 
 
 def mm(first, second):
@@ -112,6 +114,7 @@
 def prepare_kernel(y_ref, in_ref, w2s_ref, w2n_ref, wt_ref, gh_ref, spread_ref, upt_ref, count_ref):
     wt_ref[...] = jnp.concatenate([in_ref[f, :96] for f in range(16)], axis=0).T
     position = lax.broadcasted_iota(jnp.int32, (SUB, TGT), 0).astype(F32)
+    classes = []
     for g in range(4):
         upstream = in_ref[4 * y_ref[0] + g, 96:]
         turned = upstream.astype(F32).T
@@ -128,9 +131,14 @@
         low = (near_grad - high.astype(F32)).astype(BF)
         grad = mm_nt(high, spread) + mm_nt(low, spread)
         gh_ref[:, g * SUB : (g + 1) * SUB] = grad + jnp.concatenate([own.T, jnp.zeros(own.T.shape, F32)], axis=1)
-        upt_ref[:153, g * TGT : (g + 1) * TGT] = turned[:153].astype(BF)
+        classes.append(turned[:153])
         count_ref[pl.ds(g, 1), :] = count
-    upt_ref[153:] = jnp.zeros((7, 4 * TGT), BF)
+    classes = jnp.concatenate(classes, axis=1)
+    blocks = []
+    for z in range(8):
+        block = classes[z * CLS_ROWS : min((z + 1) * CLS_ROWS, 153)]
+        blocks += [block, jnp.zeros((CLS_PAD - block.shape[0], 4 * TGT), F32)]
+    upt_ref[...] = jnp.concatenate(blocks, axis=0).astype(BF)
 
 
 def prepare(row, received, w2s_x, w2n_x):
@@ -140,7 +148,7 @@
             jax.ShapeDtypeStruct((256, 1536), BF),
             jax.ShapeDtypeStruct((256, 4 * SUB), F32),
             jax.ShapeDtypeStruct((4, SUB, TGT), BF),
-            jax.ShapeDtypeStruct((160, 4 * TGT), BF),
+            jax.ShapeDtypeStruct((8 * CLS_PAD, 4 * TGT), BF),
             jax.ShapeDtypeStruct((4, TGT), F32),
         ),
         in_specs=[pl.BlockSpec(memory_space=pltpu.SMEM)] + vmem(3),
@@ -150,7 +158,7 @@
     )(row, received, w2s_x, w2n_x)
 
 
-def layers_kernel(x_ref, st_ref, wt_ref, gh_ref, spread_ref, count_ref, upt_ref, w2_ref, grads_ref, *scores_refs):
+def layers_kernel(place_ref, st_ref, wt_ref, gh_ref, spread_ref, count_ref, upt_ref, w2_ref, keep_ref, send_ref, *scores_refs):
     pre = mm(wt_ref[...], st_ref[...])
     square = pre * pre
     bend = jnp.tanh(GELU_C * pre * (1.0 + 0.044715 * square))
@@ -158,10 +166,7 @@
     hidden = (pre * half).astype(BF)
     slope = half + 0.5 * pre * (1.0 - bend * bend) * (GELU_C * (1.0 + 3.0 * 0.044715 * square))
     grad_pre = (gh_ref[...] * slope).astype(BF)
-    grad = mm_nt(st_ref[...], grad_pre).astype(BF)
-    rows = grad.shape[0] // 16
-    for f in range(16):
-        grads_ref[f, :rows] = grad[f * rows : (f + 1) * rows]
+    grad = mm_nt(st_ref[...], grad_pre)
     own, near = [], []
     for g in range(4):
         nodes = hidden[:, g * SUB : (g + 1) * SUB]
@@ -172,77 +177,109 @@
     for g in range(4):
         for step, scores_ref in enumerate(scores_refs):
 
-            @pl.when(lax.rem(x_ref[0] + step, 4) == g)
+            @pl.when(lax.rem(place_ref[0] + step, 4) == g)
             def _():
                 scores_ref[...] = scores[g * TGT : (g + 1) * TGT]
 
     head = mm_nt(upt_ref[...], both)
-    for f in range(16):
-        part = head[f * CLS_ROWS : (f + 1) * CLS_ROWS].astype(BF)
-        grads_ref[f, 96 : 96 + CLS_ROWS] = part[:, :256]
-        grads_ref[f, 112 : 112 + CLS_ROWS] = part[:, 256:]
-        grads_ref[f, 96 + CLS_ROWS : 112] = jnp.zeros((16 - CLS_ROWS, 256), BF)
-        grads_ref[f, 112 + CLS_ROWS :] = jnp.zeros((16 - CLS_ROWS, 256), BF)
-
-
-def layers(column, st, wt, gh, spread, count_y, upt, w2_x):
+
+    def pieces(side):
+        for z in range(8):
+            rows = []
+            for f in range(16):
+                tile = (z - 6 * f) % 8
+                if tile < 6:
+                    start = f * 96 + side * 48 + tile * 8
+                    rows.append(grad[start : start + 8])
+            rows.append(head[z * CLS_PAD : (z + 1) * CLS_PAD, side * 256 : (side + 1) * 256])
+            rows.append(jnp.zeros((PIECE - 96 - CLS_PAD, 256), F32))
+            yield z, jnp.concatenate(rows, axis=0)
+
+    for side in range(2):
+
+        @pl.when(place_ref[1] == side)
+        def _():
+            for z, piece in pieces(side):
+                keep_ref[z] = piece
+            for z, piece in pieces(1 - side):
+                send_ref[z] = piece.astype(BF)
+
+
+def layers(position, st, wt, gh, spread, count_y, upt, w2_x):
     return pl.pallas_call(
         layers_kernel,
         out_shape=(
-            jax.ShapeDtypeStruct((16, 128, 256), BF),
+            jax.ShapeDtypeStruct((8, PIECE, 256), F32),
+            jax.ShapeDtypeStruct((8, PIECE, 256), BF),
             *[jax.ShapeDtypeStruct((TGT, 153), F32)] * 4,
         ),
         in_specs=[pl.BlockSpec(memory_space=pltpu.SMEM)] + vmem(7),
-        out_specs=tuple(vmem(5)),
+        out_specs=tuple(vmem(6)),
         cost_estimate=pl.CostEstimate(flops=6_000_000_000, bytes_accessed=4_000_000, transcendentals=200_000),
         name="layers",
-    )(column, st, wt, gh, spread, count_y, upt, w2_x)
-
-
-def sum_feat_kernel(in_ref, out_ref):
+    )(position, st, wt, gh, spread, count_y, upt, w2_x)
+
+
+def sum_z_kernel(z_ref, in_ref, out_ref, total):
+    total[...] = sum(in_ref[z].astype(F32) for z in range(8))
+    absent = 3 - lax.div(z_ref[0], 2)
+    for f in range(16):
+        slot = (f // 4) * 3 + f % 4 - (f % 4 > absent).astype(jnp.int32)
+        own = total[pl.ds(pl.multiple_of(slot * 8, 8), 8), :]
+        out_ref[f] = jnp.concatenate([own, total[96 : 96 + CLS_PAD]], axis=0).astype(BF)
+
+
+def sum_z(z, parts):
+    return pl.pallas_call(
+        sum_z_kernel,
+        out_shape=jax.ShapeDtypeStruct((16, 8 + CLS_PAD, 256), BF),
+        in_specs=[pl.BlockSpec(memory_space=pltpu.SMEM)] + vmem(1),
+        out_specs=vmem(1)[0],
+        scratch_shapes=[pltpu.VMEM((PIECE, 256), F32)],
+        cost_estimate=pl.CostEstimate(flops=10_000_000, bytes_accessed=1_500_000, transcendentals=0),
+        name="sum_z",
+    )(z, parts)
+
+
+def sum_y_kernel(in_ref, out_ref):
     for x in range(4):
         total = sum(in_ref[4 * y + x].astype(F32) for y in range(4))
-        for h in range(2):
-            half = total[:, h * 128 : (h + 1) * 128]
-            z = 2 * x + h
-            out_ref[2 * z, :48] = half[:48]
-            out_ref[2 * z + 1, :48] = half[48:96]
-            out_ref[z, 48:] = half[96:112]
-            out_ref[8 + z, 48:] = half[112:]
-
-
-def sum_feat(parts):
-    return pl.pallas_call(
-        sum_feat_kernel,
-        out_shape=jax.ShapeDtypeStruct((16, 64, 128), F32),
+        out_ref[:, x * 256 : (x + 1) * 256] = total[: 8 + CLS_ROWS].astype(BF)
+
+
+def sum_y(parts):
+    return pl.pallas_call(
+        sum_y_kernel,
+        out_shape=jax.ShapeDtypeStruct((8 + CLS_ROWS, 1024), BF),
         in_specs=vmem(1),
         out_specs=vmem(1)[0],
-        cost_estimate=pl.CostEstimate(flops=10_000_000, bytes_accessed=1_500_000, transcendentals=0),
-        name="sum_feat",
+        cost_estimate=pl.CostEstimate(flops=1_000_000, bytes_accessed=600_000, transcendentals=0),
+        name="sum_y",
     )(parts)
 
 
-def place_kernel(in_ref, score0, score1, score2, score3, logits_ref, self_ref, neigh_ref, head_self_ref, head_neigh_ref):
+def place_kernel(x_ref, in_ref, score0, score1, score2, score3, logits_ref, self_ref, neigh_ref, head_self_ref, head_neigh_ref):
     logits_ref[...] = (score0[...] + score1[...] + score2[...] + score3[...]).astype(BF)
-    for z in range(8):
-        lanes = slice(z * 128, (z + 1) * 128)
-        self_ref[:, lanes] = in_ref[2 * z, :48].astype(F32)
-        neigh_ref[:, lanes] = in_ref[2 * z + 1, :48].astype(F32)
-        head_self_ref[:, lanes] = in_ref[z, 48:].astype(F32)[:153]
-        head_neigh_ref[:, lanes] = in_ref[8 + z, 48:].astype(F32)[:153]
-
-
-def place(parts, scores):
+    for side, (first_ref, head_ref) in enumerate(((self_ref, head_self_ref), (neigh_ref, head_neigh_ref))):
+        for tile in range(6):
+            owner = lax.rem(tile + 6 * x_ref[0], 8)
+            first_ref[tile * 8 : (tile + 1) * 8] = in_ref[2 * owner + side].astype(F32)[:8]
+        for z in range(8):
+            end = min((z + 1) * CLS_ROWS, 153)
+            head_ref[z * CLS_ROWS : end] = in_ref[2 * z + side].astype(F32)[8 : 8 + end - z * CLS_ROWS]
+
+
+def place(x, parts, scores):
     first = jax.ShapeDtypeStruct((48, 1024), F32)
     head = jax.ShapeDtypeStruct((153, 1024), F32)
     return pl.pallas_call(
         place_kernel,
         out_shape=(jax.ShapeDtypeStruct((TGT, 153), BF), first, first, head, head),
-        in_specs=vmem(5),
+        in_specs=[pl.BlockSpec(memory_space=pltpu.SMEM)] + vmem(5),
         out_specs=tuple(vmem(5)),
         cost_estimate=pl.CostEstimate(flops=1_000_000, bytes_accessed=2_500_000, transcendentals=0),
         name="place",
-    )(parts, *scores)
+    )(x, parts, *scores)
 
 
 def on_device(
@@ -268,19 +305,19 @@
     w2n_x = lax.dynamic_slice_in_dim(w_two_neigh.T, column, 256, 1)
     row = lax.axis_index("y").reshape(1)
     wt, gh, spread, upt, count_y = prepare(row, received, w2s_x, w2n_x)
-    grads, *scores = layers(
-        lax.axis_index("x").reshape(1), st.reshape(1536, 4 * SUB), wt, gh, spread, count_y, upt, jnp.concatenate([w2s_x, w2n_x], axis=1)
+    position = jnp.stack([lax.axis_index("x"), lax.axis_index("c")])
+    keep, send, *scores = layers(
+        position, st.reshape(1536, 4 * SUB), wt, gh, spread, count_y, upt, jnp.concatenate([w2s_x, w2n_x], axis=1)
     )
-    summed = sum_feat(lax.all_to_all(grads, FEAT, 0, 0, tiled=True))
     for step in (1, 2, 3):
         scores[step] = lax.ppermute(scores[step], "x", [(i, (i + step) % 4) for i in range(4)])
 
-    total = jnp.sum(lax.all_to_all(summed, REP, 0, 0, tiled=True), axis=0)
-    head = jnp.broadcast_to(total[48:][None], (16, 16, 128))
-    head = lax.all_to_all(head, FEAT, 0, 0, tiled=True)[:, :CLS_ROWS].reshape(160, 128)
-    final = jnp.concatenate([total[:48], head], axis=0).astype(BF)
+    pair = (keep + lax.ppermute(send, "c", [(0, 1), (1, 0)]).astype(F32)).astype(BF)
+    pair, scores = lax.optimization_barrier((lax.all_to_all(pair, "z", 0, 0, tiled=True), scores))
+    over_z = sum_z(lax.axis_index("z").reshape(1), pair)
+    final = sum_y(lax.all_to_all(over_z, FEAT, 0, 0, tiled=True))
     final = lax.all_gather(final, REP, axis=0)
-    logits, grad_self, grad_neigh, head_self, head_neigh = place(final, scores)
+    logits, grad_self, grad_neigh, head_self, head_neigh = place(position[:1], final, scores)
     return logits[None], grad_self, grad_neigh, head_self.T, head_neigh.T
 
 

time: 152 us -> 141 us (0.928)
  blocking collectives: 40.2 us -> 32.8 us
  waiting for transfers between devices: 36.8 us -> 32.1 us
  starting transfers between devices: 32 us -> 29.2 us
  other arithmetic: 0.74 us -> 3.49 us
  Pallas kernels: 35.8 us -> 37.4 us
    all_to_all x1, blocking collectives: 21.8 us -> 12.5 us  [on_device(): final = sum_y(lax.all_to_all(over_z, FEAT, 0, 0, tiled=True))]
    all_to_all x2 -> x1, waiting for transfers between devices: 20.9 us -> 11.6 us  [on_device(): lax.all_to_all(pair, 'z', 0, 0, tiled=True)]
    all_to_all x2 -> x1, starting transfers between devices: 14.7 us -> 8.18 us  [on_device(): lax.all_to_all(pair, 'z', 0, 0, tiled=True)]
    ppermute x0 -> x1, starting transfers between devices: none -> 3.85 us  [on_device(): lax.ppermute(send, 'c', [(0, 1), (1, 0)]).astype(F32)]
    ppermute x3, waiting for transfers between devices: 0.01 us -> 3.45 us  [on_device(): lax.ppermute(scores[step], 'x', [(i, (i + step) % 4) for i in range(4)])]
    convert_element_type x0 -> x1, other arithmetic: none -> 2.18 us  [on_device(): (keep + lax.ppermute(send, 'c', [(0, 1), (1, 0)]).astype(F32)).astype(BF)]
    all_gather x1, blocking collectives: 18.4 us -> 20.3 us  [on_device(): final = lax.all_gather(final, REP, axis=0)]
    ppermute x0 -> x1, waiting for transfers between devices: none -> 1.75 us  [on_device(): lax.ppermute(send, 'c', [(0, 1), (1, 0)]).astype(F32)]
  transfers between devices with their start and end apart: 7 -> 7, of which waited for: 3 -> 4; matrix products, arithmetic and copies ran while one was open for 2% -> 2% of each run, Pallas kernels for 16% -> 17%
where the time goes in v3:
time: 141 us; the launch traced here: 140 us
  Pallas kernels  37.4 us (27%)
  blocking collectives  32.8 us (23%)
  waiting for transfers between devices  32.1 us (23%)
  starting transfers between devices  29.2 us (21%)
  local copies, waits for them, and re-layouts  4.32 us (3%)
  other arithmetic  3.49 us (2%)
    all_gather x1, blocking collectives, on_device(): final = lax.all_gather(final, REP, axis=0)  20.3 us
    pallas_call x1, Pallas kernels, gather(): pl.pallas_call(gather_kernel, out_shape=jax.ShapeDtypeStruct((16, 2 * col...  20.3 us
    all_to_all x1, waiting for transfers between devices, on_device(): lax.all_to_all(gather(node_ids, neigh_one, count_one, feature_table), FEA...  15.3 us
    all_to_all x1, blocking collectives, on_device(): final = sum_y(lax.all_to_all(over_z, FEAT, 0, 0, tiled=True))  12.5 us
    all_to_all x1, waiting for transfers between devices, on_device(): lax.all_to_all(pair, 'z', 0, 0, tiled=True)  11.6 us
    all_to_all x1, starting transfers between devices, on_device(): lax.all_to_all(pair, 'z', 0, 0, tiled=True)  8.18 us
    all_to_all x1, starting transfers between devices, on_device(): received = lax.all_to_all(sent, FEAT, 0, 0, tiled=True)  7.77 us
    all_to_all x1, starting transfers between devices, on_device(): lax.all_to_all(gather(node_ids, neigh_one, count_one, feature_table), FEA...  6.61 us
  transfers between devices with their start and end apart: 7, of which 4 were waited for; matrix products, arithmetic and copies ran while one was open for 2% of the time, Pallas kernels for 17%

profile of v3, /device:TPU:1, one launch (start us, length us, event | category | flops | bytes accessed | tf_op | source)
XLA Modules:
  0.0 140.1 jit_solution(955681761013631437)
XLA Ops:
  0.6 1.3 copy.20
  1.9 2.4 %pack.1 = bf16[16,160,256]{2,1,0:T(8,128)(2,1)} custom-call(bf16[48,1024]{1,0:T(8,128)(2,1)} %w_self_ref.1, bf16[48,1024]{1,0:T(8,128)(2,1)} %w_neigh_ref.1, bf16[64,153]{1,0:T(8,128)(2,1)} %bitcast.20, s32[25,64]{1,0:T(8,128)} %bitcast.19, s32[1,64]{1,0:T(1,128)} %count_ref.3), custom_call_target="tpu_custom_call" | custom-call | flops 1000000 | bytes 1500000 | tf_op jit(solution)/shard_map/pack/pallas_call | solution.py:104
  4.3 7.8 %all-to-all-start.1 = ((bf16[16,160,256]{2,1,0:T(8,128)(2,1)}), bf16[16,160,256]{2,1,0:T(8,128)(2,1)}, u32[]{:S(2)}, u32[]{:S(2)}) async-start(bf16[16,160,256]{2,1,0:T(8,128)(2,1)} %pack.1), calls=%async_computation.1 | async-start | bytes 2621440 | tf_op jit(solution)/shard_map/all_to_all | solution.py:300
  12.2 20.3 %gather.1 = bf16[16,96,512]{2,1,0:T(8,128)(2,1)} custom-call(s32[1,8192]{1,0:T(1,128)S(1)} %copy-done.1, s32[1,15,2048]{2,1,0:T(8,128)S(1)} %copy.17.neigh_ref, s32[1,2048]{1,0:T(1,128)S(1)} %copy-done.2, bf16[48,32768]{1,0:T(8,128)(2,1)S(1)} %copy-done), custom_call_target="tpu_custom_call" | custom-call | flops 30000001024 | bytes 5000000 | tf_op jit(solution)/shard_map/gather/pallas_call | solution.py:80
  32.5 0.0 all-to-all-done.1.in_ref
  32.5 6.6 %all-to-all-start = ((bf16[16,96,512]{2,1,0:T(8,128)(2,1)}), bf16[16,96,512]{2,1,0:T(8,128)(2,1)S(1)}, u32[]{:S(2)}, u32[]{:S(2)}) async-start(bf16[16,96,512]{2,1,0:T(8,128)(2,1)} %gather.1), calls=%async_computation | async-start | bytes 3145728 | tf_op jit(solution)/shard_map/all_to_all | solution.py:302
  39.1 0.6 pad_add_fusion.place_ref
  39.7 0.9 dynamic-slice_bitcast_fusion
  40.7 0.0 copy-start.5
  40.7 0.0 copy-start.6
  40.7 0.7 pad_maximum_fusion.w2_ref
  41.4 3.5 %prepare.1 = (bf16[256,1536]{1,0:T(8,128)(2,1)}, f32[256,512]{1,0:T(8,128)}, bf16[4,128,64]{2,1,0:T(8,128)(2,1)}, bf16[192,256]{1,0:T(8,128)(2,1)}, f32[4,64]{1,0:T(4,128)}) custom-call(s32[1]{0:T(128)} %bitcast.4.y_ref, bf16[16,160,256]{2,1,0:T(8,128)(2,1)} %all-to-all-done.1.in_ref, bf16[153,256]{1,0:T(8,128)(2,1)} %copy-done.6, bf16[153,256]{1,0:T(8,128)(2,1)} %copy-done.5), custom_call_target="tpu_custom_call" | custom-call | flops 6000000000 | bytes 2000000 | tf_op jit(solution)/shard_map/prepare/pallas_call | solution.py:145
  44.9 15.3 %all-to-all-done = bf16[16,96,512]{2,1,0:T(8,128)(2,1)S(1)} async-done(((bf16[16,96,512]{2,1,0:T(8,128)(2,1)}), bf16[16,96,512]{2,1,0:T(8,128)(2,1)S(1)}, u32[]{:S(2)}, u32[]{:S(2)}) %all-to-all-start) | async-done | bytes 1572896 | tf_op jit(solution)/shard_map/all_to_all | solution.py:302
  60.1 1.2 copy-done.4
  61.3 5.3 %layers.1 = (f32[8,128,256]{2,1,0:T(8,128)}, bf16[8,128,256]{2,1,0:T(8,128)(2,1)}, f32[64,153]{1,0:T(8,128)}, f32[64,153]{1,0:T(8,128)}, f32[64,153]{1,0:T(8,128)}, /*index=5*/f32[64,153]{1,0:T(8,128)}) custom-call(s32[2]{0:T(128)} %pad_add_fusion.place_ref, bf16[1536,512]{1,0:T(8,128)(2,1)} %bitcast.17, bf16[256,1536]{1,0:T(8,128)(2,1)} %get-tuple-element.26.wt_ref, ...), custom_call_target="tpu_custom_call" | custom-call | flops 6000000000 | bytes 4000000 | tf_op jit(solution)/shard_map/layers/pallas_call | solution.py:209
  66.6 3.8 %collective-permute-start = (bf16[8,128,256]{2,1,0:T(8,128)(2,1)}, bf16[8,128,256]{2,1,0:T(8,128)(2,1)S(1)}, u32[]{:S(2)}, u32[]{:S(2)}) collective-permute-start(bf16[8,128,256]{2,1,0:T(8,128)(2,1)} %get-tuple-element.32), channel_id=1, source_target_pairs={{0,1},{1,0},{2,3},{3,2},{4,5},{5,4},{6,7},{7,6},{8,9},{9,8},{10,11... | collective-permute-start | bytes 1572872 | tf_op jit(solution)/shard_map/ppermute | solution.py:315
  70.5 1.7 %collective-permute-done = bf16[8,128,256]{2,1,0:T(8,128)(2,1)S(1)} collective-permute-done((bf16[8,128,256]{2,1,0:T(8,128)(2,1)}, bf16[8,128,256]{2,1,0:T(8,128)(2,1)S(1)}, u32[]{:S(2)}, u32[]{:S(2)}) %collective-permute-start) | collective-permute-done | bytes 524320 | tf_op jit(solution)/shard_map/ppermute | solution.py:315
  72.2 2.2 %add_convert_fusion = bf16[8,128,256]{2,1,0:T(8,128)(2,1)} fusion(f32[8,128,256]{2,1,0:T(8,128)} %get-tuple-element.31, bf16[8,128,256]{2,1,0:T(8,128)(2,1)S(1)} %collective-permute-done), kind=kLoop, calls=%fused_computation | loop fusion | flops 786432 | bytes 2097152 | tf_op jit(solution)/shard_map/convert_element_type | solution.py:315
  74.4 8.2 %all-to-all-start.2 = ((bf16[8,128,256]{2,1,0:T(8,128)(2,1)}), bf16[8,128,256]{2,1,0:T(8,128)(2,1)S(1)}, u32[]{:S(2)}, u32[]{:S(2)}) async-start(bf16[8,128,256]{2,1,0:T(8,128)(2,1)} %add_convert_fusion), calls=%async_computation.2 | async-start | bytes 1048576 | tf_op jit(solution)/shard_map/all_to_all | solution.py:316
  82.6 0.1 collective-permute-start.1
  82.7 0.2 collective-permute-start.2
  82.9 2.5 %collective-permute-start.3 = (f32[64,153]{1,0:T(8,128)S(1)}, f32[64,153]{1,0:T(8,128)S(1)}, u32[]{:S(2)}, u32[]{:S(2)}) collective-permute-start(f32[64,153]{1,0:T(8,128)S(1)} %copy-done.11), channel_id=1, source_target_pairs={{0,48},{16,0},{32,16},{48,32},{1,49},{17,1},{33,17},{49,33},{2,50}... | collective-permute-start | bytes 117512 | tf_op jit(solution)/shard_map/ppermute | solution.py:313
  85.4 3.4 %collective-permute-done.1.score1 = f32[64,153]{1,0:T(8,128)S(1)} collective-permute-done((f32[64,153]{1,0:T(8,128)S(1)}, f32[64,153]{1,0:T(8,128)S(1)}, u32[]{:S(2)}, u32[]{:S(2)}) %collective-permute-start.1) | collective-permute-done | bytes 39200 | tf_op jit(solution)/shard_map/ppermute | solution.py:313
  88.9 0.0 collective-permute-done.2.score2
  88.9 0.0 collective-permute-done.3.score3
  88.9 11.6 %all-to-all-done.2.in_ref = bf16[8,128,256]{2,1,0:T(8,128)(2,1)S(1)} async-done(((bf16[8,128,256]{2,1,0:T(8,128)(2,1)}), bf16[8,128,256]{2,1,0:T(8,128)(2,1)S(1)}, u32[]{:S(2)}, u32[]{:S(2)}) %all-to-all-start.2) | async-done | bytes 524320 | tf_op jit(solution)/shard_map/all_to_all | solution.py:316
  100.5 0.8 copy-done.3
  101.3 1.8 %sum_z.1 = bf16[16,32,256]{2,1,0:T(8,128)(2,1)} custom-call(s32[1]{0:T(128)} %bitcast.1.z_ref, bf16[8,128,256]{2,1,0:T(8,128)(2,1)} %copy-done.3), custom_call_target="tpu_custom_call" | custom-call | flops 10000000 | bytes 1500000 | tf_op jit(solution)/shard_map/sum_z/pallas_call | solution.py:233
  103.2 12.5 %all_to_all.20.in_ref = bf16[16,32,256]{2,1,0:T(8,128)(2,1)} all-to-all(bf16[16,32,256]{2,1,0:T(8,128)(2,1)} %sum_z.1), channel_id=1, replica_groups=mesh['y'=4,'x'=4,'z'=8,'c'=2] {'y','x'}, dimensions={0} | all-to-all | bytes 524288 | tf_op jit(solution)/shard_map/all_to_all | solution.py:318
  115.7 1.6 %sum_y.1 = bf16[28,1024]{1,0:T(8,128)(2,1)} custom-call(bf16[16,32,256]{2,1,0:T(8,128)(2,1)} %all_to_all.20.in_ref), custom_call_target="tpu_custom_call" | custom-call | flops 1000000 | bytes 600000 | tf_op jit(solution)/shard_map/sum_y/pallas_call | solution.py:251
  117.3 20.3 %all-gather.1.in_ref = bf16[16,28,1024]{2,1,0:T(8,128)(2,1)} all-gather(bf16[1,28,1024]{2,1,0:T(8,128)(2,1)} %bitcast.18), channel_id=2, replica_groups=mesh['y'=4,'x'=4,'z'=8,'c'=2] {'z','c'}, dimensions={0}, use_global_device_ids=true | all-gather | bytes 974848 | tf_op jit(solution)/shard_map/all_gather | solution.py:319
  137.6 2.5 %place.1 = (bf16[64,153]{1,0:T(8,128)(2,1)}, f32[48,1024]{1,0:T(8,128)}, f32[48,1024]{1,0:T(8,128)}, f32[153,1024]{1,0:T(8,128)}, f32[153,1024]{1,0:T(8,128)}) custom-call(s32[1]{0:T(128)} %bitcast.x_ref, bf16[16,28,1024]{2,1,0:T(8,128)(2,1)} %all-gather.1.in_ref, f32[64,153]{1,0:T(8,128)} %get-tuple-element.38.score0, f32[64,153]{1,0:T(8,128)} %copy-done.8, ...), custom_call_target="tpu_custom_call" | custom-call | flops 1000000 | bytes 2500000 | tf_op jit(solution)/shard_map/place/pallas_call | solution.py:275
  (25 shorter events, 0.1 us)
Async XLA Ops:
  1.9 10.2 %copy-start = (bf16[48,32768]{1,0:T(8,128)(2,1)S(1)}, bf16[48,32768]{1,0:T(8,128)(2,1)}, u32[]{:S(2)}) copy-start(bf16[48,32768]{1,0:T(8,128)(2,1)} %table_ref.1) | copy-start | bytes 9437188
  4.3 7.8 %copy-start.7 = (s32[1,15,2048]{2,0,1:T(1,128)S(1)}, s32[1,15,2048]{2,0,1:T(1,128)}, u32[]{:S(2)}) copy-start(s32[1,15,2048]{2,0,1:T(1,128)} %param.13) | copy-start | bytes 368644
  4.3 7.9 %copy-start.1 = (s32[1,8192]{1,0:T(1,128)S(1)}, s32[1,8192]{1,0:T(1,128)}, u32[]{:S(2)}) copy-start(s32[1,8192]{1,0:T(1,128)} %ids_ref.1) | copy-start | bytes 98308
  4.3 7.9 %copy-start.2 = (s32[1,2048]{1,0:T(1,128)S(1)}, s32[1,2048]{1,0:T(1,128)}, u32[]{:S(2)}) copy-start(s32[1,2048]{1,0:T(1,128)} %count_ref.2) | copy-start | bytes 24580
  4.3 28.2 %all-to-all-start.1 = ((bf16[16,160,256]{2,1,0:T(8,128)(2,1)}), bf16[16,160,256]{2,1,0:T(8,128)(2,1)}, u32[]{:S(2)}, u32[]{:S(2)}) async-start(bf16[16,160,256]{2,1,0:T(8,128)(2,1)} %pack.1), calls=%async_computation.1 | async-start | bytes 2621440 | tf_op jit(solution)/shard_map/all_to_all | solution.py:300
  32.5 27.7 %all-to-all-start = ((bf16[16,96,512]{2,1,0:T(8,128)(2,1)}), bf16[16,96,512]{2,1,0:T(8,128)(2,1)S(1)}, u32[]{:S(2)}, u32[]{:S(2)}) async-start(bf16[16,96,512]{2,1,0:T(8,128)(2,1)} %gather.1), calls=%async_computation | async-start | bytes 3145728 | tf_op jit(solution)/shard_map/all_to_all | solution.py:302
  40.7 0.7 copy-start.5
  40.7 0.7 copy-start.6
  60.1 1.2 copy-start.4
  66.6 5.6 %collective-permute-start = (bf16[8,128,256]{2,1,0:T(8,128)(2,1)}, bf16[8,128,256]{2,1,0:T(8,128)(2,1)S(1)}, u32[]{:S(2)}, u32[]{:S(2)}) collective-permute-start(bf16[8,128,256]{2,1,0:T(8,128)(2,1)} %get-tuple-element.32), channel_id=1, source_target_pairs={{0,1},{1,0},{2,3},{3,2},{4,5},{5,4},{6,7},{7,6},{8,9},{9,8},{10,11... | collective-permute-start | bytes 1572872 | tf_op jit(solution)/shard_map/ppermute | solution.py:315
  72.2 10.4 %copy-start.13 = (f32[64,153]{1,0:T(8,128)S(1)}, f32[64,153]{1,0:T(8,128)}, u32[]{:S(2)}) copy-start(f32[64,153]{1,0:T(8,128)} %get-tuple-element.34) | copy-start | bytes 117508
  72.2 10.5 %copy-start.12 = (f32[64,153]{1,0:T(8,128)S(1)}, f32[64,153]{1,0:T(8,128)}, u32[]{:S(2)}) copy-start(f32[64,153]{1,0:T(8,128)} %get-tuple-element.35) | copy-start | bytes 117508
  72.2 10.7 %copy-start.11 = (f32[64,153]{1,0:T(8,128)S(1)}, f32[64,153]{1,0:T(8,128)}, u32[]{:S(2)}) copy-start(f32[64,153]{1,0:T(8,128)} %get-tuple-element.36) | copy-start | bytes 117508
  74.4 26.1 %all-to-all-start.2 = ((bf16[8,128,256]{2,1,0:T(8,128)(2,1)}), bf16[8,128,256]{2,1,0:T(8,128)(2,1)S(1)}, u32[]{:S(2)}, u32[]{:S(2)}) async-start(bf16[8,128,256]{2,1,0:T(8,128)(2,1)} %add_convert_fusion), calls=%async_computation.2 | async-start | bytes 1048576 | tf_op jit(solution)/shard_map/all_to_all | solution.py:316
  82.6 6.3 %collective-permute-start.1 = (f32[64,153]{1,0:T(8,128)S(1)}, f32[64,153]{1,0:T(8,128)S(1)}, u32[]{:S(2)}, u32[]{:S(2)}) collective-permute-start(f32[64,153]{1,0:T(8,128)S(1)} %copy-done.13), channel_id=1, source_target_pairs={{0,16},{16,32},{32,48},{48,0},{1,17},{17,33},{33,49},{49,1},{2,18}... | collective-permute-start | bytes 117512 | tf_op jit(solution)/shard_map/ppermute | solution.py:313
  82.7 6.2 %collective-permute-start.2 = (f32[64,153]{1,0:T(8,128)S(1)}, f32[64,153]{1,0:T(8,128)S(1)}, u32[]{:S(2)}, u32[]{:S(2)}) collective-permute-start(f32[64,153]{1,0:T(8,128)S(1)} %copy-done.12), channel_id=1, source_target_pairs={{0,32},{16,48},{32,0},{48,16},{1,33},{17,49},{33,1},{49,17},{2,34}... | collective-permute-start | bytes 117512 | tf_op jit(solution)/shard_map/ppermute | solution.py:313
  82.9 6.0 %collective-permute-start.3 = (f32[64,153]{1,0:T(8,128)S(1)}, f32[64,153]{1,0:T(8,128)S(1)}, u32[]{:S(2)}, u32[]{:S(2)}) collective-permute-start(f32[64,153]{1,0:T(8,128)S(1)} %copy-done.11), channel_id=1, source_target_pairs={{0,48},{16,0},{32,16},{48,32},{1,49},{17,1},{33,17},{49,33},{2,50}... | collective-permute-start | bytes 117512 | tf_op jit(solution)/shard_map/ppermute | solution.py:313
  88.9 48.7 %copy-start.8 = (f32[64,153]{1,0:T(8,128)}, f32[64,153]{1,0:T(8,128)S(1)}, u32[]{:S(2)}) copy-start(f32[64,153]{1,0:T(8,128)S(1)} %collective-permute-done.1.score1) | copy-start | bytes 117508
  88.9 48.7 %copy-start.9 = (f32[64,153]{1,0:T(8,128)}, f32[64,153]{1,0:T(8,128)S(1)}, u32[]{:S(2)}) copy-start(f32[64,153]{1,0:T(8,128)S(1)} %collective-permute-done.2.score2) | copy-start | bytes 117508
  88.9 48.7 %copy-start.10 = (f32[64,153]{1,0:T(8,128)}, f32[64,153]{1,0:T(8,128)S(1)}, u32[]{:S(2)}) copy-start(f32[64,153]{1,0:T(8,128)S(1)} %collective-permute-done.3.score3) | copy-start | bytes 117508
  100.5 0.8 copy-start.3

commit v4 on v3

--- a/solution.py
+++ b/solution.py
@@ -11,12 +11,13 @@
 BF = jnp.bfloat16
 F32 = jnp.float32
 GELU_C = 0.7978845608028654
+SMALL = pltpu.CompilerParams(vmem_limit_bytes=8 * 2**20)
 FEAT = ("y", "x")
 REP = ("z", "c")
 SUB = 128
 INP = 512
 TGT = 64
-CHUNK = 512
+CHUNK = 4096
 LISTS = 160
 CLS_ROWS = 20
 CLS_PAD = 24
@@ -35,34 +36,38 @@
     return [pl.BlockSpec(memory_space=pltpu.VMEM)] * count
 
 
-def gather_kernel(ids_ref, neigh_ref, count_ref, table_ref, out_ref, turned, rows):
+def gather_kernel(ids_ref, neigh_ref, count_ref, table_ref, out_ref, turned, even, odd):
     cols, papers = table_ref.shape
+    fan = neigh_ref.shape[0]
+    share = -(-INP // (fan + 1))
 
     def turn(step, carry):
         start = pl.multiple_of(step * CHUNK, CHUNK)
-        block = table_ref[:, pl.ds(start, CHUNK)].astype(F32)
-        turned[pl.ds(start, CHUNK), :cols] = block.T
+        turned[pl.ds(start, CHUNK), :cols] = table_ref[:, pl.ds(start, CHUNK)].T.astype(F32)
         return carry
 
-    lax.fori_loop(0, papers // CHUNK, turn, 0, unroll=2)
+    lax.fori_loop(0, papers // CHUNK, turn, 0)
 
     position = lax.broadcasted_iota(jnp.int32, (INP // 2, SUB), 0).astype(F32).astype(BF)
     one = jnp.ones((INP // 2, SUB), BF)
     zero = jnp.zeros((INP // 2, SUB), BF)
 
-    def sub_batch(g, carry):
-        base = g * INP
-        for j in range(INP):
-            rows[pl.ds(j, 1), :] = turned[pl.ds(ids_ref[0, base + j], 1), :]
+    def fetch(g, rows, first, last):
+        for j in range(first, last):
+            rows[pl.ds(j, 1), :] = turned[pl.ds(ids_ref[0, g * INP + j], 1), :]
+
+    def sub_batch(g, rows, later, later_rows):
         nodes = pl.ds(pl.multiple_of(g * SUB, SUB), SUB)
         count = count_ref[:, nodes]
         halves = [zero, zero]
-        for k in range(neigh_ref.shape[1]):
-            near = jnp.where(k < count, neigh_ref[0, pl.ds(k, 1), nodes], -1)
+        for k in range(fan):
+            fetch(later, later_rows, k * share, (k + 1) * share)
+            near = jnp.where(k < count, neigh_ref[k, :, nodes], -1)
             for h in range(2):
                 here = (near - h * (INP // 2)).astype(F32).astype(BF)
                 halves[h] = halves[h] + jnp.where(position == here, one, zero)
-        picked = rows[...].T[:cols].astype(BF)
+        fetch(later, later_rows, fan * share, INP)
+        picked = rows[...].astype(BF).T[:cols]
         summed = mm(picked[:, : INP // 2], halves[0]) + mm(picked[:, INP // 2 :], halves[1])
         agg = (summed / count.astype(F32)).astype(BF)
         own = picked[:, :SUB]
@@ -70,9 +75,15 @@
         for x in range(4):
             out_ref[(g // 4) * 4 + x, :cols, lanes] = own
             out_ref[(g // 4) * 4 + x, cols:, lanes] = agg
+
+    fetch(0, even, 0, INP)
+
+    def pair(step, carry):
+        sub_batch(2 * step, even, 2 * step + 1, odd)
+        sub_batch(2 * step + 1, odd, jnp.minimum(2 * step + 2, 15), even)
         return carry
 
-    lax.fori_loop(0, 16, sub_batch, 0)
+    lax.fori_loop(0, 8, pair, 0)
 
 
 def gather(node_ids, neigh_one, count_one, feature_table):
@@ -82,28 +93,29 @@
         out_shape=jax.ShapeDtypeStruct((16, 2 * cols, 4 * SUB), BF),
         in_specs=[pl.BlockSpec(memory_space=pltpu.SMEM)] + vmem(3),
         out_specs=pl.BlockSpec(memory_space=pltpu.VMEM),
-        scratch_shapes=[pltpu.VMEM((papers, 128), F32), pltpu.VMEM((INP, 128), F32)],
-        compiler_params=pltpu.CompilerParams(vmem_limit_bytes=48 * 2**20),
+        scratch_shapes=[pltpu.VMEM((papers, 128), F32), pltpu.VMEM((INP, 128), F32), pltpu.VMEM((INP, 128), F32)],
+        compiler_params=pltpu.CompilerParams(vmem_limit_bytes=40 * 2**20),
         cost_estimate=pl.CostEstimate(flops=30_000_000_000, bytes_accessed=5_000_000, transcendentals=0),
         name="gather",
     )(node_ids, neigh_one, count_one, feature_table)
 
 
 def pack_kernel(w_self_ref, w_neigh_ref, up_ref, neigh_ref, count_ref, out_ref):
-    lists = jnp.concatenate([neigh_ref[...], count_ref[...]], axis=0).astype(F32).T.astype(BF)
+    lists = jnp.concatenate([neigh_ref[...], count_ref[...], jnp.zeros((6, TGT), jnp.int32)], axis=0).astype(F32)
+    turned = jnp.concatenate([up_ref[...].astype(F32).T, jnp.zeros((7, TGT), F32), lists], axis=0)
+    target = jnp.concatenate([turned[k * 48 : (k + 1) * 48] for k in range(4)], axis=1).astype(BF)
     for x in range(4):
         lanes = slice(x * 256, (x + 1) * 256)
         for y in range(4):
             out_ref[4 * y + x, :48] = w_self_ref[:, lanes]
             out_ref[4 * y + x, 48:96] = w_neigh_ref[:, lanes]
-            out_ref[4 * y + x, 96:, :153] = up_ref[...]
-            out_ref[4 * y + x, 96:, LISTS : LISTS + 26] = lists
+            out_ref[4 * y + x, 96:] = target
 
 
 def pack(w_self, w_neigh, upstream, neigh, count):
     return pl.pallas_call(
         pack_kernel,
-        out_shape=jax.ShapeDtypeStruct((16, 96 + TGT, 256), BF),
+        out_shape=jax.ShapeDtypeStruct((16, 144, 256), BF),
         in_specs=vmem(5),
         out_specs=vmem(1)[0],
         cost_estimate=pl.CostEstimate(flops=1_000_000, bytes_accessed=1_500_000, transcendentals=0),
@@ -116,8 +128,9 @@
     position = lax.broadcasted_iota(jnp.int32, (SUB, TGT), 0).astype(F32)
     classes = []
     for g in range(4):
-        upstream = in_ref[4 * y_ref[0] + g, 96:]
-        turned = upstream.astype(F32).T
+        target = in_ref[4 * y_ref[0] + g, 96:].astype(F32)
+        turned = jnp.concatenate([target[:, k * TGT : (k + 1) * TGT] for k in range(4)], axis=0)
+        upstream = turned[:153].T.astype(BF)
         count = turned[LISTS + 25 : LISTS + 26]
         spread = jnp.zeros((SUB, TGT), F32)
         for k in range(25):
@@ -125,8 +138,8 @@
             spread = spread + jnp.where(position == near, 1.0, 0.0)
         spread = spread.astype(BF)
         spread_ref[g] = spread
-        own = mm(upstream[:, :153], w2s_ref[...])
-        near_grad = mm(upstream[:, :153], w2n_ref[...]).T / count
+        own = mm(upstream, w2s_ref[...])
+        near_grad = mm(upstream, w2n_ref[...]).T / count
         high = near_grad.astype(BF)
         low = (near_grad - high.astype(F32)).astype(BF)
         grad = mm_nt(high, spread) + mm_nt(low, spread)
@@ -141,7 +154,7 @@
     upt_ref[...] = jnp.concatenate(blocks, axis=0).astype(BF)
 
 
-def prepare(row, received, w2s_x, w2n_x):
+def prepare(y, received, w2s_x, w2n_x):
     return pl.pallas_call(
         prepare_kernel,
         out_shape=(
@@ -154,8 +167,9 @@
         in_specs=[pl.BlockSpec(memory_space=pltpu.SMEM)] + vmem(3),
         out_specs=tuple(vmem(5)),
         cost_estimate=pl.CostEstimate(flops=6_000_000_000, bytes_accessed=2_000_000, transcendentals=0),
+        compiler_params=SMALL,
         name="prepare",
-    )(row, received, w2s_x, w2n_x)
+    )(y, received, w2s_x, w2n_x)
 
 
 def layers_kernel(place_ref, st_ref, wt_ref, gh_ref, spread_ref, count_ref, upt_ref, w2_ref, keep_ref, send_ref, *scores_refs):
@@ -216,8 +230,26 @@
         in_specs=[pl.BlockSpec(memory_space=pltpu.SMEM)] + vmem(7),
         out_specs=tuple(vmem(6)),
         cost_estimate=pl.CostEstimate(flops=6_000_000_000, bytes_accessed=4_000_000, transcendentals=200_000),
+        compiler_params=SMALL,
         name="layers",
     )(position, st, wt, gh, spread, count_y, upt, w2_x)
+
+
+def add_pair_kernel(keep_ref, came_ref, out_ref):
+    for z in range(8):
+        out_ref[z] = (keep_ref[z] + came_ref[z].astype(F32)).astype(BF)
+
+
+def add_pair(keep, came):
+    return pl.pallas_call(
+        add_pair_kernel,
+        out_shape=jax.ShapeDtypeStruct(came.shape, BF),
+        in_specs=vmem(2),
+        out_specs=vmem(1)[0],
+        cost_estimate=pl.CostEstimate(flops=1_000_000, bytes_accessed=2_000_000, transcendentals=0),
+        compiler_params=SMALL,
+        name="add_pair",
+    )(keep, came)
 
 
 def sum_z_kernel(z_ref, in_ref, out_ref, total):
@@ -237,6 +269,7 @@
         out_specs=vmem(1)[0],
         scratch_shapes=[pltpu.VMEM((PIECE, 256), F32)],
         cost_estimate=pl.CostEstimate(flops=10_000_000, bytes_accessed=1_500_000, transcendentals=0),
+        compiler_params=SMALL,
         name="sum_z",
     )(z, parts)
 
@@ -254,6 +287,7 @@
         in_specs=vmem(1),
         out_specs=vmem(1)[0],
         cost_estimate=pl.CostEstimate(flops=1_000_000, bytes_accessed=600_000, transcendentals=0),
+        compiler_params=SMALL,
         name="sum_y",
     )(parts)
 
@@ -278,8 +312,14 @@
         in_specs=[pl.BlockSpec(memory_space=pltpu.SMEM)] + vmem(5),
         out_specs=tuple(vmem(5)),
         cost_estimate=pl.CostEstimate(flops=1_000_000, bytes_accessed=2_500_000, transcendentals=0),
+        compiler_params=SMALL,
         name="place",
     )(x, parts, *scores)
+
+
+def shifted(parts, axis):
+    moves = [[(source, (source + step) % 4) for source in range(4)] for step in range(4)]
+    return [parts[0]] + [lax.ppermute(parts[step], axis, moves[step]) for step in (1, 2, 3)]
 
 
 def on_device(
@@ -295,29 +335,27 @@
     w_two_neigh,
     logit_grad,
 ):
-    column = lax.axis_index("x") * 256
+    x, y, z, c = [lax.axis_index(axis).reshape(1) for axis in ("x", "y", "z", "c")]
     sent = pack(w_one_self, w_one_neigh, logit_grad[0], neigh_two[0], count_two)
     received = lax.all_to_all(sent, FEAT, 0, 0, tiled=True)
-
-    st = lax.all_to_all(gather(node_ids, neigh_one, count_one, feature_table), FEAT, 0, 0, tiled=True)
-
-    w2s_x = lax.dynamic_slice_in_dim(w_two_self.T, column, 256, 1)
-    w2n_x = lax.dynamic_slice_in_dim(w_two_neigh.T, column, 256, 1)
-    row = lax.axis_index("y").reshape(1)
-    wt, gh, spread, upt, count_y = prepare(row, received, w2s_x, w2n_x)
-    position = jnp.stack([lax.axis_index("x"), lax.axis_index("c")])
+    gathered = gather(node_ids, neigh_one.transpose(1, 0, 2), count_one, feature_table)
+    st = lax.all_to_all(gathered, FEAT, 0, 0, tiled=True)
+
+    w2s_x = lax.dynamic_slice_in_dim(w_two_self.T, x[0] * 256, 256, 1)
+    w2n_x = lax.dynamic_slice_in_dim(w_two_neigh.T, x[0] * 256, 256, 1)
+    wt, gh, spread, upt, count_y = prepare(y, received, w2s_x, w2n_x)
+    position = jnp.concatenate([x, c])
     keep, send, *scores = layers(
         position, st.reshape(1536, 4 * SUB), wt, gh, spread, count_y, upt, jnp.concatenate([w2s_x, w2n_x], axis=1)
     )
-    for step in (1, 2, 3):
-        scores[step] = lax.ppermute(scores[step], "x", [(i, (i + step) % 4) for i in range(4)])
-
-    pair = (keep + lax.ppermute(send, "c", [(0, 1), (1, 0)]).astype(F32)).astype(BF)
+    scores = shifted(scores, "x")
+
+    pair = add_pair(keep, lax.ppermute(send, "c", [(0, 1), (1, 0)]))
     pair, scores = lax.optimization_barrier((lax.all_to_all(pair, "z", 0, 0, tiled=True), scores))
-    over_z = sum_z(lax.axis_index("z").reshape(1), pair)
+    over_z = sum_z(z, pair)
     final = sum_y(lax.all_to_all(over_z, FEAT, 0, 0, tiled=True))
     final = lax.all_gather(final, REP, axis=0)
-    logits, grad_self, grad_neigh, head_self, head_neigh = place(position[:1], final, scores)
+    logits, grad_self, grad_neigh, head_self, head_neigh = place(x, final, scores)
     return logits[None], grad_self, grad_neigh, head_self.T, head_neigh.T
 
 

time: 141 us -> 127 us (0.901)
  Pallas kernels: 37.4 us -> 24.8 us
  other arithmetic: 3.49 us -> 0.09 us
  local copies, waits for them, and re-layouts: 4.32 us -> 7.72 us
  blocking collectives: 32.8 us -> 29.7 us
  waiting for transfers between devices: 32.1 us -> 33.9 us
    pallas_call x1, Pallas kernels: 20.3 us -> 16.2 us  [gather(): pl.pallas_call(gather_kernel, out_shape=jax.ShapeDtypeStruct((16, 2 * col...]
    unnamed x30 -> x17, local copies, waits for them, and re-layouts: 3.38 us -> 6.78 us
    pallas_call x1, Pallas kernels: 5.29 us -> 2.75 us  [layers(): pl.pallas_call(layers_kernel, out_shape=(jax.ShapeDtypeStruct((8, PIECE,...]
    convert_element_type x1 -> x0, other arithmetic: 2.18 us -> none  [on_device(): (keep + lax.ppermute(send, 'c', [(0, 1), (1, 0)]).astype(F32)).astype(BF)]
    pallas_call x1, Pallas kernels: 3.48 us -> 1.4 us  [prepare(): pl.pallas_call(prepare_kernel, out_shape=(jax.ShapeDtypeStruct((256, 1536...]
    all_to_all x1, blocking collectives: 12.5 us -> 10.7 us  [on_device(): final = sum_y(lax.all_to_all(over_z, FEAT, 0, 0, tiled=True))]
    all_to_all x1, waiting for transfers between devices: 15.3 us -> 17.1 us  [on_device(): st = lax.all_to_all(gathered, FEAT, 0, 0, tiled=True)]
    pallas_call x1, Pallas kernels: 1.84 us -> 0.1 us  [sum_z(): pl.pallas_call(sum_z_kernel, out_shape=jax.ShapeDtypeStruct((16, 8 + CLS_...]
  transfers between devices with their start and end apart: 7 -> 7, of which waited for: 4 -> 4; matrix products, arithmetic and copies ran while one was open for 2% -> 1% of each run, Pallas kernels for 17% -> 14%
where the time goes in v4:
time: 127 us; the launch traced here: 126 us
  waiting for transfers between devices  33.9 us (27%)
  blocking collectives  29.7 us (23%)
  starting transfers between devices  29 us (23%)
  Pallas kernels  24.8 us (20%)
  local copies, waits for them, and re-layouts  7.72 us (6%)
    all_gather x1, blocking collectives, on_device(): final = lax.all_gather(final, REP, axis=0)  19 us
    all_to_all x1, waiting for transfers between devices, on_device(): st = lax.all_to_all(gathered, FEAT, 0, 0, tiled=True)  17.1 us
    pallas_call x1, Pallas kernels, gather(): pl.pallas_call(gather_kernel, out_shape=jax.ShapeDtypeStruct((16, 2 * col...  16.2 us
    all_to_all x1, waiting for transfers between devices, on_device(): lax.all_to_all(pair, 'z', 0, 0, tiled=True)  11.7 us
    all_to_all x1, blocking collectives, on_device(): final = sum_y(lax.all_to_all(over_z, FEAT, 0, 0, tiled=True))  10.7 us
    all_to_all x1, starting transfers between devices, on_device(): lax.all_to_all(pair, 'z', 0, 0, tiled=True)  8.18 us
    all_to_all x1, starting transfers between devices, on_device(): received = lax.all_to_all(sent, FEAT, 0, 0, tiled=True)  7.58 us
    unnamed x17, local copies, waits for them, and re-layouts  6.78 us
  transfers between devices with their start and end apart: 7, of which 4 were waited for; matrix products, arithmetic and copies ran while one was open for 1% of the time, Pallas kernels for 14%

profile of v4, /device:TPU:1, one launch (start us, length us, event | category | flops | bytes accessed | tf_op | source)
XLA Modules:
  0.0 125.9 jit_solution(296309532449669012)
XLA Ops:
  0.6 1.3 %copy.18 = s32[1,25,64]{2,1,0:T(8,128)} copy(s32[1,25,64]{2,0,1:T(1,128)} %param.15) | data formatting | bytes 12800
  2.0 2.2 %pack.1 = bf16[16,144,256]{2,1,0:T(8,128)(2,1)} custom-call(bf16[48,1024]{1,0:T(8,128)(2,1)} %w_self_ref.1, bf16[48,1024]{1,0:T(8,128)(2,1)} %w_neigh_ref.1, bf16[64,153]{1,0:T(8,128)(2,1)} %bitcast.22, s32[25,64]{1,0:T(8,128)} %bitcast.21, s32[1,64]{1,0:T(1,128)} %count_ref.3), custom_call_target="tpu_custom_call" | custom-call | flops 1000000 | bytes 1500000 | tf_op jit(solution)/shard_map/pack/pallas_call | solution.py:116
  4.2 7.6 %all-to-all-start.1 = ((bf16[16,144,256]{2,1,0:T(8,128)(2,1)}), bf16[16,144,256]{2,1,0:T(8,128)(2,1)S(1)}, u32[]{:S(2)}, u32[]{:S(2)}) async-start(bf16[16,144,256]{2,1,0:T(8,128)(2,1)} %pack.1), calls=%async_computation.1 | async-start | bytes 2359296 | tf_op jit(solution)/shard_map/all_to_all | solution.py:340
  11.8 0.0 copy-start
  11.8 1.9 %copy-done = bf16[48,32768]{1,0:T(8,128)(2,1)S(1)} copy-done((bf16[48,32768]{1,0:T(8,128)(2,1)S(1)}, bf16[48,32768]{1,0:T(8,128)(2,1)}, u32[]{:S(2)}) %copy-start) | copy-done | bytes 3145752
  13.7 16.2 %gather.1 = bf16[16,96,512]{2,1,0:T(8,128)(2,1)} custom-call(s32[1,8192]{1,0:T(1,128)S(1)} %copy-done.2, s32[15,1,2048]{2,1,0:T(1,128)S(1)} %bitcast.20, s32[1,2048]{1,0:T(1,128)S(1)} %copy-done.3, bf16[48,32768]{1,0:T(8,128)(2,1)S(1)} %copy-done), custom_call_target="tpu_custom_call" | custom-call | flops 30000001024 | bytes 5000000 | tf_op jit(solution)/shard_map/gather/pallas_call | solution.py:91
  29.9 0.0 all-to-all-done.1.in_ref
  29.9 6.7 %all-to-all-start = ((bf16[16,96,512]{2,1,0:T(8,128)(2,1)}), bf16[16,96,512]{2,1,0:T(8,128)(2,1)S(1)}, u32[]{:S(2)}, u32[]{:S(2)}) async-start(bf16[16,96,512]{2,1,0:T(8,128)(2,1)} %gather.1), calls=%async_computation | async-start | bytes 3145728 | tf_op jit(solution)/shard_map/all_to_all | solution.py:342
  36.5 0.1 pad_add_fusion.place_ref
  36.6 0.9 dynamic-slice_bitcast_fusion
  37.6 1.4 %prepare.1 = (bf16[256,1536]{1,0:T(8,128)(2,1)S(1)}, f32[256,512]{1,0:T(8,128)S(1)}, bf16[4,128,64]{2,1,0:T(8,128)(2,1)S(1)}, bf16[192,256]{1,0:T(8,128)(2,1)S(1)}, f32[4,64]{1,0:T(4,128)S(1)}) custom-call(s32[1]{0:T(128)} %bitcast.5.y_ref, bf16[16,144,256]{2,1,0:T(8,128)(2,1)S(1)} %all-to-all-done.1.in_ref, bf16[153,256]{1,0:T(8,128)(2,1)S(1)} %get-tuple-element.48.w2s_ref, ...), custom_call_target="tpu_custom_call" | custom-call | flops 6000000000 | bytes 2000000 | tf_op jit(solution)/shard_map/prepare/pallas_call | solution.py:158
  39.0 0.9 copy-done.4
  39.8 0.7 copy-done.6
  40.5 17.1 %all-to-all-done = bf16[16,96,512]{2,1,0:T(8,128)(2,1)S(1)} async-done(((bf16[16,96,512]{2,1,0:T(8,128)(2,1)}), bf16[16,96,512]{2,1,0:T(8,128)(2,1)S(1)}, u32[]{:S(2)}, u32[]{:S(2)}) %all-to-all-start) | async-done | bytes 1572896 | tf_op jit(solution)/shard_map/all_to_all | solution.py:342
  57.6 1.1 copy-done.5
  58.7 0.9 copy-done.7
  59.6 2.8 %layers.1 = (f32[8,128,256]{2,1,0:T(8,128)S(1)}, bf16[8,128,256]{2,1,0:T(8,128)(2,1)S(1)}, f32[64,153]{1,0:T(8,128)S(1)}, f32[64,153]{1,0:T(8,128)S(1)}, f32[64,153]{1,0:T(8,128)S(1)}, /*index=5*/f32[64,153]{1,0:T(8,128)S(1)}) custom-call(s32[2]{0:T(128)S(1)} %pad_add_fusion.place_ref, bf16[1536,512]{1,0:T(8,128)(2,1)S(1)} %bitcast.18, ...), custom_call_target="tpu_custom_call" | custom-call | flops 6000000000 | bytes 4000000 | tf_op jit(solution)/shard_map/layers/pallas_call | solution.py:223
  62.4 3.9 %collective-permute-start = (bf16[8,128,256]{2,1,0:T(8,128)(2,1)S(1)}, bf16[8,128,256]{2,1,0:T(8,128)(2,1)S(1)}, u32[]{:S(2)}, u32[]{:S(2)}) collective-permute-start(bf16[8,128,256]{2,1,0:T(8,128)(2,1)S(1)} %get-tuple-element.32), channel_id=1, source_target_pairs={{0,1},{1,0},{2,3},{3,2},{4,5},{5,4},{6,7},{7,6},{8,9},{9,8},{10,11... | collective-permute-start | bytes 1572872 | tf_op jit(solution)/shard_map/ppermute | solution.py:353
  66.3 1.5 %collective-permute-done.came_ref = bf16[8,128,256]{2,1,0:T(8,128)(2,1)S(1)} collective-permute-done((bf16[8,128,256]{2,1,0:T(8,128)(2,1)S(1)}, bf16[8,128,256]{2,1,0:T(8,128)(2,1)S(1)}, u32[]{:S(2)}, u32[]{:S(2)}) %collective-permute-start) | collective-permute-done | bytes 524320 | tf_op jit(solution)/shard_map/ppermute | solution.py:353
  67.8 0.9 add_pair.1
  68.7 8.2 %all-to-all-start.2 = ((bf16[8,128,256]{2,1,0:T(8,128)(2,1)}), bf16[8,128,256]{2,1,0:T(8,128)(2,1)S(1)}, u32[]{:S(2)}, u32[]{:S(2)}) async-start(bf16[8,128,256]{2,1,0:T(8,128)(2,1)} %add_pair.1), calls=%async_computation.2 | async-start | bytes 1048576 | tf_op jit(solution)/shard_map/all_to_all | solution.py:354
  76.9 0.0 collective-permute-start.1
  76.9 0.2 collective-permute-start.2
  77.1 2.4 %collective-permute-start.3 = (f32[64,153]{1,0:T(8,128)S(1)}, f32[64,153]{1,0:T(8,128)S(1)}, u32[]{:S(2)}, u32[]{:S(2)}) collective-permute-start(f32[64,153]{1,0:T(8,128)S(1)} %get-tuple-element.36), channel_id=1, source_target_pairs={{0,48},{16,0},{32,16},{48,32},{1,49},{17,1},{33,17},{49,33},{2,50}... | collective-permute-start | bytes 117512 | tf_op jit(solution)/shard_map/ppermute | solution.py:322
  79.6 3.5 %collective-permute-done.1.score1 = f32[64,153]{1,0:T(8,128)S(1)} collective-permute-done((f32[64,153]{1,0:T(8,128)S(1)}, f32[64,153]{1,0:T(8,128)S(1)}, u32[]{:S(2)}, u32[]{:S(2)}) %collective-permute-start.1) | collective-permute-done | bytes 39200 | tf_op jit(solution)/shard_map/ppermute | solution.py:322
  83.1 0.0 collective-permute-done.2.score2
  83.1 0.0 collective-permute-done.3.score3
  83.1 11.7 %all-to-all-done.2.in_ref = bf16[8,128,256]{2,1,0:T(8,128)(2,1)S(1)} async-done(((bf16[8,128,256]{2,1,0:T(8,128)(2,1)}), bf16[8,128,256]{2,1,0:T(8,128)(2,1)S(1)}, u32[]{:S(2)}, u32[]{:S(2)}) %all-to-all-start.2) | async-done | bytes 524320 | tf_op jit(solution)/shard_map/all_to_all | solution.py:354
  94.8 0.1 sum_z.1
  95.0 10.7 %all_to_all.20.in_ref = bf16[16,32,256]{2,1,0:T(8,128)(2,1)S(1)} all-to-all(bf16[16,32,256]{2,1,0:T(8,128)(2,1)S(1)} %sum_z.1), channel_id=1, replica_groups=mesh['y'=4,'x'=4,'z'=8,'c'=2] {'y','x'}, dimensions={0} | all-to-all | bytes 524288 | tf_op jit(solution)/shard_map/all_to_all | solution.py:356
  105.7 19.0 %all-gather.1.in_ref = bf16[16,28,1024]{2,1,0:T(8,128)(2,1)S(1)} all-gather(bf16[1,28,1024]{2,1,0:T(8,128)(2,1)S(1)} %bitcast.19), channel_id=2, replica_groups=mesh['y'=4,'x'=4,'z'=8,'c'=2] {'z','c'}, dimensions={0}, use_global_device_ids=true | all-gather | bytes 974848 | tf_op jit(solution)/shard_map/all_gather | solution.py:357
  124.7 1.3 %place.1 = (bf16[64,153]{1,0:T(8,128)(2,1)}, f32[48,1024]{1,0:T(8,128)}, f32[48,1024]{1,0:T(8,128)}, f32[153,1024]{1,0:T(8,128)}, f32[153,1024]{1,0:T(8,128)}) custom-call(s32[1]{0:T(128)} %bitcast.x_ref, bf16[16,28,1024]{2,1,0:T(8,128)(2,1)S(1)} %all-gather.1.in_ref, f32[64,153]{1,0:T(8,128)S(1)} %get-tuple-element.38.score0, ...), custom_call_target="tpu_custom_call" | custom-call | flops 1000000 | bytes 2500000 | tf_op jit(solution)/shard_map/place/pallas_call | solution.py:309
  (12 shorter events, 0.1 us)
Async XLA Ops:
  1.9 9.8 %copy-start.1 = (s32[1,15,2048]{2,0,1:T(1,128)S(1)}, s32[1,15,2048]{2,0,1:T(1,128)}, u32[]{:S(2)}) copy-start(s32[1,15,2048]{2,0,1:T(1,128)} %param.13) | copy-start | bytes 368644
  1.9 9.8 %copy-start.2 = (s32[1,8192]{1,0:T(1,128)S(1)}, s32[1,8192]{1,0:T(1,128)}, u32[]{:S(2)}) copy-start(s32[1,8192]{1,0:T(1,128)} %ids_ref.1) | copy-start | bytes 98308
  1.9 9.8 %copy-start.3 = (s32[1,2048]{1,0:T(1,128)S(1)}, s32[1,2048]{1,0:T(1,128)}, u32[]{:S(2)}) copy-start(s32[1,2048]{1,0:T(1,128)} %count_ref.2) | copy-start | bytes 24580
  4.2 25.7 %all-to-all-start.1 = ((bf16[16,144,256]{2,1,0:T(8,128)(2,1)}), bf16[16,144,256]{2,1,0:T(8,128)(2,1)S(1)}, u32[]{:S(2)}, u32[]{:S(2)}) async-start(bf16[16,144,256]{2,1,0:T(8,128)(2,1)} %pack.1), calls=%async_computation.1 | async-start | bytes 2359296 | tf_op jit(solution)/shard_map/all_to_all | solution.py:340
  11.8 1.9 %copy-start = (bf16[48,32768]{1,0:T(8,128)(2,1)S(1)}, bf16[48,32768]{1,0:T(8,128)(2,1)}, u32[]{:S(2)}) copy-start(bf16[48,32768]{1,0:T(8,128)(2,1)} %table_ref.1) | copy-start | bytes 9437188
  29.9 27.7 %all-to-all-start = ((bf16[16,96,512]{2,1,0:T(8,128)(2,1)}), bf16[16,96,512]{2,1,0:T(8,128)(2,1)S(1)}, u32[]{:S(2)}, u32[]{:S(2)}) async-start(bf16[16,96,512]{2,1,0:T(8,128)(2,1)} %gather.1), calls=%async_computation | async-start | bytes 3145728 | tf_op jit(solution)/shard_map/all_to_all | solution.py:342
  39.0 0.9 copy-start.4
  39.8 0.7 copy-start.6
  57.6 1.1 copy-start.5
  58.7 0.9 copy-start.7
  62.4 5.5 %collective-permute-start = (bf16[8,128,256]{2,1,0:T(8,128)(2,1)S(1)}, bf16[8,128,256]{2,1,0:T(8,128)(2,1)S(1)}, u32[]{:S(2)}, u32[]{:S(2)}) collective-permute-start(bf16[8,128,256]{2,1,0:T(8,128)(2,1)S(1)} %get-tuple-element.32), channel_id=1, source_target_pairs={{0,1},{1,0},{2,3},{3,2},{4,5},{5,4},{6,7},{7,6},{8,9},{9,8},{10,11... | collective-permute-start | bytes 1572872 | tf_op jit(solution)/shard_map/ppermute | solution.py:353
  68.7 26.1 %all-to-all-start.2 = ((bf16[8,128,256]{2,1,0:T(8,128)(2,1)}), bf16[8,128,256]{2,1,0:T(8,128)(2,1)S(1)}, u32[]{:S(2)}, u32[]{:S(2)}) async-start(bf16[8,128,256]{2,1,0:T(8,128)(2,1)} %add_pair.1), calls=%async_computation.2 | async-start | bytes 1048576 | tf_op jit(solution)/shard_map/all_to_all | solution.py:354
  76.9 6.2 %collective-permute-start.1 = (f32[64,153]{1,0:T(8,128)S(1)}, f32[64,153]{1,0:T(8,128)S(1)}, u32[]{:S(2)}, u32[]{:S(2)}) collective-permute-start(f32[64,153]{1,0:T(8,128)S(1)} %get-tuple-element.34), channel_id=1, source_target_pairs={{0,16},{16,32},{32,48},{48,0},{1,17},{17,33},{33,49},{49,1},{2,18}... | collective-permute-start | bytes 117512 | tf_op jit(solution)/shard_map/ppermute | solution.py:322
  76.9 6.2 %collective-permute-start.2 = (f32[64,153]{1,0:T(8,128)S(1)}, f32[64,153]{1,0:T(8,128)S(1)}, u32[]{:S(2)}, u32[]{:S(2)}) collective-permute-start(f32[64,153]{1,0:T(8,128)S(1)} %get-tuple-element.35), channel_id=1, source_target_pairs={{0,32},{16,48},{32,0},{48,16},{1,33},{17,49},{33,1},{49,17},{2,34}... | collective-permute-start | bytes 117512 | tf_op jit(solution)/shard_map/ppermute | solution.py:322
  77.1 6.0 %collective-permute-start.3 = (f32[64,153]{1,0:T(8,128)S(1)}, f32[64,153]{1,0:T(8,128)S(1)}, u32[]{:S(2)}, u32[]{:S(2)}) collective-permute-start(f32[64,153]{1,0:T(8,128)S(1)} %get-tuple-element.36), channel_id=1, source_target_pairs={{0,48},{16,0},{32,16},{48,32},{1,49},{17,1},{33,17},{49,33},{2,50}... | collective-permute-start | bytes 117512 | tf_op jit(solution)/shard_map/ppermute | solution.py:322

commit v5 on v4

--- a/solution.py
+++ b/solution.py
@@ -21,7 +21,7 @@
 LISTS = 160
 CLS_ROWS = 20
 CLS_PAD = 24
-PIECE = 128
+PIECE = 120
 
 
 def mm(first, second):
@@ -36,17 +36,21 @@
     return [pl.BlockSpec(memory_space=pltpu.VMEM)] * count
 
 
-def gather_kernel(ids_ref, neigh_ref, count_ref, table_ref, out_ref, turned, even, odd):
+def gather_kernel(ids_ref, neigh_ref, count_ref, table_ref, out_ref, table, turned, even, odd, arrived):
     cols, papers = table_ref.shape
     fan = neigh_ref.shape[0]
     share = -(-INP // (fan + 1))
 
-    def turn(step, carry):
-        start = pl.multiple_of(step * CHUNK, CHUNK)
-        turned[pl.ds(start, CHUNK), :cols] = table_ref[:, pl.ds(start, CHUNK)].T.astype(F32)
-        return carry
-
-    lax.fori_loop(0, papers // CHUNK, turn, 0)
+    blocks = [pl.ds(start, CHUNK) for start in range(0, papers, CHUNK)]
+    copies = [
+        pltpu.make_async_copy(table_ref.at[:, block], table.at[:, block], arrived.at[at])
+        for at, block in enumerate(blocks)
+    ]
+    for copy in copies:
+        copy.start()
+    for block, copy in zip(blocks, copies):
+        copy.wait()
+        turned[block, :cols] = table[:, block].T.astype(F32)
 
     position = lax.broadcasted_iota(jnp.int32, (INP // 2, SUB), 0).astype(F32).astype(BF)
     one = jnp.ones((INP // 2, SUB), BF)
@@ -91,44 +95,77 @@
     return pl.pallas_call(
         gather_kernel,
         out_shape=jax.ShapeDtypeStruct((16, 2 * cols, 4 * SUB), BF),
-        in_specs=[pl.BlockSpec(memory_space=pltpu.SMEM)] + vmem(3),
+        in_specs=[pl.BlockSpec(memory_space=pltpu.SMEM)] + vmem(2) + [pl.BlockSpec(memory_space=pl.ANY)],
         out_specs=pl.BlockSpec(memory_space=pltpu.VMEM),
-        scratch_shapes=[pltpu.VMEM((papers, 128), F32), pltpu.VMEM((INP, 128), F32), pltpu.VMEM((INP, 128), F32)],
-        compiler_params=pltpu.CompilerParams(vmem_limit_bytes=40 * 2**20),
+        scratch_shapes=[
+            pltpu.VMEM((cols, papers), BF),
+            pltpu.VMEM((papers, 128), F32),
+            pltpu.VMEM((INP, 128), F32),
+            pltpu.VMEM((INP, 128), F32),
+            pltpu.SemaphoreType.DMA((papers // CHUNK,)),
+        ],
+        compiler_params=pltpu.CompilerParams(vmem_limit_bytes=56 * 2**20),
         cost_estimate=pl.CostEstimate(flops=30_000_000_000, bytes_accessed=5_000_000, transcendentals=0),
         name="gather",
     )(node_ids, neigh_one, count_one, feature_table)
 
 
-def pack_kernel(w_self_ref, w_neigh_ref, up_ref, neigh_ref, count_ref, out_ref):
-    lists = jnp.concatenate([neigh_ref[...], count_ref[...], jnp.zeros((6, TGT), jnp.int32)], axis=0).astype(F32)
+def pack_kernel(c_ref, w_self_ref, w_neigh_ref, up_ref, neigh_ref, count_ref, out_ref):
+    near = [neigh_ref[k] for k in range(neigh_ref.shape[0])]
+    lists = jnp.concatenate(near + [count_ref[...], jnp.zeros((6, TGT), jnp.int32)], axis=0).astype(F32)
     turned = jnp.concatenate([up_ref[...].astype(F32).T, jnp.zeros((7, TGT), F32), lists], axis=0)
     target = jnp.concatenate([turned[k * 48 : (k + 1) * 48] for k in range(4)], axis=1).astype(BF)
     for x in range(4):
         lanes = slice(x * 256, (x + 1) * 256)
         for y in range(4):
-            out_ref[4 * y + x, :48] = w_self_ref[:, lanes]
-            out_ref[4 * y + x, 48:96] = w_neigh_ref[:, lanes]
-            out_ref[4 * y + x, 96:] = target
-
-
-def pack(w_self, w_neigh, upstream, neigh, count):
+            out_ref[4 * y + x, 48:] = target
+            for side, w_ref in enumerate((w_self_ref, w_neigh_ref)):
+
+                @pl.when(c_ref[0] == side)
+                def _():
+                    out_ref[4 * y + x, :48] = w_ref[:, lanes]
+
+
+def pack(c, w_self, w_neigh, upstream, neigh, count):
     return pl.pallas_call(
         pack_kernel,
-        out_shape=jax.ShapeDtypeStruct((16, 144, 256), BF),
-        in_specs=vmem(5),
+        out_shape=jax.ShapeDtypeStruct((16, 96, 256), BF),
+        in_specs=[pl.BlockSpec(memory_space=pltpu.SMEM)] + vmem(5),
         out_specs=vmem(1)[0],
         cost_estimate=pl.CostEstimate(flops=1_000_000, bytes_accessed=1_500_000, transcendentals=0),
         name="pack",
-    )(w_self, w_neigh, upstream, neigh, count)
-
-
-def prepare_kernel(y_ref, in_ref, w2s_ref, w2n_ref, wt_ref, gh_ref, spread_ref, upt_ref, count_ref):
-    wt_ref[...] = jnp.concatenate([in_ref[f, :96] for f in range(16)], axis=0).T
+    )(c, w_self, w_neigh, upstream, neigh, count)
+
+
+def turn_weights_kernel(place_ref, in_ref, came_ref, wt_ref, targets_ref):
+    for side in range(2):
+
+        @pl.when(place_ref[1] == side)
+        def _():
+            sides = (in_ref, came_ref) if side == 0 else (came_ref, in_ref)
+            wt_ref[...] = jnp.concatenate([ref[f, :48] for f in range(16) for ref in sides], axis=0).T
+
+    for g in range(4):
+        targets_ref[g] = in_ref[4 * place_ref[0] + g, 48:]
+
+
+def turn_weights(position, received, came):
+    return pl.pallas_call(
+        turn_weights_kernel,
+        out_shape=(jax.ShapeDtypeStruct((256, 1536), BF), jax.ShapeDtypeStruct((4, 48, 256), BF)),
+        in_specs=[pl.BlockSpec(memory_space=pltpu.SMEM)] + vmem(2),
+        out_specs=tuple(vmem(2)),
+        cost_estimate=pl.CostEstimate(flops=1_000_000, bytes_accessed=2_000_000, transcendentals=0),
+        compiler_params=SMALL,
+        name="turn_weights",
+    )(position, received, came)
+
+
+def layers_kernel(place_ref, st_ref, wt_ref, targets_ref, w2s_ref, w2n_ref, keep_ref, send_ref, *scores_refs):
     position = lax.broadcasted_iota(jnp.int32, (SUB, TGT), 0).astype(F32)
-    classes = []
+    classes, spreads, hidden_grads, counts = [], [], [], []
     for g in range(4):
-        target = in_ref[4 * y_ref[0] + g, 96:].astype(F32)
+        target = targets_ref[g].astype(F32)
         turned = jnp.concatenate([target[:, k * TGT : (k + 1) * TGT] for k in range(4)], axis=0)
         upstream = turned[:153].T.astype(BF)
         count = turned[LISTS + 25 : LISTS + 26]
@@ -137,57 +174,37 @@
             near = jnp.where(k < count, turned[LISTS + k : LISTS + k + 1], -1.0)
             spread = spread + jnp.where(position == near, 1.0, 0.0)
         spread = spread.astype(BF)
-        spread_ref[g] = spread
+        spreads.append(spread)
         own = mm(upstream, w2s_ref[...])
         near_grad = mm(upstream, w2n_ref[...]).T / count
         high = near_grad.astype(BF)
         low = (near_grad - high.astype(F32)).astype(BF)
         grad = mm_nt(high, spread) + mm_nt(low, spread)
-        gh_ref[:, g * SUB : (g + 1) * SUB] = grad + jnp.concatenate([own.T, jnp.zeros(own.T.shape, F32)], axis=1)
+        hidden_grads.append(grad + jnp.concatenate([own.T, jnp.zeros(own.T.shape, F32)], axis=1))
         classes.append(turned[:153])
-        count_ref[pl.ds(g, 1), :] = count
+        counts.append(count)
     classes = jnp.concatenate(classes, axis=1)
     blocks = []
     for z in range(8):
         block = classes[z * CLS_ROWS : min((z + 1) * CLS_ROWS, 153)]
         blocks += [block, jnp.zeros((CLS_PAD - block.shape[0], 4 * TGT), F32)]
-    upt_ref[...] = jnp.concatenate(blocks, axis=0).astype(BF)
-
-
-def prepare(y, received, w2s_x, w2n_x):
-    return pl.pallas_call(
-        prepare_kernel,
-        out_shape=(
-            jax.ShapeDtypeStruct((256, 1536), BF),
-            jax.ShapeDtypeStruct((256, 4 * SUB), F32),
-            jax.ShapeDtypeStruct((4, SUB, TGT), BF),
-            jax.ShapeDtypeStruct((8 * CLS_PAD, 4 * TGT), BF),
-            jax.ShapeDtypeStruct((4, TGT), F32),
-        ),
-        in_specs=[pl.BlockSpec(memory_space=pltpu.SMEM)] + vmem(3),
-        out_specs=tuple(vmem(5)),
-        cost_estimate=pl.CostEstimate(flops=6_000_000_000, bytes_accessed=2_000_000, transcendentals=0),
-        compiler_params=SMALL,
-        name="prepare",
-    )(y, received, w2s_x, w2n_x)
-
-
-def layers_kernel(place_ref, st_ref, wt_ref, gh_ref, spread_ref, count_ref, upt_ref, w2_ref, keep_ref, send_ref, *scores_refs):
+    classes = jnp.concatenate(blocks, axis=0).astype(BF)
+
     pre = mm(wt_ref[...], st_ref[...])
     square = pre * pre
     bend = jnp.tanh(GELU_C * pre * (1.0 + 0.044715 * square))
     half = 0.5 * (1.0 + bend)
     hidden = (pre * half).astype(BF)
     slope = half + 0.5 * pre * (1.0 - bend * bend) * (GELU_C * (1.0 + 3.0 * 0.044715 * square))
-    grad_pre = (gh_ref[...] * slope).astype(BF)
+    grad_pre = (jnp.concatenate(hidden_grads, axis=1) * slope).astype(BF)
     grad = mm_nt(st_ref[...], grad_pre)
     own, near = [], []
     for g in range(4):
         nodes = hidden[:, g * SUB : (g + 1) * SUB]
         own.append(nodes[:, :TGT])
-        near.append((mm(nodes, spread_ref[g]) / count_ref[pl.ds(g, 1), :]).astype(BF))
+        near.append((mm(nodes, spreads[g]) / counts[g]).astype(BF))
     both = jnp.concatenate([jnp.concatenate(own, axis=1), jnp.concatenate(near, axis=1)], axis=0)
-    scores = mm(w2_ref[...], both).T
+    scores = mm(jnp.concatenate([w2s_ref[...], w2n_ref[...]], axis=1), both).T
     for g in range(4):
         for step, scores_ref in enumerate(scores_refs):
 
@@ -195,7 +212,7 @@
             def _():
                 scores_ref[...] = scores[g * TGT : (g + 1) * TGT]
 
-    head = mm_nt(upt_ref[...], both)
+    head = mm_nt(classes, both)
 
     def pieces(side):
         for z in range(8):
@@ -206,7 +223,6 @@
                     start = f * 96 + side * 48 + tile * 8
                     rows.append(grad[start : start + 8])
             rows.append(head[z * CLS_PAD : (z + 1) * CLS_PAD, side * 256 : (side + 1) * 256])
-            rows.append(jnp.zeros((PIECE - 96 - CLS_PAD, 256), F32))
             yield z, jnp.concatenate(rows, axis=0)
 
     for side in range(2):
@@ -219,7 +235,7 @@
                 send_ref[z] = piece.astype(BF)
 
 
-def layers(position, st, wt, gh, spread, count_y, upt, w2_x):
+def layers(position, st, wt, targets, w2s_x, w2n_x):
     return pl.pallas_call(
         layers_kernel,
         out_shape=(
@@ -227,12 +243,12 @@
             jax.ShapeDtypeStruct((8, PIECE, 256), BF),
             *[jax.ShapeDtypeStruct((TGT, 153), F32)] * 4,
         ),
-        in_specs=[pl.BlockSpec(memory_space=pltpu.SMEM)] + vmem(7),
+        in_specs=[pl.BlockSpec(memory_space=pltpu.SMEM)] + vmem(5),
         out_specs=tuple(vmem(6)),
         cost_estimate=pl.CostEstimate(flops=6_000_000_000, bytes_accessed=4_000_000, transcendentals=200_000),
         compiler_params=SMALL,
         name="layers",
-    )(position, st, wt, gh, spread, count_y, upt, w2_x)
+    )(position, st, wt, targets, w2s_x, w2n_x)
 
 
 def add_pair_kernel(keep_ref, came_ref, out_ref):
@@ -336,17 +352,18 @@
     logit_grad,
 ):
     x, y, z, c = [lax.axis_index(axis).reshape(1) for axis in ("x", "y", "z", "c")]
-    sent = pack(w_one_self, w_one_neigh, logit_grad[0], neigh_two[0], count_two)
+    sent = pack(c, w_one_self, w_one_neigh, logit_grad[0], neigh_two.transpose(1, 0, 2), count_two)
     received = lax.all_to_all(sent, FEAT, 0, 0, tiled=True)
     gathered = gather(node_ids, neigh_one.transpose(1, 0, 2), count_one, feature_table)
     st = lax.all_to_all(gathered, FEAT, 0, 0, tiled=True)
 
     w2s_x = lax.dynamic_slice_in_dim(w_two_self.T, x[0] * 256, 256, 1)
     w2n_x = lax.dynamic_slice_in_dim(w_two_neigh.T, x[0] * 256, 256, 1)
-    wt, gh, spread, upt, count_y = prepare(y, received, w2s_x, w2n_x)
+    came = lax.ppermute(received, "c", [(0, 1), (1, 0)])
+    wt, targets = turn_weights(jnp.concatenate([y, c]), received, came)
     position = jnp.concatenate([x, c])
     keep, send, *scores = layers(
-        position, st.reshape(1536, 4 * SUB), wt, gh, spread, count_y, upt, jnp.concatenate([w2s_x, w2n_x], axis=1)
+        position, st.reshape(1536, 4 * SUB), wt, targets, w2s_x, w2n_x
     )
     scores = shifted(scores, "x")
 

time: 127 us -> 124 us (0.976)
  local copies, waits for them, and re-layouts: 7.72 us -> 2.96 us
  starting transfers between devices: 29 us -> 30.6 us
  Pallas kernels: 24.8 us -> 26.4 us
    unnamed x17 -> x4, local copies, waits for them, and re-layouts: 6.78 us -> 2.02 us
    ppermute x0 -> x1, starting transfers between devices: none -> 1.59 us  [on_device(): came = lax.ppermute(received, 'c', [(0, 1), (1, 0)])]
  transfers between devices with their start and end apart: 7 -> 8, of which waited for: 4 -> 5; matrix products, arithmetic and copies ran while one was open for 1% -> 1% of each run, Pallas kernels for 14% -> 15%
where the time goes in v5:
time: 124 us; the launch traced here: 123 us
  waiting for transfers between devices  32.7 us (26%)
  starting transfers between devices  30.6 us (25%)
  blocking collectives  29.7 us (24%)
  Pallas kernels  26.4 us (21%)
  local copies, waits for them, and re-layouts  2.96 us (2%)
    all_gather x1, blocking collectives, on_device(): final = lax.all_gather(final, REP, axis=0)  19 us
    pallas_call x1, Pallas kernels, gather(): pl.pallas_call(gather_kernel, out_shape=jax.ShapeDtypeStruct((16, 2 * col...  17.4 us
    all_to_all x1, waiting for transfers between devices, on_device(): st = lax.all_to_all(gathered, FEAT, 0, 0, tiled=True)  15.8 us
    all_to_all x1, waiting for transfers between devices, on_device(): lax.all_to_all(pair, 'z', 0, 0, tiled=True)  11 us
    all_to_all x1, blocking collectives, on_device(): final = sum_y(lax.all_to_all(over_z, FEAT, 0, 0, tiled=True))  10.7 us
    all_to_all x1, starting transfers between devices, on_device(): lax.all_to_all(pair, 'z', 0, 0, tiled=True)  8.18 us
    all_to_all x1, starting transfers between devices, on_device(): received = lax.all_to_all(sent, FEAT, 0, 0, tiled=True)  7.58 us
    all_to_all x1, starting transfers between devices, on_device(): st = lax.all_to_all(gathered, FEAT, 0, 0, tiled=True)  6.67 us
  transfers between devices with their start and end apart: 8, of which 5 were waited for; matrix products, arithmetic and copies ran while one was open for 1% of the time, Pallas kernels for 15%

profile of v5, /device:TPU:1, one launch (start us, length us, event | category | flops | bytes accessed | tf_op | source)
XLA Modules:
  0.0 123.2 jit_solution(5451320042907602911)
XLA Ops:
  0.6 2.3 %pack.1 = bf16[16,96,256]{2,1,0:T(8,128)(2,1)} custom-call(s32[1]{0:T(128)} %bitcast.2.c_ref, bf16[48,1024]{1,0:T(8,128)(2,1)} %w_self_ref.1, bf16[48,1024]{1,0:T(8,128)(2,1)} %w_neigh_ref.1, bf16[64,153]{1,0:T(8,128)(2,1)} %bitcast.18, s32[25,1,64]{2,1,0:T(1,128)} %bitcast.19, s32[1,64]{1,0:T(1,128)} %count_ref.3), custom_call_target="tpu_custom_call" | custom-call | flops 1000000 | bytes 1500000 | tf_op jit(solution)/shard_map/pack/pallas_call | solution.py:130
  2.9 7.6 %all-to-all-start.1 = ((bf16[16,96,256]{2,1,0:T(8,128)(2,1)}), bf16[16,96,256]{2,1,0:T(8,128)(2,1)S(1)}, u32[]{:S(2)}, u32[]{:S(2)}) async-start(bf16[16,96,256]{2,1,0:T(8,128)(2,1)} %pack.1), calls=%async_computation.1 | async-start | bytes 1572864 | tf_op jit(solution)/shard_map/all_to_all | solution.py:356
  10.5 17.4 %gather.1 = bf16[16,96,512]{2,1,0:T(8,128)(2,1)} custom-call(s32[1,8192]{1,0:T(1,128)} %ids_ref.1, s32[15,1,2048]{2,1,0:T(1,128)} %bitcast.22, s32[1,2048]{1,0:T(1,128)} %count_ref.2, bf16[48,32768]{1,0:T(8,128)(2,1)} %table_ref.1), custom_call_target="tpu_custom_call" | custom-call | flops 30000001024 | bytes 5000000 | tf_op jit(solution)/shard_map/gather/pallas_call | solution.py:95
  27.9 0.0 all-to-all-done.1.in_ref
  27.9 6.7 %all-to-all-start = ((bf16[16,96,512]{2,1,0:T(8,128)(2,1)}), bf16[16,96,512]{2,1,0:T(8,128)(2,1)S(1)}, u32[]{:S(2)}, u32[]{:S(2)}) async-start(bf16[16,96,512]{2,1,0:T(8,128)(2,1)} %gather.1), calls=%async_computation | async-start | bytes 3145728 | tf_op jit(solution)/shard_map/all_to_all | solution.py:358
  34.6 1.6 %collective-permute-start = (bf16[16,96,256]{2,1,0:T(8,128)(2,1)S(1)}, bf16[16,96,256]{2,1,0:T(8,128)(2,1)S(1)}, u32[]{:S(2)}, u32[]{:S(2)}) collective-permute-start(bf16[16,96,256]{2,1,0:T(8,128)(2,1)S(1)} %all-to-all-done.1.in_ref), channel_id=1, source_target_pairs={{0,1},{1,0},{2,3},{3,2},{4,5},{5,4},{6,7},{7,6},{8,9},{9,8},{10,11... | collective-permute-start | bytes 2359304 | tf_op jit(solution)/shard_map/ppermute | solution.py:362
  36.2 0.1 pad_add_fusion.1.place_ref
  36.2 0.1 pad_add_fusion.place_ref
  36.3 0.9 dynamic-slice_bitcast_fusion
  37.3 0.8 collective-permute-done.came_ref
  38.1 0.8 turn_weights.1
  38.9 0.0 copy-start
  38.9 0.9 copy-done
  39.8 15.8 %all-to-all-done = bf16[16,96,512]{2,1,0:T(8,128)(2,1)S(1)} async-done(((bf16[16,96,512]{2,1,0:T(8,128)(2,1)}), bf16[16,96,512]{2,1,0:T(8,128)(2,1)S(1)}, u32[]{:S(2)}, u32[]{:S(2)}) %all-to-all-start) | async-done | bytes 1572896 | tf_op jit(solution)/shard_map/all_to_all | solution.py:358
  55.6 0.0 copy-start.1
  55.6 1.1 copy-done.1
  56.8 3.7 %layers.1 = (f32[8,120,256]{2,1,0:T(8,128)S(1)}, bf16[8,120,256]{2,1,0:T(8,128)(2,1)S(1)}, f32[64,153]{1,0:T(8,128)S(1)}, f32[64,153]{1,0:T(8,128)S(1)}, f32[64,153]{1,0:T(8,128)S(1)}, /*index=5*/f32[64,153]{1,0:T(8,128)S(1)}) custom-call(s32[2]{0:T(128)S(1)} %pad_add_fusion.place_ref, bf16[1536,512]{1,0:T(8,128)(2,1)S(1)} %bitcast.16, ...), custom_call_target="tpu_custom_call" | custom-call | flops 6000000000 | bytes 4000000 | tf_op jit(solution)/shard_map/layers/pallas_call | solution.py:239
  60.4 3.9 %collective-permute-start.1 = (bf16[8,120,256]{2,1,0:T(8,128)(2,1)S(1)}, bf16[8,120,256]{2,1,0:T(8,128)(2,1)S(1)}, u32[]{:S(2)}, u32[]{:S(2)}) collective-permute-start(bf16[8,120,256]{2,1,0:T(8,128)(2,1)S(1)} %get-tuple-element.26), channel_id=1, source_target_pairs={{0,1},{1,0},{2,3},{3,2},{4,5},{5,4},{6,7},{7,6},{8,9},{9,8},{10,11... | collective-permute-start | bytes 1474568 | tf_op jit(solution)/shard_map/ppermute | solution.py:370
  64.4 1.5 %collective-permute-done.1.came_ref = bf16[8,120,256]{2,1,0:T(8,128)(2,1)S(1)} collective-permute-done((bf16[8,120,256]{2,1,0:T(8,128)(2,1)S(1)}, bf16[8,120,256]{2,1,0:T(8,128)(2,1)S(1)}, u32[]{:S(2)}, u32[]{:S(2)}) %collective-permute-start.1) | collective-permute-done | bytes 491552 | tf_op jit(solution)/shard_map/ppermute | solution.py:370
  65.8 0.9 add_pair.1
  66.7 8.2 %all-to-all-start.2 = ((bf16[8,120,256]{2,1,0:T(8,128)(2,1)}), bf16[8,120,256]{2,1,0:T(8,128)(2,1)S(1)}, u32[]{:S(2)}, u32[]{:S(2)}) async-start(bf16[8,120,256]{2,1,0:T(8,128)(2,1)} %add_pair.1), calls=%async_computation.2 | async-start | bytes 983040 | tf_op jit(solution)/shard_map/all_to_all | solution.py:371
  74.9 0.0 collective-permute-start.2
  74.9 0.2 collective-permute-start.3
  75.1 2.4 %collective-permute-start.4 = (f32[64,153]{1,0:T(8,128)S(1)}, f32[64,153]{1,0:T(8,128)S(1)}, u32[]{:S(2)}, u32[]{:S(2)}) collective-permute-start(f32[64,153]{1,0:T(8,128)S(1)} %get-tuple-element.30), channel_id=1, source_target_pairs={{0,48},{16,0},{32,16},{48,32},{1,49},{17,1},{33,17},{49,33},{2,50}... | collective-permute-start | bytes 117512 | tf_op jit(solution)/shard_map/ppermute | solution.py:338
  77.6 3.5 %collective-permute-done.2.score1 = f32[64,153]{1,0:T(8,128)S(1)} collective-permute-done((f32[64,153]{1,0:T(8,128)S(1)}, f32[64,153]{1,0:T(8,128)S(1)}, u32[]{:S(2)}, u32[]{:S(2)}) %collective-permute-start.2) | collective-permute-done | bytes 39200 | tf_op jit(solution)/shard_map/ppermute | solution.py:338
  81.1 0.0 collective-permute-done.3.score2
  81.1 0.0 collective-permute-done.4.score3
  81.1 11.0 %all-to-all-done.2.in_ref = bf16[8,120,256]{2,1,0:T(8,128)(2,1)S(1)} async-done(((bf16[8,120,256]{2,1,0:T(8,128)(2,1)}), bf16[8,120,256]{2,1,0:T(8,128)(2,1)S(1)}, u32[]{:S(2)}, u32[]{:S(2)}) %all-to-all-start.2) | async-done | bytes 491552 | tf_op jit(solution)/shard_map/all_to_all | solution.py:371
  92.1 0.1 sum_z.1
  92.2 10.7 %all_to_all.20.in_ref = bf16[16,32,256]{2,1,0:T(8,128)(2,1)S(1)} all-to-all(bf16[16,32,256]{2,1,0:T(8,128)(2,1)S(1)} %sum_z.1), channel_id=1, replica_groups=mesh['y'=4,'x'=4,'z'=8,'c'=2] {'y','x'}, dimensions={0} | all-to-all | bytes 524288 | tf_op jit(solution)/shard_map/all_to_all | solution.py:373
  102.9 19.0 %all-gather.1.in_ref = bf16[16,28,1024]{2,1,0:T(8,128)(2,1)S(1)} all-gather(bf16[1,28,1024]{2,1,0:T(8,128)(2,1)S(1)} %bitcast.17), channel_id=2, replica_groups=mesh['y'=4,'x'=4,'z'=8,'c'=2] {'z','c'}, dimensions={0}, use_global_device_ids=true | all-gather | bytes 974848 | tf_op jit(solution)/shard_map/all_gather | solution.py:374
  122.0 1.3 %place.1 = (bf16[64,153]{1,0:T(8,128)(2,1)}, f32[48,1024]{1,0:T(8,128)}, f32[48,1024]{1,0:T(8,128)}, f32[153,1024]{1,0:T(8,128)}, f32[153,1024]{1,0:T(8,128)}) custom-call(s32[1]{0:T(128)} %bitcast.x_ref, bf16[16,28,1024]{2,1,0:T(8,128)(2,1)S(1)} %all-gather.1.in_ref, f32[64,153]{1,0:T(8,128)S(1)} %get-tuple-element.32.score0, ...), custom_call_target="tpu_custom_call" | custom-call | flops 1000000 | bytes 2500000 | tf_op jit(solution)/shard_map/place/pallas_call | solution.py:325
  (1 shorter events, 0.0 us)
Async XLA Ops:
  2.9 25.0 %all-to-all-start.1 = ((bf16[16,96,256]{2,1,0:T(8,128)(2,1)}), bf16[16,96,256]{2,1,0:T(8,128)(2,1)S(1)}, u32[]{:S(2)}, u32[]{:S(2)}) async-start(bf16[16,96,256]{2,1,0:T(8,128)(2,1)} %pack.1), calls=%async_computation.1 | async-start | bytes 1572864 | tf_op jit(solution)/shard_map/all_to_all | solution.py:356
  27.9 27.7 %all-to-all-start = ((bf16[16,96,512]{2,1,0:T(8,128)(2,1)}), bf16[16,96,512]{2,1,0:T(8,128)(2,1)S(1)}, u32[]{:S(2)}, u32[]{:S(2)}) async-start(bf16[16,96,512]{2,1,0:T(8,128)(2,1)} %gather.1), calls=%async_computation | async-start | bytes 3145728 | tf_op jit(solution)/shard_map/all_to_all | solution.py:358
  34.6 3.5 %collective-permute-start = (bf16[16,96,256]{2,1,0:T(8,128)(2,1)S(1)}, bf16[16,96,256]{2,1,0:T(8,128)(2,1)S(1)}, u32[]{:S(2)}, u32[]{:S(2)}) collective-permute-start(bf16[16,96,256]{2,1,0:T(8,128)(2,1)S(1)} %all-to-all-done.1.in_ref), channel_id=1, source_target_pairs={{0,1},{1,0},{2,3},{3,2},{4,5},{5,4},{6,7},{7,6},{8,9},{9,8},{10,11... | collective-permute-start | bytes 2359304 | tf_op jit(solution)/shard_map/ppermute | solution.py:362
  38.9 0.9 copy-start
  55.6 1.1 copy-start.1
  60.4 5.4 %collective-permute-start.1 = (bf16[8,120,256]{2,1,0:T(8,128)(2,1)S(1)}, bf16[8,120,256]{2,1,0:T(8,128)(2,1)S(1)}, u32[]{:S(2)}, u32[]{:S(2)}) collective-permute-start(bf16[8,120,256]{2,1,0:T(8,128)(2,1)S(1)} %get-tuple-element.26), channel_id=1, source_target_pairs={{0,1},{1,0},{2,3},{3,2},{4,5},{5,4},{6,7},{7,6},{8,9},{9,8},{10,11... | collective-permute-start | bytes 1474568 | tf_op jit(solution)/shard_map/ppermute | solution.py:370
  66.7 25.4 %all-to-all-start.2 = ((bf16[8,120,256]{2,1,0:T(8,128)(2,1)}), bf16[8,120,256]{2,1,0:T(8,128)(2,1)S(1)}, u32[]{:S(2)}, u32[]{:S(2)}) async-start(bf16[8,120,256]{2,1,0:T(8,128)(2,1)} %add_pair.1), calls=%async_computation.2 | async-start | bytes 983040 | tf_op jit(solution)/shard_map/all_to_all | solution.py:371
  74.9 6.2 %collective-permute-start.2 = (f32[64,153]{1,0:T(8,128)S(1)}, f32[64,153]{1,0:T(8,128)S(1)}, u32[]{:S(2)}, u32[]{:S(2)}) collective-permute-start(f32[64,153]{1,0:T(8,128)S(1)} %get-tuple-element.28), channel_id=1, source_target_pairs={{0,16},{16,32},{32,48},{48,0},{1,17},{17,33},{33,49},{49,1},{2,18}... | collective-permute-start | bytes 117512 | tf_op jit(solution)/shard_map/ppermute | solution.py:338
  74.9 6.2 %collective-permute-start.3 = (f32[64,153]{1,0:T(8,128)S(1)}, f32[64,153]{1,0:T(8,128)S(1)}, u32[]{:S(2)}, u32[]{:S(2)}) collective-permute-start(f32[64,153]{1,0:T(8,128)S(1)} %get-tuple-element.29), channel_id=1, source_target_pairs={{0,32},{16,48},{32,0},{48,16},{1,33},{17,49},{33,1},{49,17},{2,34}... | collective-permute-start | bytes 117512 | tf_op jit(solution)/shard_map/ppermute | solution.py:338
  75.1 6.0 %collective-permute-start.4 = (f32[64,153]{1,0:T(8,128)S(1)}, f32[64,153]{1,0:T(8,128)S(1)}, u32[]{:S(2)}, u32[]{:S(2)}) collective-permute-start(f32[64,153]{1,0:T(8,128)S(1)} %get-tuple-element.30), channel_id=1, source_target_pairs={{0,48},{16,0},{32,16},{48,32},{1,49},{17,1},{33,17},{49,33},{2,50}... | collective-permute-start | bytes 117512 | tf_op jit(solution)/shard_map/ppermute | solution.py:338

commit v6 on v5

--- a/solution.py
+++ b/solution.py
@@ -36,21 +36,29 @@
     return [pl.BlockSpec(memory_space=pltpu.VMEM)] * count
 
 
-def gather_kernel(ids_ref, neigh_ref, count_ref, table_ref, out_ref, table, turned, even, odd, arrived):
-    cols, papers = table_ref.shape
-    fan = neigh_ref.shape[0]
+def gather_kernel(
+    ids_hbm, neigh_hbm, count_hbm, table_hbm, out_hbm, ids_ref, neigh_ref, count_ref, table, turned, even, odd, held, arrived, sent
+):
+    cols, papers = table_hbm.shape
+    fan = neigh_hbm.shape[0]
     share = -(-INP // (fan + 1))
 
     blocks = [pl.ds(start, CHUNK) for start in range(0, papers, CHUNK)]
     copies = [
-        pltpu.make_async_copy(table_ref.at[:, block], table.at[:, block], arrived.at[at])
+        pltpu.make_async_copy(table_hbm.at[:, block], table.at[:, block], arrived.at[at])
         for at, block in enumerate(blocks)
     ]
-    for copy in copies:
+    lists = [
+        pltpu.make_async_copy(source, target, arrived.at[len(blocks) + at])
+        for at, (source, target) in enumerate(((ids_hbm, ids_ref), (neigh_hbm, neigh_ref), (count_hbm, count_ref)))
+    ]
+    for copy in copies + lists:
         copy.start()
     for block, copy in zip(blocks, copies):
         copy.wait()
         turned[block, :cols] = table[:, block].T.astype(F32)
+    for copy in lists:
+        copy.wait()
 
     position = lax.broadcasted_iota(jnp.int32, (INP // 2, SUB), 0).astype(F32).astype(BF)
     one = jnp.ones((INP // 2, SUB), BF)
@@ -76,18 +84,29 @@
         agg = (summed / count.astype(F32)).astype(BF)
         own = picked[:, :SUB]
         lanes = pl.ds(pl.multiple_of((g % 4) * SUB, SUB), SUB)
-        for x in range(4):
-            out_ref[(g // 4) * 4 + x, :cols, lanes] = own
-            out_ref[(g // 4) * 4 + x, cols:, lanes] = agg
+        held[g // 4, :cols, lanes] = own
+        held[g // 4, cols:, lanes] = agg
+
+    def send(y, x):
+        return pltpu.make_async_copy(held.at[y], out_hbm.at[4 * y + x], sent.at[4 * y + x])
 
     fetch(0, even, 0, INP)
 
     def pair(step, carry):
         sub_batch(2 * step, even, 2 * step + 1, odd)
         sub_batch(2 * step + 1, odd, jnp.minimum(2 * step + 2, 15), even)
+
+        @pl.when(step % 2 == 1)
+        def _():
+            for x in range(4):
+                send(step // 2, x).start()
+
         return carry
 
     lax.fori_loop(0, 8, pair, 0)
+    for y in range(4):
+        for x in range(4):
+            send(y, x).wait()
 
 
 def gather(node_ids, neigh_one, count_one, feature_table):
@@ -95,14 +114,19 @@
     return pl.pallas_call(
         gather_kernel,
         out_shape=jax.ShapeDtypeStruct((16, 2 * cols, 4 * SUB), BF),
-        in_specs=[pl.BlockSpec(memory_space=pltpu.SMEM)] + vmem(2) + [pl.BlockSpec(memory_space=pl.ANY)],
-        out_specs=pl.BlockSpec(memory_space=pltpu.VMEM),
+        in_specs=[pl.BlockSpec(memory_space=pl.ANY)] * 4,
+        out_specs=pl.BlockSpec(memory_space=pl.ANY),
         scratch_shapes=[
+            pltpu.SMEM(node_ids.shape, jnp.int32),
+            pltpu.VMEM(neigh_one.shape, jnp.int32),
+            pltpu.VMEM(count_one.shape, jnp.int32),
             pltpu.VMEM((cols, papers), BF),
             pltpu.VMEM((papers, 128), F32),
             pltpu.VMEM((INP, 128), F32),
             pltpu.VMEM((INP, 128), F32),
-            pltpu.SemaphoreType.DMA((papers // CHUNK,)),
+            pltpu.VMEM((4, 2 * cols, 4 * SUB), BF),
+            pltpu.SemaphoreType.DMA((papers // CHUNK + 3,)),
+            pltpu.SemaphoreType.DMA((16,)),
         ],
         compiler_params=pltpu.CompilerParams(vmem_limit_bytes=56 * 2**20),
         cost_estimate=pl.CostEstimate(flops=30_000_000_000, bytes_accessed=5_000_000, transcendentals=0),

time: 124 us -> 122 us (0.984)
  Pallas kernels: 26.4 us -> 24.8 us
    pallas_call x1, Pallas kernels: 17.4 us -> 15.9 us  [gather(): pl.pallas_call(gather_kernel, out_shape=jax.ShapeDtypeStruct((16, 2 * col...]
  transfers between devices with their start and end apart: 8 -> 8, of which waited for: 5 -> 5; matrix products, arithmetic and copies ran while one was open for 1% -> 1% of each run, Pallas kernels for 15% -> 14%
where the time goes in v6:
time: 122 us
  waiting for transfers between devices  32.7 us (27%)
  starting transfers between devices  30.6 us (25%)
  blocking collectives  29.7 us (24%)
  Pallas kernels  24.8 us (20%)
  local copies, waits for them, and re-layouts  2.96 us (2%)
    all_gather x1, blocking collectives, on_device(): final = lax.all_gather(final, REP, axis=0)  19 us
    pallas_call x1, Pallas kernels, gather(): pl.pallas_call(gather_kernel, out_shape=jax.ShapeDtypeStruct((16, 2 * col...  15.9 us
    all_to_all x1, waiting for transfers between devices, on_device(): st = lax.all_to_all(gathered, FEAT, 0, 0, tiled=True)  15.8 us
    all_to_all x1, waiting for transfers between devices, on_device(): lax.all_to_all(pair, 'z', 0, 0, tiled=True)  11 us
    all_to_all x1, blocking collectives, on_device(): final = sum_y(lax.all_to_all(over_z, FEAT, 0, 0, tiled=True))  10.7 us
    all_to_all x1, starting transfers between devices, on_device(): lax.all_to_all(pair, 'z', 0, 0, tiled=True)  8.18 us
    all_to_all x1, starting transfers between devices, on_device(): received = lax.all_to_all(sent, FEAT, 0, 0, tiled=True)  7.58 us
    all_to_all x1, starting transfers between devices, on_device(): st = lax.all_to_all(gathered, FEAT, 0, 0, tiled=True)  6.67 us
  transfers between devices with their start and end apart: 8, of which 5 were waited for; matrix products, arithmetic and copies ran while one was open for 1% of the time, Pallas kernels for 14%

profile of v6, /device:TPU:1, one launch (start us, length us, event | category | flops | bytes accessed | tf_op | source)
XLA Modules:
  0.0 121.7 jit_solution(12753327751849166793)
XLA Ops:
  0.6 2.3 %pack.1 = bf16[16,96,256]{2,1,0:T(8,128)(2,1)} custom-call(s32[1]{0:T(128)} %bitcast.2.c_ref, bf16[48,1024]{1,0:T(8,128)(2,1)} %w_self_ref.1, bf16[48,1024]{1,0:T(8,128)(2,1)} %w_neigh_ref.1, bf16[64,153]{1,0:T(8,128)(2,1)} %bitcast.18, s32[25,1,64]{2,1,0:T(1,128)} %bitcast.19, s32[1,64]{1,0:T(1,128)} %count_ref.1), custom_call_target="tpu_custom_call" | custom-call | flops 1000000 | bytes 1500000 | tf_op jit(solution)/shard_map/pack/pallas_call | solution.py:154
  2.9 7.6 %all-to-all-start.1 = ((bf16[16,96,256]{2,1,0:T(8,128)(2,1)}), bf16[16,96,256]{2,1,0:T(8,128)(2,1)S(1)}, u32[]{:S(2)}, u32[]{:S(2)}) async-start(bf16[16,96,256]{2,1,0:T(8,128)(2,1)} %pack.1), calls=%async_computation.1 | async-start | bytes 1572864 | tf_op jit(solution)/shard_map/all_to_all | solution.py:380
  10.5 15.9 %gather.1 = bf16[16,96,512]{2,1,0:T(8,128)(2,1)} custom-call(s32[1,8192]{1,0:T(1,128)} %ids_hbm.1, s32[15,1,2048]{2,1,0:T(1,128)} %bitcast.22, s32[1,2048]{1,0:T(1,128)} %count_hbm.1, bf16[48,32768]{1,0:T(8,128)(2,1)} %table_hbm.1), custom_call_target="tpu_custom_call" | custom-call | flops 30000001024 | bytes 5000000 | tf_op jit(solution)/shard_map/gather/pallas_call | solution.py:114
  26.4 0.0 all-to-all-done.1.in_ref
  26.4 6.7 %all-to-all-start = ((bf16[16,96,512]{2,1,0:T(8,128)(2,1)}), bf16[16,96,512]{2,1,0:T(8,128)(2,1)S(1)}, u32[]{:S(2)}, u32[]{:S(2)}) async-start(bf16[16,96,512]{2,1,0:T(8,128)(2,1)} %gather.1), calls=%async_computation | async-start | bytes 3145728 | tf_op jit(solution)/shard_map/all_to_all | solution.py:382
  33.0 1.6 %collective-permute-start = (bf16[16,96,256]{2,1,0:T(8,128)(2,1)S(1)}, bf16[16,96,256]{2,1,0:T(8,128)(2,1)S(1)}, u32[]{:S(2)}, u32[]{:S(2)}) collective-permute-start(bf16[16,96,256]{2,1,0:T(8,128)(2,1)S(1)} %all-to-all-done.1.in_ref), channel_id=1, source_target_pairs={{0,1},{1,0},{2,3},{3,2},{4,5},{5,4},{6,7},{7,6},{8,9},{9,8},{10,11... | collective-permute-start | bytes 2359304 | tf_op jit(solution)/shard_map/ppermute | solution.py:386
  34.6 0.1 pad_add_fusion.1.place_ref
  34.7 0.1 pad_add_fusion.place_ref
  34.8 0.9 dynamic-slice_bitcast_fusion
  35.7 0.8 collective-permute-done.came_ref
  36.6 0.8 turn_weights.1
  37.4 0.0 copy-start
  37.4 0.9 copy-done
  38.3 15.8 %all-to-all-done = bf16[16,96,512]{2,1,0:T(8,128)(2,1)S(1)} async-done(((bf16[16,96,512]{2,1,0:T(8,128)(2,1)}), bf16[16,96,512]{2,1,0:T(8,128)(2,1)S(1)}, u32[]{:S(2)}, u32[]{:S(2)}) %all-to-all-start) | async-done | bytes 1572896 | tf_op jit(solution)/shard_map/all_to_all | solution.py:382
  54.1 0.0 copy-start.1
  54.1 1.1 copy-done.1
  55.2 3.7 %layers.1 = (f32[8,120,256]{2,1,0:T(8,128)S(1)}, bf16[8,120,256]{2,1,0:T(8,128)(2,1)S(1)}, f32[64,153]{1,0:T(8,128)S(1)}, f32[64,153]{1,0:T(8,128)S(1)}, f32[64,153]{1,0:T(8,128)S(1)}, /*index=5*/f32[64,153]{1,0:T(8,128)S(1)}) custom-call(s32[2]{0:T(128)S(1)} %pad_add_fusion.place_ref, bf16[1536,512]{1,0:T(8,128)(2,1)S(1)} %bitcast.16, ...), custom_call_target="tpu_custom_call" | custom-call | flops 6000000000 | bytes 4000000 | tf_op jit(solution)/shard_map/layers/pallas_call | solution.py:263
  58.9 3.9 %collective-permute-start.1 = (bf16[8,120,256]{2,1,0:T(8,128)(2,1)S(1)}, bf16[8,120,256]{2,1,0:T(8,128)(2,1)S(1)}, u32[]{:S(2)}, u32[]{:S(2)}) collective-permute-start(bf16[8,120,256]{2,1,0:T(8,128)(2,1)S(1)} %get-tuple-element.26), channel_id=1, source_target_pairs={{0,1},{1,0},{2,3},{3,2},{4,5},{5,4},{6,7},{7,6},{8,9},{9,8},{10,11... | collective-permute-start | bytes 1474568 | tf_op jit(solution)/shard_map/ppermute | solution.py:394
  62.8 1.5 %collective-permute-done.1.came_ref = bf16[8,120,256]{2,1,0:T(8,128)(2,1)S(1)} collective-permute-done((bf16[8,120,256]{2,1,0:T(8,128)(2,1)S(1)}, bf16[8,120,256]{2,1,0:T(8,128)(2,1)S(1)}, u32[]{:S(2)}, u32[]{:S(2)}) %collective-permute-start.1) | collective-permute-done | bytes 491552 | tf_op jit(solution)/shard_map/ppermute | solution.py:394
  64.3 0.9 add_pair.1
  65.2 8.2 %all-to-all-start.2 = ((bf16[8,120,256]{2,1,0:T(8,128)(2,1)}), bf16[8,120,256]{2,1,0:T(8,128)(2,1)S(1)}, u32[]{:S(2)}, u32[]{:S(2)}) async-start(bf16[8,120,256]{2,1,0:T(8,128)(2,1)} %add_pair.1), calls=%async_computation.2 | async-start | bytes 983040 | tf_op jit(solution)/shard_map/all_to_all | solution.py:395
  73.3 0.0 collective-permute-start.2
  73.4 0.2 collective-permute-start.3
  73.6 2.4 %collective-permute-start.4 = (f32[64,153]{1,0:T(8,128)S(1)}, f32[64,153]{1,0:T(8,128)S(1)}, u32[]{:S(2)}, u32[]{:S(2)}) collective-permute-start(f32[64,153]{1,0:T(8,128)S(1)} %get-tuple-element.30), channel_id=1, source_target_pairs={{0,48},{16,0},{32,16},{48,32},{1,49},{17,1},{33,17},{49,33},{2,50}... | collective-permute-start | bytes 117512 | tf_op jit(solution)/shard_map/ppermute | solution.py:362
  76.0 3.5 %collective-permute-done.2.score1 = f32[64,153]{1,0:T(8,128)S(1)} collective-permute-done((f32[64,153]{1,0:T(8,128)S(1)}, f32[64,153]{1,0:T(8,128)S(1)}, u32[]{:S(2)}, u32[]{:S(2)}) %collective-permute-start.2) | collective-permute-done | bytes 39200 | tf_op jit(solution)/shard_map/ppermute | solution.py:362
  79.6 0.0 collective-permute-done.3.score2
  79.6 0.0 collective-permute-done.4.score3
  79.6 11.0 %all-to-all-done.2.in_ref = bf16[8,120,256]{2,1,0:T(8,128)(2,1)S(1)} async-done(((bf16[8,120,256]{2,1,0:T(8,128)(2,1)}), bf16[8,120,256]{2,1,0:T(8,128)(2,1)S(1)}, u32[]{:S(2)}, u32[]{:S(2)}) %all-to-all-start.2) | async-done | bytes 491552 | tf_op jit(solution)/shard_map/all_to_all | solution.py:395
  90.6 0.1 sum_z.1
  90.7 10.7 %all_to_all.20.in_ref = bf16[16,32,256]{2,1,0:T(8,128)(2,1)S(1)} all-to-all(bf16[16,32,256]{2,1,0:T(8,128)(2,1)S(1)} %sum_z.1), channel_id=1, replica_groups=mesh['y'=4,'x'=4,'z'=8,'c'=2] {'y','x'}, dimensions={0} | all-to-all | bytes 524288 | tf_op jit(solution)/shard_map/all_to_all | solution.py:397
  101.4 19.0 %all-gather.1.in_ref = bf16[16,28,1024]{2,1,0:T(8,128)(2,1)S(1)} all-gather(bf16[1,28,1024]{2,1,0:T(8,128)(2,1)S(1)} %bitcast.17), channel_id=2, replica_groups=mesh['y'=4,'x'=4,'z'=8,'c'=2] {'z','c'}, dimensions={0}, use_global_device_ids=true | all-gather | bytes 974848 | tf_op jit(solution)/shard_map/all_gather | solution.py:398
  120.4 1.3 %place.1 = (bf16[64,153]{1,0:T(8,128)(2,1)}, f32[48,1024]{1,0:T(8,128)}, f32[48,1024]{1,0:T(8,128)}, f32[153,1024]{1,0:T(8,128)}, f32[153,1024]{1,0:T(8,128)}) custom-call(s32[1]{0:T(128)} %bitcast.x_ref, bf16[16,28,1024]{2,1,0:T(8,128)(2,1)S(1)} %all-gather.1.in_ref, f32[64,153]{1,0:T(8,128)S(1)} %get-tuple-element.32.score0, ...), custom_call_target="tpu_custom_call" | custom-call | flops 1000000 | bytes 2500000 | tf_op jit(solution)/shard_map/place/pallas_call | solution.py:349
  (1 shorter events, 0.0 us)
Async XLA Ops:
  2.9 23.5 %all-to-all-start.1 = ((bf16[16,96,256]{2,1,0:T(8,128)(2,1)}), bf16[16,96,256]{2,1,0:T(8,128)(2,1)S(1)}, u32[]{:S(2)}, u32[]{:S(2)}) async-start(bf16[16,96,256]{2,1,0:T(8,128)(2,1)} %pack.1), calls=%async_computation.1 | async-start | bytes 1572864 | tf_op jit(solution)/shard_map/all_to_all | solution.py:380
  26.4 27.7 %all-to-all-start = ((bf16[16,96,512]{2,1,0:T(8,128)(2,1)}), bf16[16,96,512]{2,1,0:T(8,128)(2,1)S(1)}, u32[]{:S(2)}, u32[]{:S(2)}) async-start(bf16[16,96,512]{2,1,0:T(8,128)(2,1)} %gather.1), calls=%async_computation | async-start | bytes 3145728 | tf_op jit(solution)/shard_map/all_to_all | solution.py:382
  33.0 3.5 %collective-permute-start = (bf16[16,96,256]{2,1,0:T(8,128)(2,1)S(1)}, bf16[16,96,256]{2,1,0:T(8,128)(2,1)S(1)}, u32[]{:S(2)}, u32[]{:S(2)}) collective-permute-start(bf16[16,96,256]{2,1,0:T(8,128)(2,1)S(1)} %all-to-all-done.1.in_ref), channel_id=1, source_target_pairs={{0,1},{1,0},{2,3},{3,2},{4,5},{5,4},{6,7},{7,6},{8,9},{9,8},{10,11... | collective-permute-start | bytes 2359304 | tf_op jit(solution)/shard_map/ppermute | solution.py:386
  37.4 0.9 copy-start
  54.1 1.1 copy-start.1
  58.9 5.4 %collective-permute-start.1 = (bf16[8,120,256]{2,1,0:T(8,128)(2,1)S(1)}, bf16[8,120,256]{2,1,0:T(8,128)(2,1)S(1)}, u32[]{:S(2)}, u32[]{:S(2)}) collective-permute-start(bf16[8,120,256]{2,1,0:T(8,128)(2,1)S(1)} %get-tuple-element.26), channel_id=1, source_target_pairs={{0,1},{1,0},{2,3},{3,2},{4,5},{5,4},{6,7},{7,6},{8,9},{9,8},{10,11... | collective-permute-start | bytes 1474568 | tf_op jit(solution)/shard_map/ppermute | solution.py:394
  65.2 25.4 %all-to-all-start.2 = ((bf16[8,120,256]{2,1,0:T(8,128)(2,1)}), bf16[8,120,256]{2,1,0:T(8,128)(2,1)S(1)}, u32[]{:S(2)}, u32[]{:S(2)}) async-start(bf16[8,120,256]{2,1,0:T(8,128)(2,1)} %add_pair.1), calls=%async_computation.2 | async-start | bytes 983040 | tf_op jit(solution)/shard_map/all_to_all | solution.py:395
  73.3 6.2 %collective-permute-start.2 = (f32[64,153]{1,0:T(8,128)S(1)}, f32[64,153]{1,0:T(8,128)S(1)}, u32[]{:S(2)}, u32[]{:S(2)}) collective-permute-start(f32[64,153]{1,0:T(8,128)S(1)} %get-tuple-element.28), channel_id=1, source_target_pairs={{0,16},{16,32},{32,48},{48,0},{1,17},{17,33},{33,49},{49,1},{2,18}... | collective-permute-start | bytes 117512 | tf_op jit(solution)/shard_map/ppermute | solution.py:362
  73.4 6.2 %collective-permute-start.3 = (f32[64,153]{1,0:T(8,128)S(1)}, f32[64,153]{1,0:T(8,128)S(1)}, u32[]{:S(2)}, u32[]{:S(2)}) collective-permute-start(f32[64,153]{1,0:T(8,128)S(1)} %get-tuple-element.29), channel_id=1, source_target_pairs={{0,32},{16,48},{32,0},{48,16},{1,33},{17,49},{33,1},{49,17},{2,34}... | collective-permute-start | bytes 117512 | tf_op jit(solution)/shard_map/ppermute | solution.py:362
  73.6 6.0 %collective-permute-start.4 = (f32[64,153]{1,0:T(8,128)S(1)}, f32[64,153]{1,0:T(8,128)S(1)}, u32[]{:S(2)}, u32[]{:S(2)}) collective-permute-start(f32[64,153]{1,0:T(8,128)S(1)} %get-tuple-element.30), channel_id=1, source_target_pairs={{0,48},{16,0},{32,16},{48,32},{1,49},{17,1},{33,17},{49,33},{2,50}... | collective-permute-start | bytes 117512 | tf_op jit(solution)/shard_map/ppermute | solution.py:362

commit v7 on v6

--- a/solution.py
+++ b/solution.py
@@ -134,28 +134,47 @@
     )(node_ids, neigh_one, count_one, feature_table)
 
 
-def pack_kernel(c_ref, w_self_ref, w_neigh_ref, up_ref, neigh_ref, count_ref, out_ref):
+def pack_kernel(c_ref, w_self_hbm, w_neigh_hbm, up_hbm, neigh_hbm, count_hbm, out_ref, w_ref, up_ref, neigh_ref, count_ref, arrived):
+    copies = [
+        pltpu.make_async_copy(source, target, arrived.at[at])
+        for at, (source, target) in enumerate(((up_hbm, up_ref), (neigh_hbm, neigh_ref), (count_hbm, count_ref)))
+    ]
+    for copy in copies:
+        copy.start()
+    for side, w_hbm in enumerate((w_self_hbm, w_neigh_hbm)):
+
+        @pl.when(c_ref[0] == side)
+        def _():
+            copy = pltpu.make_async_copy(w_hbm, w_ref, arrived.at[3 + side])
+            copy.start()
+            copy.wait()
+
+    for copy in copies:
+        copy.wait()
     near = [neigh_ref[k] for k in range(neigh_ref.shape[0])]
     lists = jnp.concatenate(near + [count_ref[...], jnp.zeros((6, TGT), jnp.int32)], axis=0).astype(F32)
     turned = jnp.concatenate([up_ref[...].astype(F32).T, jnp.zeros((7, TGT), F32), lists], axis=0)
     target = jnp.concatenate([turned[k * 48 : (k + 1) * 48] for k in range(4)], axis=1).astype(BF)
     for x in range(4):
-        lanes = slice(x * 256, (x + 1) * 256)
         for y in range(4):
+            out_ref[4 * y + x, :48] = w_ref[:, x * 256 : (x + 1) * 256]
             out_ref[4 * y + x, 48:] = target
-            for side, w_ref in enumerate((w_self_ref, w_neigh_ref)):
-
-                @pl.when(c_ref[0] == side)
-                def _():
-                    out_ref[4 * y + x, :48] = w_ref[:, lanes]
 
 
 def pack(c, w_self, w_neigh, upstream, neigh, count):
     return pl.pallas_call(
         pack_kernel,
         out_shape=jax.ShapeDtypeStruct((16, 96, 256), BF),
-        in_specs=[pl.BlockSpec(memory_space=pltpu.SMEM)] + vmem(5),
+        in_specs=[pl.BlockSpec(memory_space=pltpu.SMEM)] + [pl.BlockSpec(memory_space=pl.ANY)] * 5,
         out_specs=vmem(1)[0],
+        scratch_shapes=[
+            pltpu.VMEM(w_self.shape, BF),
+            pltpu.VMEM(upstream.shape, BF),
+            pltpu.VMEM(neigh.shape, jnp.int32),
+            pltpu.VMEM(count.shape, jnp.int32),
+            pltpu.SemaphoreType.DMA((5,)),
+        ],
+        compiler_params=pltpu.CompilerParams(vmem_limit_bytes=56 * 2**20),
         cost_estimate=pl.CostEstimate(flops=1_000_000, bytes_accessed=1_500_000, transcendentals=0),
         name="pack",
     )(c, w_self, w_neigh, upstream, neigh, count)
@@ -315,15 +334,15 @@
 
 
 def sum_y_kernel(in_ref, out_ref):
-    for x in range(4):
-        total = sum(in_ref[4 * y + x].astype(F32) for y in range(4))
-        out_ref[:, x * 256 : (x + 1) * 256] = total[: 8 + CLS_ROWS].astype(BF)
+    parts = [sum(in_ref[4 * y + x].astype(F32) for y in range(4))[: 8 + CLS_ROWS] for x in range(4)]
+    halves = [jnp.concatenate(parts[:2], axis=1), jnp.concatenate(parts[2:], axis=1)]
+    out_ref[...] = jnp.concatenate(halves, axis=0).astype(BF)
 
 
 def sum_y(parts):
     return pl.pallas_call(
         sum_y_kernel,
-        out_shape=jax.ShapeDtypeStruct((8 + CLS_ROWS, 1024), BF),
+        out_shape=jax.ShapeDtypeStruct((2 * (8 + CLS_ROWS), 512), BF),
         in_specs=vmem(1),
         out_specs=vmem(1)[0],
         cost_estimate=pl.CostEstimate(flops=1_000_000, bytes_accessed=600_000, transcendentals=0),
@@ -335,12 +354,18 @@
 def place_kernel(x_ref, in_ref, score0, score1, score2, score3, logits_ref, self_ref, neigh_ref, head_self_ref, head_neigh_ref):
     logits_ref[...] = (score0[...] + score1[...] + score2[...] + score3[...]).astype(BF)
     for side, (first_ref, head_ref) in enumerate(((self_ref, head_self_ref), (neigh_ref, head_neigh_ref))):
+        rows = 8 + CLS_ROWS
         for tile in range(6):
             owner = lax.rem(tile + 6 * x_ref[0], 8)
-            first_ref[tile * 8 : (tile + 1) * 8] = in_ref[2 * owner + side].astype(F32)[:8]
+            piece = in_ref[2 * owner + side].astype(F32)
+            for half in range(2):
+                first_ref[tile * 8 : (tile + 1) * 8, half * 512 : (half + 1) * 512] = piece[half * rows : half * rows + 8]
         for z in range(8):
             end = min((z + 1) * CLS_ROWS, 153)
-            head_ref[z * CLS_ROWS : end] = in_ref[2 * z + side].astype(F32)[8 : 8 + end - z * CLS_ROWS]
+            piece = in_ref[2 * z + side].astype(F32)
+            for half in range(2):
+                start = half * rows + 8
+                head_ref[z * CLS_ROWS : end, half * 512 : (half + 1) * 512] = piece[start : start + end - z * CLS_ROWS]
 
 
 def place(x, parts, scores):

time: 122 us -> 122 us (level)
  no operation moved by 1% of the time
where the time goes in v7:
time: 122 us; the launch traced here: 121 us
  waiting for transfers between devices  32.7 us (27%)
  starting transfers between devices  30.6 us (25%)
  blocking collectives  29.2 us (24%)
  Pallas kernels  24.7 us (20%)
  local copies, waits for them, and re-layouts  2.96 us (2%)
    all_gather x1, blocking collectives, on_device(): final = lax.all_gather(final, REP, axis=0)  18.6 us
    pallas_call x1, Pallas kernels, gather(): pl.pallas_call(gather_kernel, out_shape=jax.ShapeDtypeStruct((16, 2 * col...  15.9 us
    all_to_all x1, waiting for transfers between devices, on_device(): st = lax.all_to_all(gathered, FEAT, 0, 0, tiled=True)  15.8 us
    all_to_all x1, waiting for transfers between devices, on_device(): lax.all_to_all(pair, 'z', 0, 0, tiled=True)  11 us
    all_to_all x1, blocking collectives, on_device(): final = sum_y(lax.all_to_all(over_z, FEAT, 0, 0, tiled=True))  10.7 us
    all_to_all x1, starting transfers between devices, on_device(): lax.all_to_all(pair, 'z', 0, 0, tiled=True)  8.18 us
    all_to_all x1, starting transfers between devices, on_device(): received = lax.all_to_all(sent, FEAT, 0, 0, tiled=True)  7.6 us
    all_to_all x1, starting transfers between devices, on_device(): st = lax.all_to_all(gathered, FEAT, 0, 0, tiled=True)  6.67 us
  transfers between devices with their start and end apart: 8, of which 5 were waited for; matrix products, arithmetic and copies ran while one was open for 1% of the time, Pallas kernels for 14%

profile of v7, /device:TPU:1, one launch (start us, length us, event | category | flops | bytes accessed | tf_op | source)
XLA Modules:
  0.0 121.1 jit_solution(5575625890131761372)
XLA Ops:
  0.6 2.1 %pack.1 = bf16[16,96,256]{2,1,0:T(8,128)(2,1)} custom-call(s32[1]{0:T(128)} %bitcast.2.c_ref, bf16[48,1024]{1,0:T(8,128)(2,1)} %w_self_hbm.1, bf16[48,1024]{1,0:T(8,128)(2,1)} %w_neigh_hbm.1, bf16[64,153]{1,0:T(8,128)(2,1)} %bitcast.18, s32[25,1,64]{2,1,0:T(1,128)} %bitcast.19, s32[1,64]{1,0:T(1,128)} %count_hbm.3), custom_call_target="tpu_custom_call" | custom-call | flops 1000000 | bytes 1500000 | tf_op jit(solution)/shard_map/pack/pallas_call | solution.py:165
  2.7 7.6 %all-to-all-start.1 = ((bf16[16,96,256]{2,1,0:T(8,128)(2,1)}), bf16[16,96,256]{2,1,0:T(8,128)(2,1)S(1)}, u32[]{:S(2)}, u32[]{:S(2)}) async-start(bf16[16,96,256]{2,1,0:T(8,128)(2,1)} %pack.1), calls=%async_computation.1 | async-start | bytes 1572864 | tf_op jit(solution)/shard_map/all_to_all | solution.py:405
  10.3 15.9 %gather.1 = bf16[16,96,512]{2,1,0:T(8,128)(2,1)} custom-call(s32[1,8192]{1,0:T(1,128)} %ids_hbm.1, s32[15,1,2048]{2,1,0:T(1,128)} %bitcast.22, s32[1,2048]{1,0:T(1,128)} %count_hbm.2, bf16[48,32768]{1,0:T(8,128)(2,1)} %table_hbm.1), custom_call_target="tpu_custom_call" | custom-call | flops 30000001024 | bytes 5000000 | tf_op jit(solution)/shard_map/gather/pallas_call | solution.py:114
  26.2 0.0 all-to-all-done.1.in_ref
  26.2 6.7 %all-to-all-start = ((bf16[16,96,512]{2,1,0:T(8,128)(2,1)}), bf16[16,96,512]{2,1,0:T(8,128)(2,1)S(1)}, u32[]{:S(2)}, u32[]{:S(2)}) async-start(bf16[16,96,512]{2,1,0:T(8,128)(2,1)} %gather.1), calls=%async_computation | async-start | bytes 3145728 | tf_op jit(solution)/shard_map/all_to_all | solution.py:407
  32.9 1.6 %collective-permute-start = (bf16[16,96,256]{2,1,0:T(8,128)(2,1)S(1)}, bf16[16,96,256]{2,1,0:T(8,128)(2,1)S(1)}, u32[]{:S(2)}, u32[]{:S(2)}) collective-permute-start(bf16[16,96,256]{2,1,0:T(8,128)(2,1)S(1)} %all-to-all-done.1.in_ref), channel_id=1, source_target_pairs={{0,1},{1,0},{2,3},{3,2},{4,5},{5,4},{6,7},{7,6},{8,9},{9,8},{10,11... | collective-permute-start | bytes 2359304 | tf_op jit(solution)/shard_map/ppermute | solution.py:411
  34.5 0.1 pad_add_fusion.1.place_ref
  34.6 0.1 pad_add_fusion.place_ref
  34.6 0.9 dynamic-slice_bitcast_fusion
  35.6 0.8 collective-permute-done.came_ref
  36.4 0.8 turn_weights.1
  37.2 0.0 copy-start
  37.2 0.9 copy-done
  38.1 15.8 %all-to-all-done = bf16[16,96,512]{2,1,0:T(8,128)(2,1)S(1)} async-done(((bf16[16,96,512]{2,1,0:T(8,128)(2,1)}), bf16[16,96,512]{2,1,0:T(8,128)(2,1)S(1)}, u32[]{:S(2)}, u32[]{:S(2)}) %all-to-all-start) | async-done | bytes 1572896 | tf_op jit(solution)/shard_map/all_to_all | solution.py:407
  53.9 0.0 copy-start.1
  53.9 1.1 copy-done.1
  55.1 3.7 %layers.1 = (f32[8,120,256]{2,1,0:T(8,128)S(1)}, bf16[8,120,256]{2,1,0:T(8,128)(2,1)S(1)}, f32[64,153]{1,0:T(8,128)S(1)}, f32[64,153]{1,0:T(8,128)S(1)}, f32[64,153]{1,0:T(8,128)S(1)}, /*index=5*/f32[64,153]{1,0:T(8,128)S(1)}) custom-call(s32[2]{0:T(128)S(1)} %pad_add_fusion.place_ref, bf16[1536,512]{1,0:T(8,128)(2,1)S(1)} %bitcast.17, ...), custom_call_target="tpu_custom_call" | custom-call | flops 6000000000 | bytes 4000000 | tf_op jit(solution)/shard_map/layers/pallas_call | solution.py:282
  58.7 3.9 %collective-permute-start.1 = (bf16[8,120,256]{2,1,0:T(8,128)(2,1)S(1)}, bf16[8,120,256]{2,1,0:T(8,128)(2,1)S(1)}, u32[]{:S(2)}, u32[]{:S(2)}) collective-permute-start(bf16[8,120,256]{2,1,0:T(8,128)(2,1)S(1)} %get-tuple-element.26), channel_id=1, source_target_pairs={{0,1},{1,0},{2,3},{3,2},{4,5},{5,4},{6,7},{7,6},{8,9},{9,8},{10,11... | collective-permute-start | bytes 1474568 | tf_op jit(solution)/shard_map/ppermute | solution.py:419
  62.6 1.5 %collective-permute-done.1.came_ref = bf16[8,120,256]{2,1,0:T(8,128)(2,1)S(1)} collective-permute-done((bf16[8,120,256]{2,1,0:T(8,128)(2,1)S(1)}, bf16[8,120,256]{2,1,0:T(8,128)(2,1)S(1)}, u32[]{:S(2)}, u32[]{:S(2)}) %collective-permute-start.1) | collective-permute-done | bytes 491552 | tf_op jit(solution)/shard_map/ppermute | solution.py:419
  64.1 0.9 add_pair.1
  65.0 8.2 %all-to-all-start.2 = ((bf16[8,120,256]{2,1,0:T(8,128)(2,1)}), bf16[8,120,256]{2,1,0:T(8,128)(2,1)S(1)}, u32[]{:S(2)}, u32[]{:S(2)}) async-start(bf16[8,120,256]{2,1,0:T(8,128)(2,1)} %add_pair.1), calls=%async_computation.2 | async-start | bytes 983040 | tf_op jit(solution)/shard_map/all_to_all | solution.py:420
  73.2 0.0 collective-permute-start.2
  73.2 0.2 collective-permute-start.3
  73.4 2.4 %collective-permute-start.4 = (f32[64,153]{1,0:T(8,128)S(1)}, f32[64,153]{1,0:T(8,128)S(1)}, u32[]{:S(2)}, u32[]{:S(2)}) collective-permute-start(f32[64,153]{1,0:T(8,128)S(1)} %get-tuple-element.30), channel_id=1, source_target_pairs={{0,48},{16,0},{32,16},{48,32},{1,49},{17,1},{33,17},{49,33},{2,50}... | collective-permute-start | bytes 117512 | tf_op jit(solution)/shard_map/ppermute | solution.py:387
  75.9 3.5 %collective-permute-done.2.score1 = f32[64,153]{1,0:T(8,128)S(1)} collective-permute-done((f32[64,153]{1,0:T(8,128)S(1)}, f32[64,153]{1,0:T(8,128)S(1)}, u32[]{:S(2)}, u32[]{:S(2)}) %collective-permute-start.2) | collective-permute-done | bytes 39200 | tf_op jit(solution)/shard_map/ppermute | solution.py:387
  79.4 0.0 collective-permute-done.3.score2
  79.4 0.0 collective-permute-done.4.score3
  79.4 11.0 %all-to-all-done.2.in_ref = bf16[8,120,256]{2,1,0:T(8,128)(2,1)S(1)} async-done(((bf16[8,120,256]{2,1,0:T(8,128)(2,1)}), bf16[8,120,256]{2,1,0:T(8,128)(2,1)S(1)}, u32[]{:S(2)}, u32[]{:S(2)}) %all-to-all-start.2) | async-done | bytes 491552 | tf_op jit(solution)/shard_map/all_to_all | solution.py:420
  90.4 0.1 sum_z.1
  90.5 10.7 %all_to_all.20.in_ref = bf16[16,32,256]{2,1,0:T(8,128)(2,1)S(1)} all-to-all(bf16[16,32,256]{2,1,0:T(8,128)(2,1)S(1)} %sum_z.1), channel_id=1, replica_groups=mesh['y'=4,'x'=4,'z'=8,'c'=2] {'y','x'}, dimensions={0} | all-to-all | bytes 524288 | tf_op jit(solution)/shard_map/all_to_all | solution.py:422
  101.2 18.6 %all-gather = bf16[896,512]{1,0:T(8,128)(2,1)S(1)} all-gather(bf16[56,512]{1,0:T(8,128)(2,1)S(1)} %sum_y.1), channel_id=2, replica_groups=mesh['y'=4,'x'=4,'z'=8,'c'=2] {'z','c'}, dimensions={0}, use_global_device_ids=true | all-gather | bytes 974848 | tf_op jit(solution)/shard_map/all_gather | solution.py:423
  119.8 1.3 %place.1 = (bf16[64,153]{1,0:T(8,128)(2,1)}, f32[48,1024]{1,0:T(8,128)}, f32[48,1024]{1,0:T(8,128)}, f32[153,1024]{1,0:T(8,128)}, f32[153,1024]{1,0:T(8,128)}) custom-call(s32[1]{0:T(128)} %bitcast.x_ref, bf16[16,56,512]{2,1,0:T(8,128)(2,1)S(1)} %bitcast.16, f32[64,153]{1,0:T(8,128)S(1)} %get-tuple-element.32.score0, ...), custom_call_target="tpu_custom_call" | custom-call | flops 1000000 | bytes 2500000 | tf_op jit(solution)/shard_map/place/pallas_call | solution.py:374
  (1 shorter events, 0.0 us)
Async XLA Ops:
  2.7 23.5 %all-to-all-start.1 = ((bf16[16,96,256]{2,1,0:T(8,128)(2,1)}), bf16[16,96,256]{2,1,0:T(8,128)(2,1)S(1)}, u32[]{:S(2)}, u32[]{:S(2)}) async-start(bf16[16,96,256]{2,1,0:T(8,128)(2,1)} %pack.1), calls=%async_computation.1 | async-start | bytes 1572864 | tf_op jit(solution)/shard_map/all_to_all | solution.py:405
  26.2 27.7 %all-to-all-start = ((bf16[16,96,512]{2,1,0:T(8,128)(2,1)}), bf16[16,96,512]{2,1,0:T(8,128)(2,1)S(1)}, u32[]{:S(2)}, u32[]{:S(2)}) async-start(bf16[16,96,512]{2,1,0:T(8,128)(2,1)} %gather.1), calls=%async_computation | async-start | bytes 3145728 | tf_op jit(solution)/shard_map/all_to_all | solution.py:407
  32.9 3.5 %collective-permute-start = (bf16[16,96,256]{2,1,0:T(8,128)(2,1)S(1)}, bf16[16,96,256]{2,1,0:T(8,128)(2,1)S(1)}, u32[]{:S(2)}, u32[]{:S(2)}) collective-permute-start(bf16[16,96,256]{2,1,0:T(8,128)(2,1)S(1)} %all-to-all-done.1.in_ref), channel_id=1, source_target_pairs={{0,1},{1,0},{2,3},{3,2},{4,5},{5,4},{6,7},{7,6},{8,9},{9,8},{10,11... | collective-permute-start | bytes 2359304 | tf_op jit(solution)/shard_map/ppermute | solution.py:411
  37.2 0.9 copy-start
  53.9 1.1 copy-start.1
  58.7 5.4 %collective-permute-start.1 = (bf16[8,120,256]{2,1,0:T(8,128)(2,1)S(1)}, bf16[8,120,256]{2,1,0:T(8,128)(2,1)S(1)}, u32[]{:S(2)}, u32[]{:S(2)}) collective-permute-start(bf16[8,120,256]{2,1,0:T(8,128)(2,1)S(1)} %get-tuple-element.26), channel_id=1, source_target_pairs={{0,1},{1,0},{2,3},{3,2},{4,5},{5,4},{6,7},{7,6},{8,9},{9,8},{10,11... | collective-permute-start | bytes 1474568 | tf_op jit(solution)/shard_map/ppermute | solution.py:419
  65.0 25.4 %all-to-all-start.2 = ((bf16[8,120,256]{2,1,0:T(8,128)(2,1)}), bf16[8,120,256]{2,1,0:T(8,128)(2,1)S(1)}, u32[]{:S(2)}, u32[]{:S(2)}) async-start(bf16[8,120,256]{2,1,0:T(8,128)(2,1)} %add_pair.1), calls=%async_computation.2 | async-start | bytes 983040 | tf_op jit(solution)/shard_map/all_to_all | solution.py:420
  73.2 6.2 %collective-permute-start.2 = (f32[64,153]{1,0:T(8,128)S(1)}, f32[64,153]{1,0:T(8,128)S(1)}, u32[]{:S(2)}, u32[]{:S(2)}) collective-permute-start(f32[64,153]{1,0:T(8,128)S(1)} %get-tuple-element.28), channel_id=1, source_target_pairs={{0,16},{16,32},{32,48},{48,0},{1,17},{17,33},{33,49},{49,1},{2,18}... | collective-permute-start | bytes 117512 | tf_op jit(solution)/shard_map/ppermute | solution.py:387
  73.2 6.2 %collective-permute-start.3 = (f32[64,153]{1,0:T(8,128)S(1)}, f32[64,153]{1,0:T(8,128)S(1)}, u32[]{:S(2)}, u32[]{:S(2)}) collective-permute-start(f32[64,153]{1,0:T(8,128)S(1)} %get-tuple-element.29), channel_id=1, source_target_pairs={{0,32},{16,48},{32,0},{48,16},{1,33},{17,49},{33,1},{49,17},{2,34}... | collective-permute-start | bytes 117512 | tf_op jit(solution)/shard_map/ppermute | solution.py:387
  73.4 6.0 %collective-permute-start.4 = (f32[64,153]{1,0:T(8,128)S(1)}, f32[64,153]{1,0:T(8,128)S(1)}, u32[]{:S(2)}, u32[]{:S(2)}) collective-permute-start(f32[64,153]{1,0:T(8,128)S(1)} %get-tuple-element.30), channel_id=1, source_target_pairs={{0,48},{16,0},{32,16},{48,32},{1,49},{17,1},{33,17},{49,33},{2,50}... | collective-permute-start | bytes 117512 | tf_op jit(solution)/shard_map/ppermute | solution.py:387
